TPU v7x, 32 devices: a whole 2x2x4 slice. The times are simulated.
32 devices in a mesh: tiles: 2 (over x), morton: 16 (over z, y, core).
Axes of the slice: x: 2, y: 2, z: 4, core: 2. Of those that a mesh axis runs over, the one named last changes fastest.
Arguments:
- features: bfloat16 [256, 512, 64], P(('tiles', 'morton')), parts along dimension 0, may hold values from -6 to 6
- neighbours: int32 [256, 27], P(('tiles', 'morton')), parts along dimension 0, may hold values from -1 to 127, as said below
- occupancy: int32 [256, 16], P(('tiles', 'morton')), parts along dimension 0, may hold values from -2147483648 to 2147483647, as said below
- conv_one: bfloat16 [27, 64, 64], replicated, may hold values from -0.21875 to 0.21875
- first_reduce_kernel: bfloat16 [8, 64, 128], replicated, may hold values from -0.5 to 0.5
- conv_two: bfloat16 [27, 128, 128], replicated, may hold values from -0.1875 to 0.1875
- second_reduce_kernel: bfloat16 [8, 128, 256], replicated, may hold values from -0.375 to 0.375
- conv_three: bfloat16 [27, 256, 256], replicated, may hold values from -0.125 to 0.125
Outputs:
- first_level_features: bfloat16 [256, 512, 64], P(('tiles', 'morton')), parts along dimension 0
- second_level_features: bfloat16 [256, 64, 128], P(('tiles', 'morton')), parts along dimension 0
- skip_three: bfloat16 [256, 8, 256], P(('tiles', 'morton')), parts along dimension 0
There are 2 independent parts, one for each index of `tiles`. A program takes and returns all parts, laid end to end along the dimension named above; an argument that names none is the same for every part. Nothing has to cross between parts.
Inputs may be any that keep to these rules, and one draw needn't show every extreme that they name: `neighbours`: bricks are numbered by x slice, then by cell of the slice's 4 x 4 cross-section in rising order, 8 occupied bricks to a slice. Entry 9 (a+1) + 3 (c+1) + (e+1) of a brick's row is the number of the brick at offset (a, c, e), or -1 if that cell is empty or outside the tile; entry 13 is the brick itself. Every neighbour lies in the brick's own slice or in an adjacent one. Bit k, the lowest being bit 0, of word w of a brick's row is the occupancy of voxel 32 w + k; bit 31 is the sign bit of the word.
All inputs are finite; a program needn't handle non-finite values.
Results may differ from a plain program's by a relative error of at most 0.008.
Values may be sent and summed in bfloat16 or wider, within the bound.
No kernel may reach another device: no remote copies, remote signals or barrier semaphores. Data moves between devices by JAX's collectives and lax.ppermute only.
A program may use at most 128 MiB of HBM per device.

v0:
```python
import jax
import jax.numpy as jnp
import numpy as np
from jax import lax
from jax.experimental import pallas as pl
from jax.experimental.pallas import tpu as pltpu
from jax.sharding import PartitionSpec as P

F32 = jnp.float32
BF16 = jnp.bfloat16
LINE = "morton"
TAPS = [(a, q) for a in range(3) for q in range(9)]


def dot(x, y):
    return jnp.dot(x, y, preferred_element_type=F32)


def iota(shape, axis):
    return lax.broadcasted_iota(jnp.int32, shape, axis)


def stack(parts):
    return jnp.concatenate(parts, axis=0)


def beside(parts):
    return jnp.concatenate(parts, axis=1)


def bits_of(words, shift):
    return jnp.bitwise_and(lax.shift_right_logical(words, shift), 1).astype(F32)


def either(x, y):
    return jnp.bitwise_or(x, y)


def on_odd_place():
    return lax.rem(lax.axis_index(LINE), 2) == 1


def word_lanes(words, w):
    return jnp.broadcast_to(words[:, w : w + 1], (words.shape[0], 128))


def column_bits(words, column):
    lane = iota((words.shape[0], 128), 1)
    w = [word_lanes(words, 4 * column + q) for q in range(4)]
    chosen = jnp.where(
        lane < 64, jnp.where(lane < 32, w[0], w[1]), jnp.where(lane < 96, w[2], w[3])
    )
    return bits_of(chosen, jnp.bitwise_and(lane, 31))


def slots_of(neighbours, first, count, b, tap):
    numbers = [neighbours[b, tap + q] for q in range(9)]
    shift = (1 - tap // 9) * count - first
    return [jnp.where(n < 0, count, n + shift) for n in numbers]


def edges_kernel(features, occupancy, to_a, to_b, columns, words, arrived):
    count = words.shape[0]
    last = features.shape[2] - 128
    copies = [
        pltpu.make_async_copy(occupancy, words, arrived.at[0]),
        pltpu.make_async_copy(features.at[:, :, pl.ds(0, 128)], columns.at[0], arrived.at[1]),
        pltpu.make_async_copy(features.at[:, :, pl.ds(last, 128)], columns.at[1], arrived.at[2]),
    ]
    for copy in copies:
        copy.start()
    for copy in copies:
        copy.wait()
    bits = [column_bits(words[...], 0), column_bits(words[...], last // 128)]
    lane = iota((64, 128), 1)
    odd = on_odd_place()
    for q in range(count // 2):
        low, high = [
            [columns[side, b].astype(F32) * bits[side][b : b + 1] for b in (2 * q, 2 * q + 1)]
            for side in range(2)
        ]
        lows = jnp.where(lane < 64, low[0], pltpu.roll(low[1], 64, 1))
        highs = jnp.where(lane < 64, pltpu.roll(high[0], 64, 1), high[1])
        to_a[q] = jnp.where(odd, lows, highs).astype(BF16)
        to_b[q] = jnp.where(odd, highs, lows).astype(BF16)


def tables_kernel(
    neighbours, occupancy, pick_two, add_two, pick_three, add_three,
    own_two, low_two, high_two, own_three, faces_three, pair_words, mask_two, mask_three,
):
    count = neighbours.shape[0]
    number = neighbours[...]
    tap = iota(number.shape, 1)
    shift = jnp.where(tap < 9, count, jnp.where(tap < 18, 0, -count))
    slot = jnp.where(
        number < 0, 4 * count, number + shift - lax.axis_index(LINE) * count
    ).astype(BF16)
    across = (((1,), (1,)), ((), ()))
    rows = lax.dot_general(pick_two[...], slot, across, preferred_element_type=F32)
    rows = (rows + add_two[...]).astype(jnp.int32)
    lane = iota((16, 16 * count), 1)
    for a, table in enumerate((low_two, own_two, high_two)):
        for q in range(9):
            for b in range(count):
                at = 16 * (9 * a + q)
                table[16 * (count * q + b) : 16 * (count * q + b + 1), :] = jnp.where(
                    rows[at : at + 16, b : b + 1] == lane, 1.0, 0.0
                ).astype(BF16)
    rows = lax.dot_general(pick_three[...], slot, across, preferred_element_type=F32)
    rows = (rows + add_three[...]).astype(jnp.int32)
    for table, begin in ((own_three, 0), (faces_three, 27)):
        lane = iota((8, table.shape[1]), 1)
        for q in range(table.shape[0] // (8 * count)):
            at = 8 * (begin + q)
            table[8 * count * q : 8 * count * (q + 1), :] = stack(
                [
                    jnp.where(rows[at : at + 8, b : b + 1] == lane, 1.0, 0.0)
                    for b in range(count)
                ]
            ).astype(BF16)

    words = [word_lanes(occupancy[...], w) for w in range(16)]
    lane = iota((count, 128), 1)
    row = iota((8, 128), 0)
    any_two = []
    for i in range(4):
        for half in range(2):
            low, high = words[4 * i + half], words[4 * i + 2 + half]
            pair_words[2 * i + half] = jnp.where(lane < 64, low, high)
            word = either(low, high)
            word = either(word, lax.shift_right_logical(word, 1))
            any_two.append(either(word, lax.shift_right_logical(word, 8)))
    two_shift = 16 * lax.shift_right_logical(row, 2) + 2 * jnp.bitwise_and(row, 3)
    for i in range(4):
        for b in range(count):
            mask_two[i, 16 * b : 16 * (b + 1)] = stack(
                [
                    bits_of(
                        jnp.broadcast_to(any_two[2 * i + half][b : b + 1], (8, 128)), two_shift
                    )
                    for half in range(2)
                ]
            )
    any_three = []
    for i in range(2):
        for j in range(2):
            word = either(any_two[4 * i + j], any_two[4 * i + 2 + j])
            word = either(word, lax.shift_right_logical(word, 16))
            any_three.append(either(word, lax.shift_right_logical(word, 2)))
    for b in range(count):
        tile = [jnp.broadcast_to(word[b : b + 1], (8, 128)) for word in any_three]
        tile = jnp.where(
            row < 4, jnp.where(row < 2, tile[0], tile[1]), jnp.where(row < 6, tile[2], tile[3])
        )
        mask = bits_of(tile, 4 * jnp.bitwise_and(row, 1))
        mask_three[8 * b : 8 * (b + 1)] = beside([mask, mask])


def shifted_windows(source, row):
    shifted = []
    for j in range(-1, 9):
        c, at = (0, 7) if j < 0 else (2, 0) if j > 7 else (1, j)
        left, mid, right = [source(3 * c + e, at) for e in range(3)]
        shifted.append(
            (
                pltpu.roll(jnp.where(row == 7, left, mid), 1, 0),
                mid,
                pltpu.roll(jnp.where(row == 0, right, mid), 7, 0),
            )
        )
    return [
        [stack([shifted[jr][e], shifted[jr + 4][e]]).astype(BF16) for e in range(3)]
        for jr in range(6)
    ]


def outer_kernel(
    neighbours, occupancy, features, kernel,
    padded, taps, face_taps, partial,
    pairs, low_edge, high_edge, numbers, arrived,
):
    count = features.shape[0]
    first = lax.axis_index(LINE) * count
    lane = iota((64, 128), 1)
    row = iota((8, 128), 0)
    copy = pltpu.make_async_copy(neighbours, numbers, arrived)
    copy.start()

    none = jnp.zeros((64, 64), F32)
    for q in range(9):
        w = [kernel[9 * a + q].astype(F32) for a in range(3)]
        taps[q * 256 : (q + 1) * 256, :] = stack(
            [beside([w[p] if p < 3 else none, w[p - 1] if p else none]) for p in range(4)]
        ).astype(BF16)
        face_taps[q * 128 : (q + 1) * 128, :] = stack(
            [beside([w[0], none]), beside([none, w[2]])]
        ).astype(BF16)

    for table in (pairs.at[0], pairs.at[1], pairs.at[2], low_edge, high_edge):
        table[count] = jnp.zeros((64, 128), F32)
    bits = [column_bits(occupancy[...], q) for q in range(4)]
    for b in range(count):
        cols = [
            features[b, :, 128 * q : 128 * (q + 1)].astype(F32) * bits[q][b : b + 1]
            for q in range(4)
        ]
        rolled = [pltpu.roll(col, 64, 1) for col in cols]
        m = stack(
            [
                jnp.where(lane < 64, rolled[0], cols[1]),
                jnp.where(lane < 64, cols[1], rolled[2]),
            ]
        ).T
        pairs[0, b] = m[:64]
        pairs[1, b] = m[64:]
        m = stack(
            [
                jnp.where(lane < 64, rolled[2], cols[3]),
                jnp.where(lane < 64, cols[3], rolled[0]),
            ]
        ).T
        pairs[2, b] = m[:64]
        low_edge[b] = jnp.where(lane < 64, 0.0, m[64:])
        high_edge[b] = jnp.where(lane < 64, m[64:], 0.0)

    copy.wait()
    tables = [low_edge, pairs.at[0], pairs.at[1], pairs.at[2], high_edge]
    for b in range(count):
        slot = slots_of(numbers, first, count, b, 9)
        for pair in range(5):
            windows = shifted_windows(
                lambda q, j: tables[pair][slot[q], pl.ds(8 * j, 8), :], row
            )
            for jr in range(6):
                for e in range(3):
                    padded[b, e, pair, jr] = windows[jr][e]

    group = count // 2
    for g in range(2):
        bricks = slice(g * group, (g + 1) * group)
        for side in range(2):
            partial[side, g * group * 64 : (g + 1) * group * 64] = dot(
                beside(
                    [
                        padded[bricks, e, 3 * side + p, c : c + 4].reshape(group * 64, 128)
                        for c in range(3)
                        for e in range(3)
                        for p in range(2)
                    ]
                ),
                taps[...],
            )


def masked_tiles(sums, pair_words, b, i):
    row = iota((8, 128), 0)
    tiles = {}
    for half in range(2):
        words = jnp.broadcast_to(pair_words[2 * i + half, b : b + 1, :], (8, 128))
        for jr in range(4):
            at = jr * 16 + half * 8
            tiles[4 * half + jr] = jnp.maximum(sums[at : at + 8], 0.0) * bits_of(
                words, row + 8 * jr
            )
    return [tiles[j] for j in range(8)]


def reduce_planes(groups, reduce, low_sums, high_sums):
    left = stack(
        [beside([tiles[j], tiles[j + 1]]) for tiles in groups for j in (0, 2, 4, 6)]
    ).astype(BF16)
    weights = stack(
        [
            beside([reduce[4 * ci + 2 * cj], reduce[4 * ci + 2 * cj + 1]])
            for cj in range(2)
            for ci in range(2)
        ]
    )
    sums = dot(left, weights)
    low_sums[...] = sums[:, :128]
    high_sums[...] = sums[:, 128:]
    return [
        low_sums[pl.ds(32 * g, 16, stride=2), :] + high_sums[pl.ds(32 * g + 1, 16, stride=2), :]
        for g in range(len(groups))
    ]


def faces_one_kernel(
    neighbours, from_a, from_b, face_taps, partial, reduce, pair_words, mask_two,
    outer, second, to_a, to_b,
    halo, windows, low_sums, high_sums, numbers, arrived,
):
    count = outer.shape[0]
    first = lax.axis_index(LINE) * count
    lane = iota((64, 128), 1)
    small = iota((8, 128), 1)
    row = iota((8, 128), 0)
    odd = on_odd_place()
    copy = pltpu.make_async_copy(neighbours, numbers, arrived)
    copy.start()
    halo[count] = jnp.zeros((64, 128), F32)
    for q in range(count // 2):
        one, two = from_a[q].astype(F32), from_b[q].astype(F32)
        m = stack([jnp.where(odd, one, two), jnp.where(odd, two, one)]).T
        halo[2 * q] = m[:64]
        halo[2 * q + 1] = m[64:]
    copy.wait()
    for b in range(count):
        low = slots_of(numbers, first, count, b, 0)
        high = slots_of(numbers, first, count, b, 18)

        def source(q, j):
            rows = pl.ds(8 * j, 8)
            return jnp.where(small < 64, halo[low[q], rows, :], halo[high[q], rows, :])

        tiles = shifted_windows(source, row)
        for jr in range(6):
            for e in range(3):
                windows[b, e, jr] = tiles[jr][e]
    added = dot(
        beside(
            [
                windows[:, e, c : c + 4].reshape(count * 64, 128)
                for c in range(3)
                for e in range(3)
            ]
        ),
        face_taps[...],
    )
    groups = []
    for b in range(count):
        at = slice(64 * b, 64 * (b + 1))
        for side in range(2):
            near = (lane < 64) == (side == 0)
            sums = partial[side, at] + jnp.where(near, added[at], 0.0)
            groups.append(masked_tiles(sums, pair_words, b, 3 * side))
            outer[b, side] = stack(groups[-1]).astype(BF16)
    sums = reduce_planes(groups, reduce, low_sums, high_sums)
    for b in range(count):
        at = slice(16 * b, 16 * (b + 1))
        planes = [
            (jnp.maximum(sums[2 * b + side], 0.0) * mask_two[3 * side, at]).astype(BF16)
            for side in range(2)
        ]
        second[0, at] = planes[0]
        second[1, at] = planes[1]
        to_a[at] = jnp.where(odd, planes[0], planes[1])
        to_b[at] = jnp.where(odd, planes[1], planes[0])


def inner_kernel(
    padded, taps, outer, reduce, pair_words, mask_two,
    result, second,
    out, low_sums, high_sums, stored,
):
    count = padded.shape[0]
    lane = iota((64, 128), 1)
    total = dot(
        beside(
            [
                padded[:, e, 1 + p : 3 + p, c : c + 4].reshape(count * 128, 128)
                for c in range(3)
                for e in range(3)
                for p in range(2)
            ]
        ),
        taps[...],
    )
    groups = []
    copies = []
    for b in range(count):
        for i in (1, 2):
            at = 128 * b + 64 * (i - 1)
            groups.append(masked_tiles(total[at : at + 64], pair_words, b, i))
        ordered = [
            outer[b, 0].astype(F32),
            stack(groups[2 * b]),
            stack(groups[2 * b + 1]),
            outer[b, 1].astype(F32),
        ]
        for i in (0, 2):
            m = stack(ordered[i : i + 2]).T
            top, bottom = m[:64], m[64:]
            out[b, :, 128 * i : 128 * (i + 1)] = jnp.where(
                lane < 64, top, pltpu.roll(bottom, 64, 1)
            ).astype(BF16)
            out[b, :, 128 * (i + 1) : 128 * (i + 2)] = jnp.where(
                lane < 64, pltpu.roll(top, 64, 1), bottom
            ).astype(BF16)
        copies.append(pltpu.make_async_copy(out.at[b], result.at[b], stored.at[b]))
        copies[-1].start()
    sums = reduce_planes(groups, reduce, low_sums, high_sums)
    for b in range(count):
        at = slice(16 * b, 16 * (b + 1))
        for i in (1, 2):
            second[i - 1, at] = (
                jnp.maximum(sums[2 * b + i - 1], 0.0) * mask_two[i, at]
            ).astype(BF16)
    for copy in copies:
        copy.wait()


def own_two_kernel(outer, inner, gather, kernel, partial):
    rows = outer.shape[1]
    planes = beside([outer[0], inner[0], inner[1], outer[1]])
    moved = dot(gather[...], planes).astype(BF16)
    none = jnp.zeros((rows, 128), BF16)
    left = beside(
        [
            stack(
                [
                    moved[q * rows : (q + 1) * rows, 128 * (i + a - 1) : 128 * (i + a)]
                    if 0 <= i + a - 1 < 4
                    else none
                    for i in range(4)
                ]
            )
            for a, q in TAPS
        ]
    )
    partial[...] = dot(left, kernel[...].reshape(27 * 128, 128))


def faces_two_kernel(
    low_gather, high_gather, children, partial, from_a, from_b, kernel, reduce,
    mask_two, mask_three,
    second, third,
):
    count = second.shape[0]
    rows = 16 * count
    odd = on_odd_place()
    one, two = from_a[...], from_b[...]
    added = []
    for gather, face, tap in (
        (low_gather, jnp.where(odd, one, two), 0),
        (high_gather, jnp.where(odd, two, one), 18),
    ):
        moved = dot(gather[...], face).astype(BF16)
        left = beside([moved[q * rows : (q + 1) * rows] for q in range(9)])
        added.append(dot(left, kernel[tap : tap + 9].reshape(9 * 128, 128)))
    planes = []
    for i in range(4):
        sums = partial[i * rows : (i + 1) * rows]
        if i == 0:
            sums = sums + added[0]
        if i == 3:
            sums = sums + added[1]
        planes.append((jnp.maximum(sums, 0.0) * mask_two[i]).astype(BF16))
    bricks = [
        stack([planes[i][16 * b : 16 * (b + 1)] for i in range(4)]) for b in range(count)
    ]
    for b in range(count):
        second[b] = bricks[b]
    moved = dot(children[...], beside(bricks))
    left = beside(
        [
            stack([moved[8 * q : 8 * (q + 1), 128 * b : 128 * (b + 1)] for b in range(count)])
            for q in range(8)
        ]
    ).astype(BF16)
    sums = dot(left, reduce[...].reshape(8 * 128, 256))
    third[...] = (jnp.maximum(sums, 0.0) * mask_three[...]).astype(BF16)


def own_three_kernel(gather, third, kernel, second, partial, result, stored):
    copy = pltpu.make_async_copy(second, result, stored)
    copy.start()
    rows = third.shape[0]
    moved = dot(gather[...], third[...]).astype(BF16)
    left = beside([moved[q * rows : (q + 1) * rows] for q in range(27)])
    partial[...] = dot(left, kernel[...].reshape(27 * 256, 256))
    copy.wait()


def faces_three_kernel(gather, partial, from_a, from_b, kernel, mask_three, out):
    rows = partial.shape[0]
    odd = on_odd_place()
    one, two = from_a[...], from_b[...]
    faces = stack([jnp.where(odd, one, two), jnp.where(odd, two, one)])
    moved = dot(gather[...], faces).astype(BF16)
    left = beside([moved[q * rows : (q + 1) * rows] for q in range(18)])
    weights = stack([kernel[:9].reshape(9 * 256, 256), kernel[18:].reshape(9 * 256, 256)])
    sums = partial[...] + dot(left, weights)
    out[...] = (jnp.maximum(sums, 0.0) * mask_three[...]).astype(BF16).reshape(out.shape)


def level_two_rows(count):
    pick = np.zeros((432, 27), np.float32)
    add = np.zeros((432, count), np.float32)
    for a in range(3):
        for q in range(9):
            for r in range(16):
                y, z = r // 4 + q // 3 - 1, r % 4 + q % 3 - 1
                at = 16 * (9 * a + q) + r
                pick[at, 9 * a + 3 * (y // 4 + 1) + z // 4 + 1] = 16
                add[at] = 4 * (y % 4) + z % 4
    return jnp.asarray(pick, BF16), jnp.asarray(add)


def level_three_rows(count):
    pick = np.zeros((360, 27), np.float32)
    add = np.full((360, count), -1, np.float32)
    for tap in range(27):
        for u in range(8):
            x, y, z = (u >> 2) + tap // 9 - 1, ((u >> 1) & 1) + tap // 3 % 3 - 1, (u & 1) + tap % 3 - 1
            side = x // 2
            at = 8 * tap if side == 0 else 8 * (27 + tap) if side < 0 else 8 * (36 + tap - 18)
            pick[at + u, 9 * (side + 1) + 3 * (y // 2 + 1) + z // 2 + 1] = 8
            add[at + u] = 4 * (x % 2) + 2 * (y % 2) + z % 2 + (8 * count if side > 0 else 0)
    return jnp.asarray(pick, BF16), jnp.asarray(add)


def child_rows():
    pick = np.zeros((64, 64), np.float32)
    for q in range(8):
        for u in range(8):
            x, y, z = [2 * ((u >> s) & 1) + ((q >> s) & 1) for s in (2, 1, 0)]
            pick[8 * q + u, 16 * x + 4 * y + z] = 1
    return jnp.asarray(pick, BF16)


ANY = pl.BlockSpec(memory_space=pl.ANY)
VMEM = pl.BlockSpec(memory_space=pltpu.VMEM)
DMA = pltpu.SemaphoreType.DMA


def call(kernel, cost, out_shape, scratch, *args, remain=(), store=()):
    single = not isinstance(out_shape, tuple)
    outs = (out_shape,) if single else out_shape
    specs = tuple(ANY if n in store else VMEM for n in range(len(outs)))
    return pl.pallas_call(
        kernel,
        out_shape=out_shape,
        in_specs=[ANY if n in remain else VMEM for n in range(len(args))],
        out_specs=specs[0] if single else specs,
        scratch_shapes=scratch,
        compiler_params=pltpu.CompilerParams(vmem_limit_bytes=24 * 1024 * 1024),
        cost_estimate=pl.CostEstimate(
            flops=cost * 10**9, bytes_accessed=10**7, transcendentals=0
        ),
    )(*args)


def swaps(tiles, count):
    within, across = [], []
    for t in range(tiles):
        for m in range(count):
            if m ^ 1 < count:
                within.append((t * count + m, t * count + (m ^ 1)))
            other = ((m - 1) ^ 1) + 1 if m else -1
            if 0 <= other < count:
                across.append((t * count + m, t * count + other))
            elif t ^ 1 < tiles:
                across.append((t * count + m, (t ^ 1) * count + m))
    return within, across


def on_device(
    features,
    neighbours,
    occupancy,
    conv_one,
    first_reduce_kernel,
    conv_two,
    second_reduce_kernel,
    conv_three,
):
    axes = ("tiles", LINE)
    within, across = swaps(lax.axis_size("tiles"), lax.axis_size(LINE))
    count = features.shape[0]
    features = jnp.swapaxes(features, 1, 2)
    shape = jax.ShapeDtypeStruct
    scalars = [pltpu.SMEM(neighbours.shape, jnp.int32), DMA(())]

    def exchange(to_a, to_b):
        from_b = lax.ppermute(to_b, axes, across)
        return lax.ppermute(to_a, axes, within), from_b

    face = shape((count // 2, 64, 128), BF16)
    from_a, from_b = exchange(
        *call(
            edges_kernel,
            1,
            (face, face),
            [
                pltpu.VMEM((2, count, 64, 128), BF16),
                pltpu.VMEM(occupancy.shape, jnp.int32),
                DMA((3,)),
            ],
            features, occupancy,
            remain=(0, 1),
        )
    )
    own_two, low_two, high_two, own_three, faces_three, pair_words, mask_two, mask_three = call(
        tables_kernel,
        1,
        (shape((9 * 16 * count, 16 * count), BF16),) * 3
        + (
            shape((27 * 8 * count, 8 * count), BF16),
            shape((18 * 8 * count, 16 * count), BF16),
            shape((8, count, 128), jnp.int32),
            shape((4, 16 * count, 128), F32),
            shape((8 * count, 256), F32),
        ),
        [],
        neighbours, occupancy, *level_two_rows(count), *level_three_rows(count),
    )
    padded, taps, face_taps, partial = call(
        outer_kernel,
        4,
        (
            shape((count, 3, 5, 6, 16, 128), BF16),
            shape((9 * 256, 128), BF16),
            shape((9 * 128, 128), BF16),
            shape((2, count * 64, 128), F32),
        ),
        [
            pltpu.VMEM((3, count + 1, 64, 128), F32),
            pltpu.VMEM((count + 1, 64, 128), F32),
            pltpu.VMEM((count + 1, 64, 128), F32),
        ]
        + scalars,
        neighbours, occupancy, features, conv_one,
        remain=(0,),
    )
    plane = shape((16 * count, 128), BF16)
    planes = shape((2, 16 * count, 128), BF16)
    sums = pltpu.VMEM((count * 64, 128), F32)
    outer, outer_two, to_a, to_b = call(
        faces_one_kernel,
        2,
        (shape((count, 2, 64, 128), BF16), planes, plane, plane),
        [
            pltpu.VMEM((count + 1, 64, 128), F32),
            pltpu.VMEM((count, 3, 6, 16, 128), BF16),
            sums,
            sums,
        ]
        + scalars,
        neighbours, from_a, from_b, face_taps, partial, first_reduce_kernel, pair_words, mask_two,
        remain=(0,),
    )
    from_a, from_b = exchange(to_a, to_b)

    first_level, inner_two = call(
        inner_kernel,
        4,
        (shape(features.shape, BF16), planes),
        [pltpu.VMEM(features.shape, BF16), sums, sums, DMA((count,))],
        padded, taps, outer, first_reduce_kernel, pair_words, mask_two,
        store=(0,),
    )
    partial = call(
        own_two_kernel,
        2,
        shape((4 * 16 * count, 128), F32),
        [],
        outer_two, inner_two, own_two, conv_two,
    )
    second_level, third = call(
        faces_two_kernel,
        2,
        (shape((count, 64, 128), BF16), shape((8 * count, 256), BF16)),
        [],
        low_two, high_two, child_rows(), partial, from_a, from_b, conv_two, second_reduce_kernel,
        mask_two, mask_three,
    )
    from_a, from_b = exchange(third, third)

    partial, second_level = call(
        own_three_kernel,
        2,
        (shape((8 * count, 256), F32), shape(second_level.shape, BF16)),
        [DMA(())],
        own_three, third, conv_three, second_level,
        store=(1,),
    )
    third_level = call(
        faces_three_kernel,
        1,
        shape((count, 8, 256), BF16),
        [],
        faces_three, partial, from_a, from_b, conv_three, mask_three,
    )
    return jnp.swapaxes(first_level, 1, 2), second_level, third_level


def solution(mesh):
    split = P(("tiles", LINE))
    return jax.shard_map(
        on_device,
        mesh=mesh,
        in_specs=(split, split, split, P(), P(), P(), P(), P()),
        out_specs=(split, split, split),
        check_vma=False,
    )
```

profile of v0, /device:TPU:0, one launch (start us, length us, event | category | flops | bytes accessed | tf_op | source)
XLA Modules:
  0.0 23.7 jit_solution(5300275420846018586)
XLA Ops:
  0.6 0.0 copy-start.2
  0.6 1.0 %copy-done.2 = bf16[8,512,64]{1,2,0:T(8,128)(2,1)S(1)} copy-done((bf16[8,512,64]{1,2,0:T(8,128)(2,1)S(1)}, bf16[8,512,64]{1,2,0:T(8,128)(2,1)}, u32[]{:S(2)}) %copy-start.2) | copy-done | bytes 524312
  1.7 0.0 copy-start.7
  1.7 0.7 %copy-done.7 = s32[8,16]{1,0:T(8,128)S(1)} copy-done((s32[8,16]{1,0:T(8,128)S(1)}, s32[8,16]{1,0:T(8,128)}, u32[]{:S(2)}) %copy-start.7) | copy-done | bytes 536
  2.4 0.0 copy-start.3
  2.4 0.0 copy-start.5
  2.4 0.0 copy-start.8
  2.4 0.0 copy-start.9
  2.4 0.3 %shard_map.149 = (bf16[4,64,128]{2,1,0:T(8,128)(2,1)S(1)}, bf16[4,64,128]{2,1,0:T(8,128)(2,1)S(1)}) custom-call(bf16[8,64,512]{2,1,0:T(8,128)(2,1)S(1)} %bitcast.2, s32[8,16]{1,0:T(8,128)S(1)} %copy-done.7), custom_call_target="tpu_custom_call" | custom-call | flops 1000000000 | bytes 10000000 | tf_op jit(solution)/shard_map/pallas_call | solution.py:532
  2.7 0.5 %collective-permute-start = (bf16[4,64,128]{2,1,0:T(8,128)(2,1)S(1)}, bf16[4,64,128]{2,1,0:T(8,128)(2,1)S(1)}, u32[]{:S(2)}, u32[]{:S(2)}) collective-permute-start(bf16[4,64,128]{2,1,0:T(8,128)(2,1)S(1)} %get-tuple-element.29), channel_id=1, source_target_pairs={{0,1},{1,0},{2,3},{3,2},{4,5},{5,4},{6,7},{7,6},{8,9},{9,8},{10,11... | collective-permute-start | bytes 196616 | tf_op jit(solution)/shard_map/ppermute | solution.py:578
  3.2 0.0 copy-start.10
  3.2 0.0 copy-start.11
  3.2 2.6 %collective-permute-start.1 = (bf16[4,64,128]{2,1,0:T(8,128)(2,1)S(1)}, bf16[4,64,128]{2,1,0:T(8,128)(2,1)S(1)}, u32[]{:S(2)}, u32[]{:S(2)}) collective-permute-start(bf16[4,64,128]{2,1,0:T(8,128)(2,1)S(1)} %get-tuple-element.30), channel_id=1, source_target_pairs={{0,16},{1,2},{2,1},{3,4},{4,3},{5,6},{6,5},{7,8},{8,7},{9,10},{10,... | collective-permute-start | bytes 196616 | tf_op jit(solution)/shard_map/ppermute | solution.py:577
  5.8 0.0 copy-done.3
  5.8 0.0 copy-done.5
  5.8 0.0 copy-done.8
  5.8 0.0 copy-done.9
  5.8 2.2 %shard_map.148 = (bf16[8,3,5,6,16,128]{5,4,3,2,1,0:T(8,128)(2,1)S(1)}, bf16[2304,128]{1,0:T(8,128)(2,1)S(1)}, bf16[1152,128]{1,0:T(8,128)(2,1)S(1)}, f32[2,512,128]{2,1,0:T(8,128)S(1)}) custom-call(s32[8,27]{1,0:T(8,128)S(1)} %copy-done.9, s32[8,16]{1,0:T(8,128)S(1)} %copy-done.8, bf16[8,64,512]{2,1,0:T(8,128)(2,1)S(1)} %bitcast.3, ...), custom_call_target="tpu_custom_call" | custom-call | flops 4000000000 | bytes 10000000 | tf_op jit(solution)/shard_map/pallas_call | solution.py:532
  8.0 0.0 copy-done.10
  8.0 0.0 copy-done.11
  8.0 0.0 copy-done.12
  8.0 0.0 copy-done.13
  8.0 0.0 copy-start.6
  8.0 1.6 %shard_map.150 = (bf16[1152,128]{1,0:T(8,128)(2,1)S(1)}, bf16[1152,128]{1,0:T(8,128)(2,1)S(1)}, bf16[1152,128]{1,0:T(8,128)(2,1)S(1)}, bf16[1728,64]{1,0:T(8,128...) custom-call(s32[8,27]{1,0:T(8,128)S(1)} %copy-done.9, ...), custom_call_target="tpu_custom_call" | custom-call | flops 1000000000 | bytes 10000000 | tf_op jit(solution)/shard_map/pallas_call | solution.py:532
  9.7 0.0 collective-permute-done.from_a
  9.7 0.0 collective-permute-done.1.from_b
  9.7 0.0 copy-done.6
  9.7 1.4 %shard_map.151 = (bf16[8,2,64,128]{3,2,1,0:T(8,128)(2,1)S(1)}, bf16[2,128,128]{2,1,0:T(8,128)(2,1)S(1)}, bf16[128,128]{1,0:T(8,128)(2,1)S(1)}, bf16[128,128]{1,0:T(8,128)(2,1)S(1)}) custom-call(s32[8,27]{1,0:T(8,128)S(1)} %copy-done.9, bf16[4,64,128]{2,1,0:T(8,128)(2,1)S(1)} %collective-permute-done.from_a, ...), custom_call_target="tpu_custom_call" | custom-call | flops 2000000000 | bytes 10000000 | tf_op jit(solution)/shard_map/pallas_call | solution.py:532
  11.2 0.2 collective-permute-start.2
  11.4 1.5 %collective-permute-start.3 = (bf16[128,128]{1,0:T(8,128)(2,1)S(1)}, bf16[128,128]{1,0:T(8,128)(2,1)S(1)}, u32[]{:S(2)}, u32[]{:S(2)}) collective-permute-start(bf16[128,128]{1,0:T(8,128)(2,1)S(1)} %get-tuple-element.44), channel_id=1, source_target_pairs={{0,16},{1,2},{2,1},{3,4},{4,3},{5,6},{6,5},{7,8},{8,7},{9,10},{10,... | collective-permute-start | bytes 98312 | tf_op jit(solution)/shard_map/ppermute | solution.py:577
  12.9 2.4 %shard_map.152 = (bf16[8,64,512]{2,1,0:T(8,128)(2,1)}, bf16[2,128,128]{2,1,0:T(8,128)(2,1)S(1)}) custom-call(bf16[8,3,5,6,16,128]{5,4,3,2,1,0:T(8,128)(2,1)S(1)} %get-tuple-element.27.padded, bf16[2304,128]{1,0:T(8,128)(2,1)S(1)} %get-tuple-element.28.taps, bf16[8,2,64,128]{3,2,1,0:T(8,128)(2,1)S(1)} %get-tuple-element.35.outer, ...), custom_call_target="tpu_custom_call" | custom-call | flops 4000000000 | bytes 10000000 | tf_op jit(solution)/shard_map/pallas_call | solution.py:532
  15.3 0.0 copy-done.1
  15.3 0.0 copy-start.4
  15.3 0.0 copy-start.14
  15.3 2.0 %shard_map.153.partial = f32[512,128]{1,0:T(8,128)S(1)} custom-call(bf16[2,128,128]{2,1,0:T(8,128)(2,1)S(1)} %get-tuple-element.40.outer, bf16[2,128,128]{2,1,0:T(8,128)(2,1)S(1)} %get-tuple-element.41.inner, bf16[1152,128]{1,0:T(8,128)(2,1)S(1)} %get-tuple-element.42.gather, bf16[27,128,128]{2,1,0:T(8,128)(2,1)S(1)} %copy-done.1), custom_call_target="tpu_custom_call" | custom-call | flops 2000000000 | bytes 10000000 | tf_op jit(solution)/shard_map/pallas_call | solution.py:532
  17.3 0.0 collective-permute-done.2.from_a
  17.3 0.0 collective-permute-done.3.from_b
  17.3 0.0 copy-done.4
  17.3 0.0 copy-done.14
  17.3 0.0 copy-start
  17.3 1.0 %shard_map.154 = (bf16[8,64,128]{2,1,0:T(8,128)(2,1)S(1)}, bf16[64,256]{1,0:T(8,128)(2,1)S(1)}) custom-call(bf16[1152,128]{1,0:T(8,128)(2,1)S(1)} %get-tuple-element.38.low_gather, bf16[1152,128]{1,0:T(8,128)(2,1)S(1)} %get-tuple-element.39.high_gather, bf16[64,64]{1,0:T(8,128)(2,1)S(1)} %copy-done.14, f32[512,128]{1,0:T(8,128)S(1)} %shard_map.153.partial, ...), custom_call_target="tpu_custom_call" | custom-call | flops 2000000000 | bytes 10000000 | tf_op jit(solution)/shard_map/pallas_call | solution.py:532
  18.3 0.6 %collective-permute-start.5 = (bf16[64,256]{1,0:T(8,128)(2,1)S(1)}, bf16[64,256]{1,0:T(8,128)(2,1)S(1)}, u32[]{:S(2)}, u32[]{:S(2)}) collective-permute-start(bf16[64,256]{1,0:T(8,128)(2,1)S(1)} %get-tuple-element.46.third), channel_id=1, source_target_pairs={{0,16},{1,2},{2,1},{3,4},{4,3},{5,6},{6,5},{7,8},{8,7},{9,10},{10,... | collective-permute-start | bytes 98312 | tf_op jit(solution)/shard_map/ppermute | solution.py:577
  18.9 0.1 collective-permute-start.4
  19.0 0.3 %copy-done = bf16[27,256,256]{2,1,0:T(8,128)(2,1)S(1)} copy-done((bf16[27,256,256]{2,1,0:T(8,128)(2,1)S(1)}, bf16[27,256,256]{2,1,0:T(8,128)(2,1)}, u32[]{:S(2)}) %copy-start) | copy-done | bytes 3538968
  19.3 1.1 %shard_map.155 = (f32[64,256]{1,0:T(8,128)S(1)}, bf16[8,64,128]{2,1,0:T(8,128)(2,1)}) custom-call(bf16[1728,64]{1,0:T(8,128)(2,1)S(1)} %get-tuple-element.37.gather, bf16[64,256]{1,0:T(8,128)(2,1)S(1)} %get-tuple-element.46.third, bf16[27,256,256]{2,1,0:T(8,128)(2,1)S(1)} %copy-done, bf16[8,64,128]{2,1,0:T(8,128)(2,1)S(1)} %get-tuple-element.47.second), custom_call_target="tpu_custom_call" | custom-call | flops 2000000000 | bytes 10000000 | tf_op jit(solution)/shard_map/pallas_call | solution.py:532
  20.4 1.9 %collective-permute-done.5.from_b = bf16[64,256]{1,0:T(8,128)(2,1)S(1)} collective-permute-done((bf16[64,256]{1,0:T(8,128)(2,1)S(1)}, bf16[64,256]{1,0:T(8,128)(2,1)S(1)}, u32[]{:S(2)}, u32[]{:S(2)}) %collective-permute-start.5) | collective-permute-done | bytes 32800 | tf_op jit(solution)/shard_map/ppermute | solution.py:577
  22.3 0.0 collective-permute-done.4.from_a
  22.3 1.5 %shard_map.156 = bf16[8,8,256]{2,1,0:T(8,128)(2,1)} custom-call(bf16[1152,128]{1,0:T(8,128)(2,1)S(1)} %get-tuple-element.49.gather, f32[64,256]{1,0:T(8,128)S(1)} %get-tuple-element.50.partial, bf16[64,256]{1,0:T(8,128)(2,1)S(1)} %collective-permute-done.4.from_a, bf16[64,256]{1,0:T(8,128)(2,1)S(1)} %collective-permute-done.5.from_b, ...), custom_call_target="tpu_custom_call" | custom-call | flops 1000000000 | bytes 10000000 | tf_op jit(solution)/shard_map/pallas_call | solution.py:532
  (3 shorter events, 0.0 us)
Async XLA Ops:
  0.6 1.0 %copy-start.2 = (bf16[8,512,64]{1,2,0:T(8,128)(2,1)S(1)}, bf16[8,512,64]{1,2,0:T(8,128)(2,1)}, u32[]{:S(2)}) copy-start(bf16[8,512,64]{1,2,0:T(8,128)(2,1)} %param.13) | copy-start | bytes 1572868
  1.7 0.7 %copy-start.7 = (s32[8,16]{1,0:T(8,128)S(1)}, s32[8,16]{1,0:T(8,128)}, u32[]{:S(2)}) copy-start(s32[8,16]{1,0:T(8,128)} %occupancy.5) | copy-start | bytes 1540
  2.4 3.4 %copy-start.3 = (bf16[8,512,64]{1,2,0:T(8,128)(2,1)S(1)}, bf16[8,512,64]{1,2,0:T(8,128)(2,1)}, u32[]{:S(2)}) copy-start(bf16[8,512,64]{1,2,0:T(8,128)(2,1)} %param.13) | copy-start | bytes 1572868
  2.4 3.4 %copy-start.5 = (bf16[27,64,64]{2,1,0:T(8,128)(2,1)S(1)}, bf16[27,64,64]{2,1,0:T(8,128)(2,1)}, u32[]{:S(2)}) copy-start(bf16[27,64,64]{2,1,0:T(8,128)(2,1)} %kernel.5) | copy-start | bytes 663556
  2.4 3.4 %copy-start.8 = (s32[8,16]{1,0:T(8,128)S(1)}, s32[8,16]{1,0:T(8,128)}, u32[]{:S(2)}) copy-start(s32[8,16]{1,0:T(8,128)} %occupancy.5) | copy-start | bytes 1540
  2.4 3.4 %copy-start.9 = (s32[8,27]{1,0:T(8,128)S(1)}, s32[8,27]{1,0:T(8,128)}, u32[]{:S(2)}) copy-start(s32[8,27]{1,0:T(8,128)} %neighbours.5) | copy-start | bytes 2596
  2.7 7.0 %collective-permute-start = (bf16[4,64,128]{2,1,0:T(8,128)(2,1)S(1)}, bf16[4,64,128]{2,1,0:T(8,128)(2,1)S(1)}, u32[]{:S(2)}, u32[]{:S(2)}) collective-permute-start(bf16[4,64,128]{2,1,0:T(8,128)(2,1)S(1)} %get-tuple-element.29), channel_id=1, source_target_pairs={{0,1},{1,0},{2,3},{3,2},{4,5},{5,4},{6,7},{7,6},{8,9},{9,8},{10,11... | collective-permute-start | bytes 196616 | tf_op jit(solution)/shard_map/ppermute | solution.py:578
  3.2 4.8 %copy-start.10 = (f32[432,8]{1,0:T(8,128)S(1)}, f32[432,8]{1,0:T(8,128)}, u32[]{:S(2)}) copy-start(f32[432,8]{1,0:T(8,128)} %constant.11.clone.add_two) | copy-start | bytes 41476
  3.2 4.8 %copy-start.11 = (f32[360,8]{1,0:T(8,128)S(1)}, f32[360,8]{1,0:T(8,128)}, u32[]{:S(2)}) copy-start(f32[360,8]{1,0:T(8,128)} %constant.13.clone.add_three) | copy-start | bytes 34564
  3.2 4.8 %copy-start.12 = (bf16[432,27]{1,0:T(8,128)(2,1)S(1)}, bf16[432,27]{1,0:T(8,128)(2,1)}, u32[]{:S(2)}) copy-start(bf16[432,27]{1,0:T(8,128)(2,1)} %constant.10.clone.pick_two) | copy-start | bytes 69988
  3.2 4.9 %copy-start.13 = (bf16[360,27]{1,0:T(8,128)(2,1)S(1)}, bf16[360,27]{1,0:T(8,128)(2,1)}, u32[]{:S(2)}) copy-start(bf16[360,27]{1,0:T(8,128)(2,1)} %constant.12.clone.pick_three) | copy-start | bytes 58324
  3.2 6.5 %collective-permute-start.1 = (bf16[4,64,128]{2,1,0:T(8,128)(2,1)S(1)}, bf16[4,64,128]{2,1,0:T(8,128)(2,1)S(1)}, u32[]{:S(2)}, u32[]{:S(2)}) collective-permute-start(bf16[4,64,128]{2,1,0:T(8,128)(2,1)S(1)} %get-tuple-element.30), channel_id=1, source_target_pairs={{0,16},{1,2},{2,1},{3,4},{4,3},{5,6},{6,5},{7,8},{8,7},{9,10},{10,... | collective-permute-start | bytes 196616 | tf_op jit(solution)/shard_map/ppermute | solution.py:577
  8.0 1.7 %copy-start.6 = (bf16[8,64,128]{2,1,0:T(8,128)(2,1)S(1)}, bf16[8,64,128]{2,1,0:T(8,128)(2,1)}, u32[]{:S(2)}) copy-start(bf16[8,64,128]{2,1,0:T(8,128)(2,1)} %reduce.4) | copy-start | bytes 393220
  11.2 6.1 %collective-permute-start.2 = (bf16[128,128]{1,0:T(8,128)(2,1)S(1)}, bf16[128,128]{1,0:T(8,128)(2,1)S(1)}, u32[]{:S(2)}, u32[]{:S(2)}) collective-permute-start(bf16[128,128]{1,0:T(8,128)(2,1)S(1)} %get-tuple-element.43), channel_id=1, source_target_pairs={{0,1},{1,0},{2,3},{3,2},{4,5},{5,4},{6,7},{7,6},{8,9},{9,8},{10,11... | collective-permute-start | bytes 98312 | tf_op jit(solution)/shard_map/ppermute | solution.py:578
  11.4 5.9 %collective-permute-start.3 = (bf16[128,128]{1,0:T(8,128)(2,1)S(1)}, bf16[128,128]{1,0:T(8,128)(2,1)S(1)}, u32[]{:S(2)}, u32[]{:S(2)}) collective-permute-start(bf16[128,128]{1,0:T(8,128)(2,1)S(1)} %get-tuple-element.44), channel_id=1, source_target_pairs={{0,16},{1,2},{2,1},{3,4},{4,3},{5,6},{6,5},{7,8},{8,7},{9,10},{10,... | collective-permute-start | bytes 98312 | tf_op jit(solution)/shard_map/ppermute | solution.py:577
  12.9 2.4 %copy-start.1 = (bf16[27,128,128]{2,1,0:T(8,128)(2,1)S(1)}, bf16[27,128,128]{2,1,0:T(8,128)(2,1)}, u32[]{:S(2)}) copy-start(bf16[27,128,128]{2,1,0:T(8,128)(2,1)} %kernel.7) | copy-start | bytes 2654212
  15.3 2.0 %copy-start.4 = (bf16[8,128,256]{2,1,0:T(8,128)(2,1)S(1)}, bf16[8,128,256]{2,1,0:T(8,128)(2,1)}, u32[]{:S(2)}) copy-start(bf16[8,128,256]{2,1,0:T(8,128)(2,1)} %reduce.5) | copy-start | bytes 1572868
  15.3 2.0 %copy-start.14 = (bf16[64,64]{1,0:T(8,128)(2,1)S(1)}, bf16[64,64]{1,0:T(8,128)(2,1)}, u32[]{:S(2)}) copy-start(bf16[64,64]{1,0:T(8,128)(2,1)} %constant.14.clone.children) | copy-start | bytes 24580
  17.3 2.0 %copy-start = (bf16[27,256,256]{2,1,0:T(8,128)(2,1)S(1)}, bf16[27,256,256]{2,1,0:T(8,128)(2,1)}, u32[]{:S(2)}) copy-start(bf16[27,256,256]{2,1,0:T(8,128)(2,1)} %kernel.9) | copy-start | bytes 10616836
  18.3 4.0 %collective-permute-start.5 = (bf16[64,256]{1,0:T(8,128)(2,1)S(1)}, bf16[64,256]{1,0:T(8,128)(2,1)S(1)}, u32[]{:S(2)}, u32[]{:S(2)}) collective-permute-start(bf16[64,256]{1,0:T(8,128)(2,1)S(1)} %get-tuple-element.46.third), channel_id=1, source_target_pairs={{0,16},{1,2},{2,1},{3,4},{4,3},{5,6},{6,5},{7,8},{8,7},{9,10},{10,... | collective-permute-start | bytes 98312 | tf_op jit(solution)/shard_map/ppermute | solution.py:577
  18.9 3.4 %collective-permute-start.4 = (bf16[64,256]{1,0:T(8,128)(2,1)S(1)}, bf16[64,256]{1,0:T(8,128)(2,1)S(1)}, u32[]{:S(2)}, u32[]{:S(2)}) collective-permute-start(bf16[64,256]{1,0:T(8,128)(2,1)S(1)} %get-tuple-element.46.third), channel_id=1, source_target_pairs={{0,1},{1,0},{2,3},{3,2},{4,5},{5,4},{6,7},{7,6},{8,9},{9,8},{10,11... | collective-permute-start | bytes 98312 | tf_op jit(solution)/shard_map/ppermute | solution.py:578
where the time goes:
time: 24 us; the launch traced here: 23.7 us
  Pallas kernels  13.4 us (56%)
  starting transfers between devices  5.5 us (23%)
  local copies, waits for them, and re-layouts  2.12 us (9%)
  waiting for transfers between devices  1.88 us (8%)
  between operations  0.85 us (4%)
    pallas_call x9, Pallas kernels, call(): pl.pallas_call(kernel, out_shape=out_shape, in_specs=[ANY if n in remain...  13.4 us
    ppermute x3, starting transfers between devices, exchange(): from_b = lax.ppermute(to_b, axes, across)  4.69 us
    unnamed x30, local copies, waits for them, and re-layouts  2.12 us
    ppermute x3, waiting for transfers between devices, exchange(): from_b = lax.ppermute(to_b, axes, across)  1.87 us
    ppermute x3, starting transfers between devices, exchange(): return (lax.ppermute(to_a, axes, within), from_b)  0.82 us
  transfers between devices with their start and end apart: 6, of which 1 were waited for; matrix products, arithmetic and copies ran while one was open for 0% of the time, Pallas kernels for 39%

commit v1 on v0

--- a/solution.py
+++ b/solution.py
@@ -9,7 +9,6 @@
 F32 = jnp.float32
 BF16 = jnp.bfloat16
 LINE = "morton"
-TAPS = [(a, q) for a in range(3) for q in range(9)]
 
 
 def dot(x, y):
@@ -59,67 +58,10 @@
     return [jnp.where(n < 0, count, n + shift) for n in numbers]
 
 
-def edges_kernel(features, occupancy, to_a, to_b, columns, words, arrived):
-    count = words.shape[0]
-    last = features.shape[2] - 128
-    copies = [
-        pltpu.make_async_copy(occupancy, words, arrived.at[0]),
-        pltpu.make_async_copy(features.at[:, :, pl.ds(0, 128)], columns.at[0], arrived.at[1]),
-        pltpu.make_async_copy(features.at[:, :, pl.ds(last, 128)], columns.at[1], arrived.at[2]),
-    ]
-    for copy in copies:
-        copy.start()
-    for copy in copies:
-        copy.wait()
-    bits = [column_bits(words[...], 0), column_bits(words[...], last // 128)]
-    lane = iota((64, 128), 1)
-    odd = on_odd_place()
-    for q in range(count // 2):
-        low, high = [
-            [columns[side, b].astype(F32) * bits[side][b : b + 1] for b in (2 * q, 2 * q + 1)]
-            for side in range(2)
-        ]
-        lows = jnp.where(lane < 64, low[0], pltpu.roll(low[1], 64, 1))
-        highs = jnp.where(lane < 64, pltpu.roll(high[0], 64, 1), high[1])
-        to_a[q] = jnp.where(odd, lows, highs).astype(BF16)
-        to_b[q] = jnp.where(odd, highs, lows).astype(BF16)
-
-
-def tables_kernel(
-    neighbours, occupancy, pick_two, add_two, pick_three, add_three,
-    own_two, low_two, high_two, own_three, faces_three, pair_words, mask_two, mask_three,
-):
-    count = neighbours.shape[0]
-    number = neighbours[...]
-    tap = iota(number.shape, 1)
-    shift = jnp.where(tap < 9, count, jnp.where(tap < 18, 0, -count))
-    slot = jnp.where(
-        number < 0, 4 * count, number + shift - lax.axis_index(LINE) * count
-    ).astype(BF16)
-    across = (((1,), (1,)), ((), ()))
-    rows = lax.dot_general(pick_two[...], slot, across, preferred_element_type=F32)
-    rows = (rows + add_two[...]).astype(jnp.int32)
-    lane = iota((16, 16 * count), 1)
-    for a, table in enumerate((low_two, own_two, high_two)):
-        for q in range(9):
-            for b in range(count):
-                at = 16 * (9 * a + q)
-                table[16 * (count * q + b) : 16 * (count * q + b + 1), :] = jnp.where(
-                    rows[at : at + 16, b : b + 1] == lane, 1.0, 0.0
-                ).astype(BF16)
-    rows = lax.dot_general(pick_three[...], slot, across, preferred_element_type=F32)
-    rows = (rows + add_three[...]).astype(jnp.int32)
-    for table, begin in ((own_three, 0), (faces_three, 27)):
-        lane = iota((8, table.shape[1]), 1)
-        for q in range(table.shape[0] // (8 * count)):
-            at = 8 * (begin + q)
-            table[8 * count * q : 8 * count * (q + 1), :] = stack(
-                [
-                    jnp.where(rows[at : at + 8, b : b + 1] == lane, 1.0, 0.0)
-                    for b in range(count)
-                ]
-            ).astype(BF16)
-
+def masks_kernel(occupancy, bits, pair_words, mask_two, mask_three):
+    count = occupancy.shape[0]
+    for q in range(4):
+        bits[q] = column_bits(occupancy[...], q)
     words = [word_lanes(occupancy[...], w) for w in range(16)]
     lane = iota((count, 128), 1)
     row = iota((8, 128), 0)
@@ -157,6 +99,88 @@
         mask_three[8 * b : 8 * (b + 1)] = beside([mask, mask])
 
 
+def edges_kernel(features, bits, to_a, to_b):
+    last = features.shape[2] - 128
+    lane = iota((64, 128), 1)
+    odd = on_odd_place()
+    for q in range(features.shape[0] // 2):
+        low, high = [
+            [
+                features[b, :, column * last : column * last + 128].astype(F32)
+                * bits[3 * column, b : b + 1]
+                for b in (2 * q, 2 * q + 1)
+            ]
+            for column in range(2)
+        ]
+        lows = jnp.where(lane < 64, low[0], pltpu.roll(low[1], 64, 1))
+        highs = jnp.where(lane < 64, pltpu.roll(high[0], 64, 1), high[1])
+        to_a[q] = jnp.where(odd, lows, highs).astype(BF16)
+        to_b[q] = jnp.where(odd, highs, lows).astype(BF16)
+
+
+def slot_rows(neighbours):
+    count = neighbours.shape[0]
+    number = neighbours[...]
+    tap = iota(number.shape, 1)
+    shift = jnp.where(tap < 9, count, jnp.where(tap < 18, 0, -count))
+    slot = jnp.where(
+        number < 0, 4 * count, number + shift - lax.axis_index(LINE) * count
+    ).astype(F32)
+    return stack(
+        [jnp.broadcast_to(slot[b : b + 1], (128, number.shape[1])) for b in range(count)]
+    ).astype(BF16)
+
+
+def times_transposed(x, y):
+    return lax.dot_general(x, y, (((1,), (1,)), ((), ())), preferred_element_type=F32)
+
+
+def level_two_tables_kernel(neighbours, pick, own_two, low_two, high_two):
+    count = neighbours.shape[0]
+    rows = times_transposed(pick[...], slot_rows(neighbours))
+    lane = iota((16, 16 * count), 1)
+    row = iota((16, 16 * count), 0)
+    j, k = lax.shift_right_logical(row, 2), jnp.bitwise_and(row, 3)
+    for q in range(9):
+        source = 4 * jnp.bitwise_and(j + q // 3 + 3, 3) + jnp.bitwise_and(k + q % 3 + 3, 3)
+        wanted = (lane - source).astype(F32)
+        for a, table in enumerate((low_two, own_two, high_two)):
+            at = 16 * (9 * a + q)
+            for b in range(count):
+                table[16 * (count * q + b) : 16 * (count * q + b + 1), :] = jnp.where(
+                    rows[at : at + 16, 128 * b : 128 * b + 16 * count] == wanted, 1.0, 0.0
+                ).astype(BF16)
+
+
+def level_three_tables_kernel(neighbours, pick, later, own_three, faces_three):
+    count = neighbours.shape[0]
+    rows = times_transposed(pick[...], slot_rows(neighbours))
+    row = iota((8, 128), 0)
+    voxel = [jnp.bitwise_and(lax.shift_right_logical(row, s), 1) for s in (2, 1, 0)]
+    lane = iota((8, 128), 1)
+    at = base = 0
+    for table, sides in ((own_three, (0,)), (faces_three, (-1, 1))):
+        for side in sides:
+            for tap in range(27):
+                if side and tap // 9 != side + 1:
+                    continue
+                shift = (tap // 9 - 1, tap // 3 % 3 - 1, tap % 3 - 1)
+                x, y, z = [v + d for v, d in zip(voxel, shift)]
+                here = (x < 0) if side < 0 else (x > 1) if side else (x >= 0) & (x <= 1)
+                x, y, z = [jnp.bitwise_and(v + 2, 1) for v in (x, y, z)]
+                source = 4 * x + 2 * y + z + (8 * count if side > 0 else 0)
+                wanted = jnp.where(here, lane - source, -1).astype(F32)
+                tiles = [
+                    jnp.where(rows[at : at + 8, 128 * b : 128 * (b + 1)] == wanted, 1.0, 0.0)
+                    for b in range(count)
+                ]
+                table[count * at - base : count * (at + 8) - base, :] = stack(tiles)[
+                    :, : table.shape[1]
+                ].astype(BF16)
+                at += 8
+        base = count * at
+
+
 def shifted_windows(source, row):
     shifted = []
     for j in range(-1, 9):
@@ -176,9 +200,9 @@
 
 
 def outer_kernel(
-    neighbours, occupancy, features, kernel,
-    padded, taps, face_taps, partial,
-    pairs, low_edge, high_edge, numbers, arrived,
+    neighbours, bits, features, kernel, reduce,
+    middle, taps, face_taps, reduce_taps, partial,
+    tables, windows, wrap_taps, numbers, arrived,
 ):
     count = features.shape[0]
     first = lax.axis_index(LINE) * count
@@ -190,67 +214,74 @@
     none = jnp.zeros((64, 64), F32)
     for q in range(9):
         w = [kernel[9 * a + q].astype(F32) for a in range(3)]
-        taps[q * 256 : (q + 1) * 256, :] = stack(
-            [beside([w[p] if p < 3 else none, w[p - 1] if p else none]) for p in range(4)]
+        rows = slice(q * 128, (q + 1) * 128)
+        taps[rows, :] = stack(
+            [beside([w[2], w[1], w[0], none]), beside([none, w[2], w[1], w[0]])]
         ).astype(BF16)
-        face_taps[q * 128 : (q + 1) * 128, :] = stack(
-            [beside([w[0], none]), beside([none, w[2]])]
+        wrap_taps[rows, :] = stack(
+            [beside([w[2], w[1], none, none]), beside([none, none, w[1], w[0]])]
         ).astype(BF16)
-
-    for table in (pairs.at[0], pairs.at[1], pairs.at[2], low_edge, high_edge):
-        table[count] = jnp.zeros((64, 128), F32)
-    bits = [column_bits(occupancy[...], q) for q in range(4)]
+        face_taps[rows, :] = stack([beside([w[0], none]), beside([none, w[2]])]).astype(BF16)
+
+    reduce_taps[...] = stack(
+        [
+            beside([reduce[4 * ci + 2 * cj], reduce[4 * ci + 2 * cj + 1]])
+            for cj in range(2)
+            for ci in range(2)
+        ]
+    )
+
+    for pair in range(4):
+        tables[pair, count] = jnp.zeros((64, 128), F32)
     for b in range(count):
         cols = [
-            features[b, :, 128 * q : 128 * (q + 1)].astype(F32) * bits[q][b : b + 1]
+            features[b, :, 128 * q : 128 * (q + 1)].astype(F32) * bits[q, b : b + 1]
             for q in range(4)
         ]
         rolled = [pltpu.roll(col, 64, 1) for col in cols]
-        m = stack(
-            [
-                jnp.where(lane < 64, rolled[0], cols[1]),
-                jnp.where(lane < 64, cols[1], rolled[2]),
-            ]
-        ).T
-        pairs[0, b] = m[:64]
-        pairs[1, b] = m[64:]
-        m = stack(
-            [
-                jnp.where(lane < 64, rolled[2], cols[3]),
-                jnp.where(lane < 64, cols[3], rolled[0]),
-            ]
-        ).T
-        pairs[2, b] = m[:64]
-        low_edge[b] = jnp.where(lane < 64, 0.0, m[64:])
-        high_edge[b] = jnp.where(lane < 64, m[64:], 0.0)
+        for p in (0, 2):
+            m = stack(
+                [
+                    jnp.where(lane < 64, rolled[p], cols[p + 1]),
+                    jnp.where(lane < 64, cols[p + 1], rolled[(p + 2) % 4]),
+                ]
+            ).T
+            tables[p, b] = m[:64]
+            tables[p + 1, b] = m[64:]
 
     copy.wait()
-    tables = [low_edge, pairs.at[0], pairs.at[1], pairs.at[2], high_edge]
     for b in range(count):
         slot = slots_of(numbers, first, count, b, 9)
-        for pair in range(5):
-            windows = shifted_windows(
-                lambda q, j: tables[pair][slot[q], pl.ds(8 * j, 8), :], row
-            )
+        for pair in range(4):
+            tiles = shifted_windows(lambda q, j: tables[pair, slot[q], pl.ds(8 * j, 8), :], row)
             for jr in range(6):
                 for e in range(3):
-                    padded[b, e, pair, jr] = windows[jr][e]
+                    if pair == 1:
+                        middle[b, e, jr] = tiles[jr][e]
+                    else:
+                        windows[b, e, pair, jr] = tiles[jr][e]
 
     group = count // 2
     for g in range(2):
         bricks = slice(g * group, (g + 1) * group)
-        for side in range(2):
-            partial[side, g * group * 64 : (g + 1) * group * 64] = dot(
+        rows = slice(g * group * 64, (g + 1) * group * 64)
+        low, high, wrap = [
+            dot(
                 beside(
                     [
-                        padded[bricks, e, 3 * side + p, c : c + 4].reshape(group * 64, 128)
+                        windows[bricks, e, pair, c : c + 4].reshape(group * 64, 128)
                         for c in range(3)
                         for e in range(3)
-                        for p in range(2)
                     ]
                 ),
-                taps[...],
+                weights[...],
             )
+            for pair, weights in ((0, taps), (2, taps), (3, wrap_taps))
+        ]
+        partial[0, rows] = low[:, :128] + wrap[:, 128:]
+        partial[1, rows] = low[:, 128:]
+        partial[2, rows] = high[:, :128]
+        partial[3, rows] = high[:, 128:] + wrap[:, :128]
 
 
 def masked_tiles(sums, pair_words, b, i):
@@ -266,18 +297,11 @@
     return [tiles[j] for j in range(8)]
 
 
-def reduce_planes(groups, reduce, low_sums, high_sums):
+def reduce_planes(groups, weights, low_sums, high_sums):
     left = stack(
         [beside([tiles[j], tiles[j + 1]]) for tiles in groups for j in (0, 2, 4, 6)]
     ).astype(BF16)
-    weights = stack(
-        [
-            beside([reduce[4 * ci + 2 * cj], reduce[4 * ci + 2 * cj + 1]])
-            for cj in range(2)
-            for ci in range(2)
-        ]
-    )
-    sums = dot(left, weights)
+    sums = dot(left, weights[...])
     low_sums[...] = sums[:, :128]
     high_sums[...] = sums[:, 128:]
     return [
@@ -333,7 +357,7 @@
         at = slice(64 * b, 64 * (b + 1))
         for side in range(2):
             near = (lane < 64) == (side == 0)
-            sums = partial[side, at] + jnp.where(near, added[at], 0.0)
+            sums = partial[3 * side, at] + jnp.where(near, added[at], 0.0)
             groups.append(masked_tiles(sums, pair_words, b, 3 * side))
             outer[b, side] = stack(groups[-1]).astype(BF16)
     sums = reduce_planes(groups, reduce, low_sums, high_sums)
@@ -350,29 +374,28 @@
 
 
 def inner_kernel(
-    padded, taps, outer, reduce, pair_words, mask_two,
-    result, second,
-    out, low_sums, high_sums, stored,
+    middle, taps, partial, outer, reduce, pair_words, mask_two,
+    out, second,
+    low_sums, high_sums,
 ):
-    count = padded.shape[0]
+    count = middle.shape[0]
     lane = iota((64, 128), 1)
-    total = dot(
+    added = dot(
         beside(
             [
-                padded[:, e, 1 + p : 3 + p, c : c + 4].reshape(count * 128, 128)
+                middle[:, e, c : c + 4].reshape(count * 64, 128)
                 for c in range(3)
                 for e in range(3)
-                for p in range(2)
             ]
         ),
         taps[...],
     )
     groups = []
-    copies = []
     for b in range(count):
         for i in (1, 2):
-            at = 128 * b + 64 * (i - 1)
-            groups.append(masked_tiles(total[at : at + 64], pair_words, b, i))
+            at = slice(64 * b, 64 * (b + 1))
+            sums = partial[i, at] + added[at, 128 * (i - 1) : 128 * i]
+            groups.append(masked_tiles(sums, pair_words, b, i))
         ordered = [
             outer[b, 0].astype(F32),
             stack(groups[2 * b]),
@@ -388,8 +411,6 @@
             out[b, :, 128 * (i + 1) : 128 * (i + 2)] = jnp.where(
                 lane < 64, pltpu.roll(top, 64, 1), bottom
             ).astype(BF16)
-        copies.append(pltpu.make_async_copy(out.at[b], result.at[b], stored.at[b]))
-        copies[-1].start()
     sums = reduce_planes(groups, reduce, low_sums, high_sums)
     for b in range(count):
         at = slice(16 * b, 16 * (b + 1))
@@ -397,29 +418,36 @@
             second[i - 1, at] = (
                 jnp.maximum(sums[2 * b + i - 1], 0.0) * mask_two[i, at]
             ).astype(BF16)
-    for copy in copies:
-        copy.wait()
-
-
-def own_two_kernel(outer, inner, gather, kernel, partial):
+
+
+def own_two_kernel(outer, inner, gather, kernel, first, partial, result, stored):
+    copy = pltpu.make_async_copy(first, result, stored)
+    copy.start()
     rows = outer.shape[1]
     planes = beside([outer[0], inner[0], inner[1], outer[1]])
     moved = dot(gather[...], planes).astype(BF16)
-    none = jnp.zeros((rows, 128), BF16)
     left = beside(
         [
             stack(
                 [
-                    moved[q * rows : (q + 1) * rows, 128 * (i + a - 1) : 128 * (i + a)]
-                    if 0 <= i + a - 1 < 4
-                    else none
+                    moved[q * rows : (q + 1) * rows, 128 * i : 128 * (i + 1)]
                     for i in range(4)
                 ]
             )
-            for a, q in TAPS
-        ]
-    )
-    partial[...] = dot(left, kernel[...].reshape(27 * 128, 128))
+            for q in range(9)
+        ]
+    )
+    weights = [kernel[9 * a : 9 * (a + 1)].reshape(9 * 128, 128) for a in range(3)]
+    sums = dot(left, beside(weights[:2]))
+    later = dot(left[rows:], weights[2])
+    for i in range(4):
+        total = sums[i * rows : (i + 1) * rows, 128:]
+        if i:
+            total = total + sums[(i - 1) * rows : i * rows, :128]
+        if i < 3:
+            total = total + later[i * rows : (i + 1) * rows]
+        partial[i * rows : (i + 1) * rows] = total
+    copy.wait()
 
 
 def faces_two_kernel(
@@ -485,30 +513,27 @@
     out[...] = (jnp.maximum(sums, 0.0) * mask_three[...]).astype(BF16).reshape(out.shape)
 
 
-def level_two_rows(count):
+def level_two_picks():
     pick = np.zeros((432, 27), np.float32)
-    add = np.zeros((432, count), np.float32)
-    for a in range(3):
-        for q in range(9):
-            for r in range(16):
-                y, z = r // 4 + q // 3 - 1, r % 4 + q % 3 - 1
-                at = 16 * (9 * a + q) + r
-                pick[at, 9 * a + 3 * (y // 4 + 1) + z // 4 + 1] = 16
-                add[at] = 4 * (y % 4) + z % 4
-    return jnp.asarray(pick, BF16), jnp.asarray(add)
-
-
-def level_three_rows(count):
-    pick = np.zeros((360, 27), np.float32)
-    add = np.full((360, count), -1, np.float32)
+    for tap in range(27):
+        for r in range(16):
+            y, z = r // 4 + tap // 3 % 3 - 1, r % 4 + tap % 3 - 1
+            pick[16 * tap + r, tap // 9 * 9 + 3 * (y // 4 + 1) + z // 4 + 1] = 16
+    return jnp.asarray(pick, BF16)
+
+
+def level_three_picks():
+    pick = np.zeros((45 * 8, 27), np.float32)
     for tap in range(27):
         for u in range(8):
-            x, y, z = (u >> 2) + tap // 9 - 1, ((u >> 1) & 1) + tap // 3 % 3 - 1, (u & 1) + tap % 3 - 1
+            x, y, z = [
+                ((u >> s) & 1) + d - 1
+                for s, d in ((2, tap // 9), (1, tap // 3 % 3), (0, tap % 3))
+            ]
             side = x // 2
-            at = 8 * tap if side == 0 else 8 * (27 + tap) if side < 0 else 8 * (36 + tap - 18)
+            at = 8 * (tap + (0, 18, 27)[side])
             pick[at + u, 9 * (side + 1) + 3 * (y // 2 + 1) + z // 2 + 1] = 8
-            add[at + u] = 4 * (x % 2) + 2 * (y % 2) + z % 2 + (8 * count if side > 0 else 0)
-    return jnp.asarray(pick, BF16), jnp.asarray(add)
+    return jnp.asarray(pick, BF16)
 
 
 def child_rows():
@@ -537,7 +562,7 @@
         scratch_shapes=scratch,
         compiler_params=pltpu.CompilerParams(vmem_limit_bytes=24 * 1024 * 1024),
         cost_estimate=pl.CostEstimate(
-            flops=cost * 10**9, bytes_accessed=10**7, transcendentals=0
+            flops=int(cost * 10**10), bytes_accessed=10**7, transcendentals=0
         ),
     )(*args)
 
@@ -578,50 +603,43 @@
         return lax.ppermute(to_a, axes, within), from_b
 
     face = shape((count // 2, 64, 128), BF16)
-    from_a, from_b = exchange(
-        *call(
-            edges_kernel,
-            1,
-            (face, face),
-            [
-                pltpu.VMEM((2, count, 64, 128), BF16),
-                pltpu.VMEM(occupancy.shape, jnp.int32),
-                DMA((3,)),
-            ],
-            features, occupancy,
-            remain=(0, 1),
-        )
-    )
-    own_two, low_two, high_two, own_three, faces_three, pair_words, mask_two, mask_three = call(
-        tables_kernel,
-        1,
-        (shape((9 * 16 * count, 16 * count), BF16),) * 3
-        + (
-            shape((27 * 8 * count, 8 * count), BF16),
-            shape((18 * 8 * count, 16 * count), BF16),
+    bits, pair_words, mask_two, mask_three = call(
+        masks_kernel,
+        0.3,
+        (
+            shape((4, count, 128), F32),
             shape((8, count, 128), jnp.int32),
             shape((4, 16 * count, 128), F32),
             shape((8 * count, 256), F32),
         ),
         [],
-        neighbours, occupancy, *level_two_rows(count), *level_three_rows(count),
-    )
-    padded, taps, face_taps, partial = call(
+        occupancy,
+    )
+    from_a, from_b = exchange(*call(edges_kernel, 0.3, (face, face), [], features, bits))
+    own_two, low_two, high_two = call(
+        level_two_tables_kernel,
+        0.4,
+        (shape((9 * 16 * count, 16 * count), BF16),) * 3,
+        [],
+        neighbours, level_two_picks(),
+    )
+    middle, taps, face_taps, reduce_taps, partial = call(
         outer_kernel,
-        4,
+        2.0,
         (
-            shape((count, 3, 5, 6, 16, 128), BF16),
-            shape((9 * 256, 128), BF16),
+            shape((count, 3, 6, 16, 128), BF16),
+            shape((9 * 128, 256), BF16),
             shape((9 * 128, 128), BF16),
-            shape((2, count * 64, 128), F32),
+            shape((256, 256), BF16),
+            shape((4, count * 64, 128), F32),
         ),
         [
-            pltpu.VMEM((3, count + 1, 64, 128), F32),
-            pltpu.VMEM((count + 1, 64, 128), F32),
-            pltpu.VMEM((count + 1, 64, 128), F32),
+            pltpu.VMEM((4, count + 1, 64, 128), F32),
+            pltpu.VMEM((count, 3, 4, 6, 16, 128), BF16),
+            pltpu.VMEM((9 * 128, 256), BF16),
         ]
         + scalars,
-        neighbours, occupancy, features, conv_one,
+        neighbours, bits, features, conv_one, first_reduce_kernel,
         remain=(0,),
     )
     plane = shape((16 * count, 128), BF16)
@@ -629,7 +647,7 @@
     sums = pltpu.VMEM((count * 64, 128), F32)
     outer, outer_two, to_a, to_b = call(
         faces_one_kernel,
-        2,
+        1.5,
         (shape((count, 2, 64, 128), BF16), planes, plane, plane),
         [
             pltpu.VMEM((count + 1, 64, 128), F32),
@@ -638,29 +656,29 @@
             sums,
         ]
         + scalars,
-        neighbours, from_a, from_b, face_taps, partial, first_reduce_kernel, pair_words, mask_two,
+        neighbours, from_a, from_b, face_taps, partial, reduce_taps, pair_words, mask_two,
         remain=(0,),
     )
     from_a, from_b = exchange(to_a, to_b)
 
     first_level, inner_two = call(
         inner_kernel,
-        4,
+        1.2,
         (shape(features.shape, BF16), planes),
-        [pltpu.VMEM(features.shape, BF16), sums, sums, DMA((count,))],
-        padded, taps, outer, first_reduce_kernel, pair_words, mask_two,
-        store=(0,),
-    )
-    partial = call(
+        [sums, sums],
+        middle, taps, partial, outer, reduce_taps, pair_words, mask_two,
+    )
+    partial, first_level = call(
         own_two_kernel,
-        2,
-        shape((4 * 16 * count, 128), F32),
-        [],
-        outer_two, inner_two, own_two, conv_two,
+        1.0,
+        (shape((4 * 16 * count, 128), F32), shape(features.shape, BF16)),
+        [DMA(())],
+        outer_two, inner_two, own_two, conv_two, first_level,
+        store=(1,),
     )
     second_level, third = call(
         faces_two_kernel,
-        2,
+        0.9,
         (shape((count, 64, 128), BF16), shape((8 * count, 256), BF16)),
         [],
         low_two, high_two, child_rows(), partial, from_a, from_b, conv_two, second_reduce_kernel,
@@ -668,9 +686,16 @@
     )
     from_a, from_b = exchange(third, third)
 
+    own_three, faces_three = call(
+        level_three_tables_kernel,
+        0.4,
+        (shape((27 * 8 * count, 8 * count), BF16), shape((18 * 8 * count, 16 * count), BF16)),
+        [],
+        neighbours, level_three_picks(), third,
+    )
     partial, second_level = call(
         own_three_kernel,
-        2,
+        1.0,
         (shape((8 * count, 256), F32), shape(second_level.shape, BF16)),
         [DMA(())],
         own_three, third, conv_three, second_level,

time: 24 us -> 20.6 us (0.86)
  Pallas kernels: 13.4 us -> 9.88 us
  starting transfers between devices: 5.5 us -> 7.46 us
  waiting for transfers between devices: 1.88 us -> 0.94 us
  local copies, waits for them, and re-layouts: 2.12 us -> 1.28 us
    pallas_call x9 -> x11, Pallas kernels: 13.4 us -> 9.88 us  [call(): pl.pallas_call(kernel, out_shape=out_shape, in_specs=[ANY if n in remain...]
    ppermute x3, starting transfers between devices: 4.69 us -> 5.9 us  [exchange(): from_b = lax.ppermute(to_b, axes, across)]
    ppermute x3, waiting for transfers between devices: 1.87 us -> 0.93 us  [exchange(): from_b = lax.ppermute(to_b, axes, across)]
    unnamed x30 -> x22, local copies, waits for them, and re-layouts: 2.12 us -> 1.28 us
    ppermute x3, starting transfers between devices: 0.82 us -> 1.56 us  [exchange(): return (lax.ppermute(to_a, axes, within), from_b)]
  transfers between devices with their start and end apart: 6 -> 6, of which waited for: 1 -> 1; matrix products, arithmetic and copies ran while one was open for 0% -> 0% of each run, Pallas kernels for 39% -> 28%
where the time goes in v1:
time: 20.6 us; the launch traced here: 20.4 us
  Pallas kernels  9.88 us (48%)
  starting transfers between devices  7.46 us (36%)
  local copies, waits for them, and re-layouts  1.28 us (6%)
  waiting for transfers between devices  0.94 us (5%)
  between operations  0.79 us (4%)
    pallas_call x11, Pallas kernels, call(): pl.pallas_call(kernel, out_shape=out_shape, in_specs=[ANY if n in remain...  9.88 us
    ppermute x3, starting transfers between devices, exchange(): from_b = lax.ppermute(to_b, axes, across)  5.9 us
    ppermute x3, starting transfers between devices, exchange(): return (lax.ppermute(to_a, axes, within), from_b)  1.56 us
    unnamed x22, local copies, waits for them, and re-layouts  1.28 us
    ppermute x3, waiting for transfers between devices, exchange(): from_b = lax.ppermute(to_b, axes, across)  0.93 us
  transfers between devices with their start and end apart: 6, of which 1 were waited for; matrix products, arithmetic and copies ran while one was open for 0% of the time, Pallas kernels for 28%

profile of v1, /device:TPU:0, one launch (start us, length us, event | category | flops | bytes accessed | tf_op | source)
XLA Modules:
  0.0 20.4 jit_solution(7412501167479389811)
XLA Ops:
  0.6 0.0 copy-start.2
  0.6 0.0 copy-start.6
  0.6 0.7 %copy-done.6 = s32[8,16]{1,0:T(8,128)S(1)} copy-done((s32[8,16]{1,0:T(8,128)S(1)}, s32[8,16]{1,0:T(8,128)}, u32[]{:S(2)}) %copy-start.6) | copy-done | bytes 536
  1.4 0.1 shard_map.130
  1.5 0.1 copy-done.2
  1.7 0.0 copy-start.4
  1.7 0.0 copy-start.5
  1.7 0.0 copy-start.7
  1.7 0.1 shard_map.131
  1.8 0.5 %collective-permute-start = (bf16[4,64,128]{2,1,0:T(8,128)(2,1)S(1)}, bf16[4,64,128]{2,1,0:T(8,128)(2,1)S(1)}, u32[]{:S(2)}, u32[]{:S(2)}) collective-permute-start(bf16[4,64,128]{2,1,0:T(8,128)(2,1)S(1)} %get-tuple-element.32), channel_id=1, source_target_pairs={{0,1},{1,0},{2,3},{3,2},{4,5},{5,4},{6,7},{7,6},{8,9},{9,8},{10,11... | collective-permute-start | bytes 196616 | tf_op jit(solution)/shard_map/ppermute | solution.py:603
  2.3 0.0 copy-start.8
  2.3 2.6 %collective-permute-start.1 = (bf16[4,64,128]{2,1,0:T(8,128)(2,1)S(1)}, bf16[4,64,128]{2,1,0:T(8,128)(2,1)S(1)}, u32[]{:S(2)}, u32[]{:S(2)}) collective-permute-start(bf16[4,64,128]{2,1,0:T(8,128)(2,1)S(1)} %get-tuple-element.33), channel_id=1, source_target_pairs={{0,16},{1,2},{2,1},{3,4},{4,3},{5,6},{6,5},{7,8},{8,7},{9,10},{10,... | collective-permute-start | bytes 196616 | tf_op jit(solution)/shard_map/ppermute | solution.py:602
  4.9 0.0 copy-done.4
  4.9 0.0 copy-done.5
  4.9 0.0 copy-done.7
  4.9 1.9 %shard_map.132 = (bf16[8,3,6,16,128]{4,3,2,1,0:T(8,128)(2,1)S(1)}, bf16[1152,256]{1,0:T(8,128)(2,1)S(1)}, bf16[1152,128]{1,0:T(8,128)(2,1)S(1)}, bf16[256,256]{1,0:T(8,128)(2,1)S(1)}, f32[4,512,128]{2,1,0:T(8,128)S(1)}) custom-call(s32[8,27]{1,0:T(8,128)S(1)} %copy-done.7, f32[4,8,128]{2,1,0:T(8,128)S(1)} %get-tuple-element.31.bits, ...), custom_call_target="tpu_custom_call" | custom-call | flops 20000000000 | bytes 10000000 | tf_op jit(solution)/shard_map/pallas_call | solution.py:557
  6.9 0.0 copy-done.8
  6.9 0.4 %shard_map.135 = (bf16[1152,128]{1,0:T(8,128)(2,1)S(1)}, bf16[1152,128]{1,0:T(8,128)(2,1)S(1)}, bf16[1152,128]{1,0:T(8,128)(2,1)S(1)}) custom-call(s32[8,27]{1,0:T(8,128)S(1)} %copy-done.7, bf16[432,27]{1,0:T(8,128)(2,1)S(1)} %copy-done.8), custom_call_target="tpu_custom_call" | custom-call | flops 4000000000 | bytes 10000000 | tf_op jit(solution)/shard_map/pallas_call | solution.py:557
  7.3 0.0 collective-permute-done.from_a
  7.3 0.0 collective-permute-done.1.from_b
  7.3 1.4 %shard_map.133 = (bf16[8,2,64,128]{3,2,1,0:T(8,128)(2,1)S(1)}, bf16[2,128,128]{2,1,0:T(8,128)(2,1)S(1)}, bf16[128,128]{1,0:T(8,128)(2,1)S(1)}, bf16[128,128]{1,0:T(8,128)(2,1)S(1)}) custom-call(s32[8,27]{1,0:T(8,128)S(1)} %copy-done.7, bf16[4,64,128]{2,1,0:T(8,128)(2,1)S(1)} %collective-permute-done.from_a, ...), custom_call_target="tpu_custom_call" | custom-call | flops 15000000512 | bytes 10000000 | tf_op jit(solution)/shard_map/pallas_call | solution.py:557
  8.7 0.2 %collective-permute-start.2 = (bf16[128,128]{1,0:T(8,128)(2,1)S(1)}, bf16[128,128]{1,0:T(8,128)(2,1)S(1)}, u32[]{:S(2)}, u32[]{:S(2)}) collective-permute-start(bf16[128,128]{1,0:T(8,128)(2,1)S(1)} %get-tuple-element.50), channel_id=1, source_target_pairs={{0,1},{1,0},{2,3},{3,2},{4,5},{5,4},{6,7},{7,6},{8,9},{9,8},{10,11... | collective-permute-start | bytes 98312 | tf_op jit(solution)/shard_map/ppermute | solution.py:603
  8.9 1.8 %collective-permute-start.3 = (bf16[128,128]{1,0:T(8,128)(2,1)S(1)}, bf16[128,128]{1,0:T(8,128)(2,1)S(1)}, u32[]{:S(2)}, u32[]{:S(2)}) collective-permute-start(bf16[128,128]{1,0:T(8,128)(2,1)S(1)} %get-tuple-element.51), channel_id=1, source_target_pairs={{0,16},{1,2},{2,1},{3,4},{4,3},{5,6},{6,5},{7,8},{8,7},{9,10},{10,... | collective-permute-start | bytes 98312 | tf_op jit(solution)/shard_map/ppermute | solution.py:602
  10.8 0.0 copy-start.1
  10.8 1.0 %shard_map.134 = (bf16[8,64,512]{2,1,0:T(8,128)(2,1)S(1)}, bf16[2,128,128]{2,1,0:T(8,128)(2,1)S(1)}) custom-call(bf16[8,3,6,16,128]{4,3,2,1,0:T(8,128)(2,1)S(1)} %get-tuple-element.40.middle, bf16[1152,256]{1,0:T(8,128)(2,1)S(1)} %get-tuple-element.41.taps, f32[4,512,128]{2,1,0:T(8,128)S(1)} %get-tuple-element.35.partial, ...), custom_call_target="tpu_custom_call" | custom-call | flops 12000000000 | bytes 10000000 | tf_op jit(solution)/shard_map/pallas_call | solution.py:557
  11.7 0.2 copy-done.1
  11.9 0.0 copy-start.3
  11.9 0.0 copy-start.10
  11.9 1.0 %shard_map.136 = (f32[512,128]{1,0:T(8,128)S(1)}, bf16[8,64,512]{2,1,0:T(8,128)(2,1)}) custom-call(bf16[2,128,128]{2,1,0:T(8,128)(2,1)S(1)} %get-tuple-element.39.outer, bf16[2,128,128]{2,1,0:T(8,128)(2,1)S(1)} %get-tuple-element.43.inner, bf16[1152,128]{1,0:T(8,128)(2,1)S(1)} %get-tuple-element.44.gather, bf16[27,128,128]{2,1,0:T(8,128)(2,1)S(1)} %copy-done.1, ...), custom_call_target="tpu_custom_call" | custom-call | flops 10000000000 | bytes 10000000 | tf_op jit(solution)/shard_map/pallas_call | solution.py:557
  13.0 0.0 collective-permute-done.2.from_a
  13.0 0.0 collective-permute-done.3.from_b
  13.0 0.2 copy-done.3
  13.2 0.0 copy-done.10
  13.2 0.0 copy-start.9
  13.2 1.0 %shard_map.137 = (bf16[8,64,128]{2,1,0:T(8,128)(2,1)S(1)}, bf16[64,256]{1,0:T(8,128)(2,1)S(1)}) custom-call(bf16[1152,128]{1,0:T(8,128)(2,1)S(1)} %get-tuple-element.47.low_gather, bf16[1152,128]{1,0:T(8,128)(2,1)S(1)} %get-tuple-element.48.high_gather, bf16[64,64]{1,0:T(8,128)(2,1)S(1)} %copy-done.10, f32[512,128]{1,0:T(8,128)S(1)} %get-tuple-element.49.partial, ...), custom_call_target="tpu_custom_call" | custom-call | flops 8999999488 | bytes 10000000 | tf_op jit(solution)/shard_map/pallas_call | solution.py:557
  14.1 0.0 copy-start
  14.1 0.8 %collective-permute-start.4 = (bf16[64,256]{1,0:T(8,128)(2,1)S(1)}, bf16[64,256]{1,0:T(8,128)(2,1)S(1)}, u32[]{:S(2)}, u32[]{:S(2)}) collective-permute-start(bf16[64,256]{1,0:T(8,128)(2,1)S(1)} %get-tuple-element.53.later.third), channel_id=1, source_target_pairs={{0,1},{1,0},{2,3},{3,2},{4,5},{5,4},{6,7},{7,6},{8,9},{9,8},{10,11... | collective-permute-start | bytes 98312 | tf_op jit(solution)/shard_map/ppermute | solution.py:603
  15.0 1.5 %collective-permute-start.5 = (bf16[64,256]{1,0:T(8,128)(2,1)S(1)}, bf16[64,256]{1,0:T(8,128)(2,1)S(1)}, u32[]{:S(2)}, u32[]{:S(2)}) collective-permute-start(bf16[64,256]{1,0:T(8,128)(2,1)S(1)} %get-tuple-element.53.later.third), channel_id=1, source_target_pairs={{0,16},{1,2},{2,1},{3,4},{4,3},{5,6},{6,5},{7,8},{8,7},{9,10},{10,... | collective-permute-start | bytes 98312 | tf_op jit(solution)/shard_map/ppermute | solution.py:602
  16.5 0.0 copy-done.9
  16.5 0.4 %shard_map.138 = (bf16[1728,64]{1,0:T(8,128)(2,1)S(1)}, bf16[1152,128]{1,0:T(8,128)(2,1)S(1)}) custom-call(s32[8,27]{1,0:T(8,128)S(1)} %copy-done.7, bf16[360,27]{1,0:T(8,128)(2,1)S(1)} %copy-done.9, bf16[64,256]{1,0:T(8,128)(2,1)S(1)} %get-tuple-element.53.later.third), custom_call_target="tpu_custom_call" | custom-call | flops 4000000000 | bytes 10000000 | tf_op jit(solution)/shard_map/pallas_call | solution.py:557
  16.9 0.0 copy-done
  16.9 1.1 %shard_map.139 = (f32[64,256]{1,0:T(8,128)S(1)}, bf16[8,64,128]{2,1,0:T(8,128)(2,1)}) custom-call(bf16[1728,64]{1,0:T(8,128)(2,1)S(1)} %get-tuple-element.54.gather, bf16[64,256]{1,0:T(8,128)(2,1)S(1)} %get-tuple-element.53.later.third, bf16[27,256,256]{2,1,0:T(8,128)(2,1)S(1)} %copy-done, bf16[8,64,128]{2,1,0:T(8,128)(2,1)S(1)} %get-tuple-element.55.second), custom_call_target="tpu_custom_call" | custom-call | flops 10000000000 | bytes 10000000 | tf_op jit(solution)/shard_map/pallas_call | solution.py:557
  18.0 0.0 collective-permute-done.4.from_a
  18.0 0.9 %collective-permute-done.5.from_b = bf16[64,256]{1,0:T(8,128)(2,1)S(1)} collective-permute-done((bf16[64,256]{1,0:T(8,128)(2,1)S(1)}, bf16[64,256]{1,0:T(8,128)(2,1)S(1)}, u32[]{:S(2)}, u32[]{:S(2)}) %collective-permute-start.5) | collective-permute-done | bytes 32800 | tf_op jit(solution)/shard_map/ppermute | solution.py:602
  18.9 1.5 %shard_map.140 = bf16[8,8,256]{2,1,0:T(8,128)(2,1)} custom-call(bf16[1152,128]{1,0:T(8,128)(2,1)S(1)} %get-tuple-element.57.gather, f32[64,256]{1,0:T(8,128)S(1)} %get-tuple-element.58.partial, bf16[64,256]{1,0:T(8,128)(2,1)S(1)} %collective-permute-done.4.from_a, bf16[64,256]{1,0:T(8,128)(2,1)S(1)} %collective-permute-done.5.from_b, ...), custom_call_target="tpu_custom_call" | custom-call | flops 10000000000 | bytes 10000000 | tf_op jit(solution)/shard_map/pallas_call | solution.py:557
Async XLA Ops:
  0.6 1.1 %copy-start.2 = (bf16[8,512,64]{1,2,0:T(8,128)(2,1)S(1)}, bf16[8,512,64]{1,2,0:T(8,128)(2,1)}, u32[]{:S(2)}) copy-start(bf16[8,512,64]{1,2,0:T(8,128)(2,1)} %param.11) | copy-start | bytes 1572868
  0.6 0.7 %copy-start.6 = (s32[8,16]{1,0:T(8,128)S(1)}, s32[8,16]{1,0:T(8,128)}, u32[]{:S(2)}) copy-start(s32[8,16]{1,0:T(8,128)} %occupancy.1) | copy-start | bytes 1540
  1.7 3.2 %copy-start.4 = (bf16[27,64,64]{2,1,0:T(8,128)(2,1)S(1)}, bf16[27,64,64]{2,1,0:T(8,128)(2,1)}, u32[]{:S(2)}) copy-start(bf16[27,64,64]{2,1,0:T(8,128)(2,1)} %kernel.5) | copy-start | bytes 663556
  1.7 3.2 %copy-start.5 = (bf16[8,64,128]{2,1,0:T(8,128)(2,1)S(1)}, bf16[8,64,128]{2,1,0:T(8,128)(2,1)}, u32[]{:S(2)}) copy-start(bf16[8,64,128]{2,1,0:T(8,128)(2,1)} %reduce.2) | copy-start | bytes 393220
  1.7 3.2 %copy-start.7 = (s32[8,27]{1,0:T(8,128)S(1)}, s32[8,27]{1,0:T(8,128)}, u32[]{:S(2)}) copy-start(s32[8,27]{1,0:T(8,128)} %neighbours.7) | copy-start | bytes 2596
  1.8 5.5 %collective-permute-start = (bf16[4,64,128]{2,1,0:T(8,128)(2,1)S(1)}, bf16[4,64,128]{2,1,0:T(8,128)(2,1)S(1)}, u32[]{:S(2)}, u32[]{:S(2)}) collective-permute-start(bf16[4,64,128]{2,1,0:T(8,128)(2,1)S(1)} %get-tuple-element.32), channel_id=1, source_target_pairs={{0,1},{1,0},{2,3},{3,2},{4,5},{5,4},{6,7},{7,6},{8,9},{9,8},{10,11... | collective-permute-start | bytes 196616 | tf_op jit(solution)/shard_map/ppermute | solution.py:603
  2.3 4.5 %copy-start.8 = (bf16[432,27]{1,0:T(8,128)(2,1)S(1)}, bf16[432,27]{1,0:T(8,128)(2,1)}, u32[]{:S(2)}) copy-start(bf16[432,27]{1,0:T(8,128)(2,1)} %constant.6.clone.pick) | copy-start | bytes 69988
  2.3 5.0 %collective-permute-start.1 = (bf16[4,64,128]{2,1,0:T(8,128)(2,1)S(1)}, bf16[4,64,128]{2,1,0:T(8,128)(2,1)S(1)}, u32[]{:S(2)}, u32[]{:S(2)}) collective-permute-start(bf16[4,64,128]{2,1,0:T(8,128)(2,1)S(1)} %get-tuple-element.33), channel_id=1, source_target_pairs={{0,16},{1,2},{2,1},{3,4},{4,3},{5,6},{6,5},{7,8},{8,7},{9,10},{10,... | collective-permute-start | bytes 196616 | tf_op jit(solution)/shard_map/ppermute | solution.py:602
  8.7 4.2 %collective-permute-start.2 = (bf16[128,128]{1,0:T(8,128)(2,1)S(1)}, bf16[128,128]{1,0:T(8,128)(2,1)S(1)}, u32[]{:S(2)}, u32[]{:S(2)}) collective-permute-start(bf16[128,128]{1,0:T(8,128)(2,1)S(1)} %get-tuple-element.50), channel_id=1, source_target_pairs={{0,1},{1,0},{2,3},{3,2},{4,5},{5,4},{6,7},{7,6},{8,9},{9,8},{10,11... | collective-permute-start | bytes 98312 | tf_op jit(solution)/shard_map/ppermute | solution.py:603
  8.9 4.1 %collective-permute-start.3 = (bf16[128,128]{1,0:T(8,128)(2,1)S(1)}, bf16[128,128]{1,0:T(8,128)(2,1)S(1)}, u32[]{:S(2)}, u32[]{:S(2)}) collective-permute-start(bf16[128,128]{1,0:T(8,128)(2,1)S(1)} %get-tuple-element.51), channel_id=1, source_target_pairs={{0,16},{1,2},{2,1},{3,4},{4,3},{5,6},{6,5},{7,8},{8,7},{9,10},{10,... | collective-permute-start | bytes 98312 | tf_op jit(solution)/shard_map/ppermute | solution.py:602
  10.8 1.2 %copy-start.1 = (bf16[27,128,128]{2,1,0:T(8,128)(2,1)S(1)}, bf16[27,128,128]{2,1,0:T(8,128)(2,1)}, u32[]{:S(2)}) copy-start(bf16[27,128,128]{2,1,0:T(8,128)(2,1)} %kernel.7) | copy-start | bytes 2654212
  11.9 1.2 %copy-start.3 = (bf16[8,128,256]{2,1,0:T(8,128)(2,1)S(1)}, bf16[8,128,256]{2,1,0:T(8,128)(2,1)}, u32[]{:S(2)}) copy-start(bf16[8,128,256]{2,1,0:T(8,128)(2,1)} %reduce.3) | copy-start | bytes 1572868
  11.9 1.2 %copy-start.10 = (bf16[64,64]{1,0:T(8,128)(2,1)S(1)}, bf16[64,64]{1,0:T(8,128)(2,1)}, u32[]{:S(2)}) copy-start(bf16[64,64]{1,0:T(8,128)(2,1)} %constant.7.clone.children) | copy-start | bytes 24580
  13.2 3.3 %copy-start.9 = (bf16[360,27]{1,0:T(8,128)(2,1)S(1)}, bf16[360,27]{1,0:T(8,128)(2,1)}, u32[]{:S(2)}) copy-start(bf16[360,27]{1,0:T(8,128)(2,1)} %constant.8.clone.pick) | copy-start | bytes 58324
  14.1 2.7 %copy-start = (bf16[27,256,256]{2,1,0:T(8,128)(2,1)S(1)}, bf16[27,256,256]{2,1,0:T(8,128)(2,1)}, u32[]{:S(2)}) copy-start(bf16[27,256,256]{2,1,0:T(8,128)(2,1)} %kernel.9) | copy-start | bytes 10616836
  14.1 3.8 %collective-permute-start.4 = (bf16[64,256]{1,0:T(8,128)(2,1)S(1)}, bf16[64,256]{1,0:T(8,128)(2,1)S(1)}, u32[]{:S(2)}, u32[]{:S(2)}) collective-permute-start(bf16[64,256]{1,0:T(8,128)(2,1)S(1)} %get-tuple-element.53.later.third), channel_id=1, source_target_pairs={{0,1},{1,0},{2,3},{3,2},{4,5},{5,4},{6,7},{7,6},{8,9},{9,8},{10,11... | collective-permute-start | bytes 98312 | tf_op jit(solution)/shard_map/ppermute | solution.py:603
  15.0 3.9 %collective-permute-start.5 = (bf16[64,256]{1,0:T(8,128)(2,1)S(1)}, bf16[64,256]{1,0:T(8,128)(2,1)S(1)}, u32[]{:S(2)}, u32[]{:S(2)}) collective-permute-start(bf16[64,256]{1,0:T(8,128)(2,1)S(1)} %get-tuple-element.53.later.third), channel_id=1, source_target_pairs={{0,16},{1,2},{2,1},{3,4},{4,3},{5,6},{6,5},{7,8},{8,7},{9,10},{10,... | collective-permute-start | bytes 98312 | tf_op jit(solution)/shard_map/ppermute | solution.py:602

commit v2 on v1

--- a/solution.py
+++ b/solution.py
@@ -52,10 +52,12 @@
     return bits_of(chosen, jnp.bitwise_and(lane, 31))
 
 
-def slots_of(neighbours, first, count, b, tap):
-    numbers = [neighbours[b, tap + q] for q in range(9)]
-    shift = (1 - tap // 9) * count - first
-    return [jnp.where(n < 0, count, n + shift) for n in numbers]
+def slot_numbers(neighbours):
+    count = neighbours.shape[0]
+    number = neighbours[...]
+    tap = iota(number.shape, 1)
+    shift = jnp.where(tap < 9, count, jnp.where(tap < 18, 0, -count))
+    return jnp.where(number < 0, count, number + shift - lax.axis_index(LINE) * count)
 
 
 def masks_kernel(occupancy, bits, pair_words, mask_two, mask_three):
@@ -90,13 +92,19 @@
             word = either(any_two[4 * i + j], any_two[4 * i + 2 + j])
             word = either(word, lax.shift_right_logical(word, 16))
             any_three.append(either(word, lax.shift_right_logical(word, 2)))
-    for b in range(count):
-        tile = [jnp.broadcast_to(word[b : b + 1], (8, 128)) for word in any_three]
-        tile = jnp.where(
-            row < 4, jnp.where(row < 2, tile[0], tile[1]), jnp.where(row < 6, tile[2], tile[3])
-        )
-        mask = bits_of(tile, 4 * jnp.bitwise_and(row, 1))
-        mask_three[8 * b : 8 * (b + 1)] = beside([mask, mask])
+    for i in range(2):
+        for b in range(0, count, 2):
+            tile = [
+                jnp.broadcast_to(any_three[2 * i + j][n : n + 1], (8, 128))
+                for n in (b, b + 1)
+                for j in range(2)
+            ]
+            tile = jnp.where(
+                row < 4, jnp.where(row < 2, tile[0], tile[1]), jnp.where(row < 6, tile[2], tile[3])
+            )
+            mask = bits_of(tile, 4 * jnp.bitwise_and(row, 1))
+            at = 4 * (count * i + b)
+            mask_three[at : at + 8] = beside([mask, mask])
 
 
 def edges_kernel(features, bits, to_a, to_b):
@@ -120,14 +128,9 @@
 
 def slot_rows(neighbours):
     count = neighbours.shape[0]
-    number = neighbours[...]
-    tap = iota(number.shape, 1)
-    shift = jnp.where(tap < 9, count, jnp.where(tap < 18, 0, -count))
-    slot = jnp.where(
-        number < 0, 4 * count, number + shift - lax.axis_index(LINE) * count
-    ).astype(F32)
+    slot = jnp.where(neighbours[...] < 0, 4 * count, slot_numbers(neighbours)).astype(F32)
     return stack(
-        [jnp.broadcast_to(slot[b : b + 1], (128, number.shape[1])) for b in range(count)]
+        [jnp.broadcast_to(slot[b : b + 1], (128, slot.shape[1])) for b in range(count)]
     ).astype(BF16)
 
 
@@ -135,7 +138,7 @@
     return lax.dot_general(x, y, (((1,), (1,)), ((), ())), preferred_element_type=F32)
 
 
-def level_two_tables_kernel(neighbours, pick, own_two, low_two, high_two):
+def level_two_tables_kernel(neighbours, pick, own_two, sides_two):
     count = neighbours.shape[0]
     rows = times_transposed(pick[...], slot_rows(neighbours))
     lane = iota((16, 16 * count), 1)
@@ -144,7 +147,7 @@
     for q in range(9):
         source = 4 * jnp.bitwise_and(j + q // 3 + 3, 3) + jnp.bitwise_and(k + q % 3 + 3, 3)
         wanted = (lane - source).astype(F32)
-        for a, table in enumerate((low_two, own_two, high_two)):
+        for a, table in enumerate((sides_two.at[0], own_two, sides_two.at[1])):
             at = 16 * (9 * a + q)
             for b in range(count):
                 table[16 * (count * q + b) : 16 * (count * q + b + 1), :] = jnp.where(
@@ -152,33 +155,41 @@
                 ).astype(BF16)
 
 
-def level_three_tables_kernel(neighbours, pick, later, own_three, faces_three):
+def level_three_tables_kernel(neighbours, pick, later, own_three, far_three):
     count = neighbours.shape[0]
+    odd = on_odd_place()
     rows = times_transposed(pick[...], slot_rows(neighbours))
     row = iota((8, 128), 0)
-    voxel = [jnp.bitwise_and(lax.shift_right_logical(row, s), 1) for s in (2, 1, 0)]
     lane = iota((8, 128), 1)
-    at = base = 0
-    for table, sides in ((own_three, (0,)), (faces_three, (-1, 1))):
-        for side in sides:
-            for tap in range(27):
-                if side and tap // 9 != side + 1:
-                    continue
-                shift = (tap // 9 - 1, tap // 3 % 3 - 1, tap % 3 - 1)
-                x, y, z = [v + d for v, d in zip(voxel, shift)]
-                here = (x < 0) if side < 0 else (x > 1) if side else (x >= 0) & (x <= 1)
-                x, y, z = [jnp.bitwise_and(v + 2, 1) for v in (x, y, z)]
-                source = 4 * x + 2 * y + z + (8 * count if side > 0 else 0)
-                wanted = jnp.where(here, lane - source, -1).astype(F32)
-                tiles = [
-                    jnp.where(rows[at : at + 8, 128 * b : 128 * (b + 1)] == wanted, 1.0, 0.0)
-                    for b in range(count)
-                ]
-                table[count * at - base : count * (at + 8) - base, :] = stack(tiles)[
-                    :, : table.shape[1]
-                ].astype(BF16)
-                at += 8
-        base = count * at
+    j, k = [jnp.bitwise_and(lax.shift_right_logical(row, n), 1) for n in (1, 0)]
+
+    def block(tap, i, begin):
+        c, e = tap // 3 % 3, tap % 3
+        source = 2 * jnp.bitwise_and(j + c + 1, 1) + jnp.bitwise_and(k + e + 1, 1)
+        wanted = (lane - source - begin).astype(F32)
+        at = 8 * (2 * tap + i)
+        tiles = []
+        for b in range(0, count, 2):
+            first, second = [rows[at : at + 8, 128 * n : 128 * (n + 1)] for n in (b, b + 1)]
+            hit = jnp.where(row < 4, first, second) == wanted
+            tiles.append(jnp.where(hit, 1.0, 0.0))
+        return stack(tiles)
+
+    nowhere = 16 * 4 * count
+    for tap in range(27):
+        for i in range(2):
+            x = i + tap // 9 - 1
+            if x < 0:
+                begin = jnp.where(odd, 8 * count, nowhere)
+            elif x > 1:
+                begin = jnp.where(odd, nowhere, 8 * count)
+            else:
+                begin = 4 * count * x
+            at = 8 * count * tap + 4 * count * i
+            own_three[at : at + 4 * count, :] = block(tap, i, begin)[:, : 12 * count].astype(BF16)
+    for q in range(9):
+        tile = jnp.where(odd, block(18 + q, 1, 0), block(q, 0, 0))
+        far_three[4 * count * q : 4 * count * (q + 1), :] = tile[:, : 4 * count].astype(BF16)
 
 
 def shifted_windows(source, row):
@@ -202,14 +213,12 @@
 def outer_kernel(
     neighbours, bits, features, kernel, reduce,
     middle, taps, face_taps, reduce_taps, partial,
-    tables, windows, wrap_taps, numbers, arrived,
+    tables, windows, wrap_taps,
 ):
     count = features.shape[0]
-    first = lax.axis_index(LINE) * count
     lane = iota((64, 128), 1)
     row = iota((8, 128), 0)
-    copy = pltpu.make_async_copy(neighbours, numbers, arrived)
-    copy.start()
+    numbers = slot_numbers(neighbours)
 
     none = jnp.zeros((64, 64), F32)
     for q in range(9):
@@ -249,9 +258,8 @@
             tables[p, b] = m[:64]
             tables[p + 1, b] = m[64:]
 
-    copy.wait()
     for b in range(count):
-        slot = slots_of(numbers, first, count, b, 9)
+        slot = [numbers[b, 9 + q] for q in range(9)]
         for pair in range(4):
             tiles = shifted_windows(lambda q, j: tables[pair, slot[q], pl.ds(8 * j, 8), :], row)
             for jr in range(6):
@@ -313,26 +321,23 @@
 def faces_one_kernel(
     neighbours, from_a, from_b, face_taps, partial, reduce, pair_words, mask_two,
     outer, second, to_a, to_b,
-    halo, windows, low_sums, high_sums, numbers, arrived,
+    halo, windows, low_sums, high_sums,
 ):
     count = outer.shape[0]
-    first = lax.axis_index(LINE) * count
     lane = iota((64, 128), 1)
     small = iota((8, 128), 1)
     row = iota((8, 128), 0)
     odd = on_odd_place()
-    copy = pltpu.make_async_copy(neighbours, numbers, arrived)
-    copy.start()
+    slot = slot_numbers(neighbours)
     halo[count] = jnp.zeros((64, 128), F32)
     for q in range(count // 2):
         one, two = from_a[q].astype(F32), from_b[q].astype(F32)
         m = stack([jnp.where(odd, one, two), jnp.where(odd, two, one)]).T
         halo[2 * q] = m[:64]
         halo[2 * q + 1] = m[64:]
-    copy.wait()
     for b in range(count):
-        low = slots_of(numbers, first, count, b, 0)
-        high = slots_of(numbers, first, count, b, 18)
+        low = [slot[b, q] for q in range(9)]
+        high = [slot[b, 18 + q] for q in range(9)]
 
         def source(q, j):
             rows = pl.ds(8 * j, 8)
@@ -420,12 +425,23 @@
             ).astype(BF16)
 
 
-def own_two_kernel(outer, inner, gather, kernel, first, partial, result, stored):
+def face_part(gather, face, kernel, high):
+    moved = dot(gather, face).astype(BF16)
+    rows = moved.shape[0] // 9
+    left = beside([moved[q * rows : (q + 1) * rows] for q in range(9)])
+    weights = kernel[pl.ds(18 * high, 9)]
+    return dot(left, weights.reshape(9 * weights.shape[1], weights.shape[2]))
+
+
+def own_two_kernel(
+    outer, inner, own_gather, gathers, from_a, kernel, first,
+    partial, result, stored,
+):
     copy = pltpu.make_async_copy(first, result, stored)
     copy.start()
     rows = outer.shape[1]
     planes = beside([outer[0], inner[0], inner[1], outer[1]])
-    moved = dot(gather[...], planes).astype(BF16)
+    moved = dot(own_gather[...], planes).astype(BF16)
     left = beside(
         [
             stack(
@@ -440,77 +456,86 @@
     weights = [kernel[9 * a : 9 * (a + 1)].reshape(9 * 128, 128) for a in range(3)]
     sums = dot(left, beside(weights[:2]))
     later = dot(left[rows:], weights[2])
+    high = jnp.where(on_odd_place(), 0, 1)
+    near = face_part(gathers[high], from_a[...], kernel, high)
     for i in range(4):
         total = sums[i * rows : (i + 1) * rows, 128:]
         if i:
             total = total + sums[(i - 1) * rows : i * rows, :128]
         if i < 3:
             total = total + later[i * rows : (i + 1) * rows]
+        if i in (0, 3):
+            total = total + jnp.where(high == i // 3, near, 0.0)
         partial[i * rows : (i + 1) * rows] = total
     copy.wait()
 
 
 def faces_two_kernel(
-    low_gather, high_gather, children, partial, from_a, from_b, kernel, reduce,
-    mask_two, mask_three,
-    second, third,
+    gathers, children, partial, from_b, kernel, reduce, mask_two, mask_three,
+    second, third, to_a, to_b,
 ):
     count = second.shape[0]
     rows = 16 * count
     odd = on_odd_place()
-    one, two = from_a[...], from_b[...]
-    added = []
-    for gather, face, tap in (
-        (low_gather, jnp.where(odd, one, two), 0),
-        (high_gather, jnp.where(odd, two, one), 18),
-    ):
-        moved = dot(gather[...], face).astype(BF16)
-        left = beside([moved[q * rows : (q + 1) * rows] for q in range(9)])
-        added.append(dot(left, kernel[tap : tap + 9].reshape(9 * 128, 128)))
+    high = jnp.where(odd, 1, 0)
+    far = face_part(gathers[high], from_b[...], kernel, high)
     planes = []
     for i in range(4):
         sums = partial[i * rows : (i + 1) * rows]
-        if i == 0:
-            sums = sums + added[0]
-        if i == 3:
-            sums = sums + added[1]
+        if i in (0, 3):
+            sums = sums + jnp.where(high == i // 3, far, 0.0)
         planes.append((jnp.maximum(sums, 0.0) * mask_two[i]).astype(BF16))
     bricks = [
         stack([planes[i][16 * b : 16 * (b + 1)] for i in range(4)]) for b in range(count)
     ]
     for b in range(count):
         second[b] = bricks[b]
-    moved = dot(children[...], beside(bricks))
+    moved = dot(
+        children[...], beside([stack(bricks[b : b + 2]) for b in range(0, count, 2)])
+    )
     left = beside(
         [
-            stack([moved[8 * q : 8 * (q + 1), 128 * b : 128 * (b + 1)] for b in range(count)])
+            stack(
+                [
+                    moved[16 * q + 8 * i : 16 * q + 8 * (i + 1), 128 * n : 128 * (n + 1)]
+                    for i in range(2)
+                    for n in range(count // 2)
+                ]
+            )
             for q in range(8)
         ]
     ).astype(BF16)
     sums = dot(left, reduce[...].reshape(8 * 128, 256))
-    third[...] = (jnp.maximum(sums, 0.0) * mask_three[...]).astype(BF16)
-
-
-def own_three_kernel(gather, third, kernel, second, partial, result, stored):
+    value = jnp.maximum(sums, 0.0) * mask_three[...]
+    third[...] = value.astype(BF16)
+    low, high = value[: 4 * count], value[4 * count :]
+    to_a[...] = jnp.where(odd, low, high).astype(BF16)
+    to_b[...] = jnp.where(odd, high, low).astype(BF16)
+
+
+def own_three_kernel(gather, third, from_a, kernel, second, partial, result, stored):
     copy = pltpu.make_async_copy(second, result, stored)
     copy.start()
     rows = third.shape[0]
-    moved = dot(gather[...], third[...]).astype(BF16)
+    moved = dot(gather[...], stack([third[...], from_a[...]])).astype(BF16)
     left = beside([moved[q * rows : (q + 1) * rows] for q in range(27)])
     partial[...] = dot(left, kernel[...].reshape(27 * 256, 256))
     copy.wait()
 
 
-def faces_three_kernel(gather, partial, from_a, from_b, kernel, mask_three, out):
-    rows = partial.shape[0]
+def faces_three_kernel(gather, partial, from_b, kernel, mask_three, out):
+    rows = from_b.shape[0]
     odd = on_odd_place()
-    one, two = from_a[...], from_b[...]
-    faces = stack([jnp.where(odd, one, two), jnp.where(odd, two, one)])
-    moved = dot(gather[...], faces).astype(BF16)
-    left = beside([moved[q * rows : (q + 1) * rows] for q in range(18)])
-    weights = stack([kernel[:9].reshape(9 * 256, 256), kernel[18:].reshape(9 * 256, 256)])
-    sums = partial[...] + dot(left, weights)
-    out[...] = (jnp.maximum(sums, 0.0) * mask_three[...]).astype(BF16).reshape(out.shape)
+    far = face_part(gather[...], from_b[...], kernel, jnp.where(odd, 1, 0))
+    low = partial[:rows] + jnp.where(odd, 0.0, far)
+    high = partial[rows:] + jnp.where(odd, far, 0.0)
+    low = jnp.maximum(low, 0.0) * mask_three[:rows]
+    high = jnp.maximum(high, 0.0) * mask_three[rows:]
+    row = iota((8, 256), 0)
+    for n in range(rows // 8):
+        near, past = low[8 * n : 8 * (n + 1)], high[8 * n : 8 * (n + 1)]
+        out[2 * n] = jnp.where(row < 4, near, pltpu.roll(past, 4, 0)).astype(BF16)
+        out[2 * n + 1] = jnp.where(row < 4, pltpu.roll(near, 4, 0), past).astype(BF16)
 
 
 def level_two_picks():
@@ -523,25 +548,27 @@
 
 
 def level_three_picks():
-    pick = np.zeros((45 * 8, 27), np.float32)
+    pick = np.zeros((27 * 16, 27), np.float32)
     for tap in range(27):
-        for u in range(8):
+        for r in range(16):
             x, y, z = [
-                ((u >> s) & 1) + d - 1
-                for s, d in ((2, tap // 9), (1, tap // 3 % 3), (0, tap % 3))
+                n + d - 1
+                for n, d in (
+                    (r // 8, tap // 9), (r // 2 % 2, tap // 3 % 3), (r % 2, tap % 3)
+                )
             ]
-            side = x // 2
-            at = 8 * (tap + (0, 18, 27)[side])
-            pick[at + u, 9 * (side + 1) + 3 * (y // 2 + 1) + z // 2 + 1] = 8
+            pick[16 * tap + r, 9 * (x // 2 + 1) + 3 * (y // 2 + 1) + z // 2 + 1] = 4
     return jnp.asarray(pick, BF16)
 
 
 def child_rows():
-    pick = np.zeros((64, 64), np.float32)
+    pick = np.zeros((128, 128), np.float32)
     for q in range(8):
-        for u in range(8):
-            x, y, z = [2 * ((u >> s) & 1) + ((q >> s) & 1) for s in (2, 1, 0)]
-            pick[8 * q + u, 16 * x + 4 * y + z] = 1
+        for r in range(16):
+            x, y, z = [
+                2 * n + (q >> s & 1) for n, s in ((r // 8, 2), (r // 2 % 2, 1), (r % 2, 0))
+            ]
+            pick[16 * q + r, 64 * (r // 4 % 2) + 16 * x + 4 * y + z] = 1
     return jnp.asarray(pick, BF16)
 
 
@@ -596,7 +623,6 @@
     count = features.shape[0]
     features = jnp.swapaxes(features, 1, 2)
     shape = jax.ShapeDtypeStruct
-    scalars = [pltpu.SMEM(neighbours.shape, jnp.int32), DMA(())]
 
     def exchange(to_a, to_b):
         from_b = lax.ppermute(to_b, axes, across)
@@ -615,11 +641,14 @@
         [],
         occupancy,
     )
-    from_a, from_b = exchange(*call(edges_kernel, 0.3, (face, face), [], features, bits))
-    own_two, low_two, high_two = call(
+    from_a, from_b = exchange(*call(edges_kernel, 0.02, (face, face), [], features, bits))
+    own_two, sides_two = call(
         level_two_tables_kernel,
         0.4,
-        (shape((9 * 16 * count, 16 * count), BF16),) * 3,
+        (
+            shape((9 * 16 * count, 16 * count), BF16),
+            shape((2, 9 * 16 * count, 16 * count), BF16),
+        ),
         [],
         neighbours, level_two_picks(),
     )
@@ -637,10 +666,8 @@
             pltpu.VMEM((4, count + 1, 64, 128), F32),
             pltpu.VMEM((count, 3, 4, 6, 16, 128), BF16),
             pltpu.VMEM((9 * 128, 256), BF16),
-        ]
-        + scalars,
+        ],
         neighbours, bits, features, conv_one, first_reduce_kernel,
-        remain=(0,),
     )
     plane = shape((16 * count, 128), BF16)
     planes = shape((2, 16 * count, 128), BF16)
@@ -654,16 +681,14 @@
             pltpu.VMEM((count, 3, 6, 16, 128), BF16),
             sums,
             sums,
-        ]
-        + scalars,
+        ],
         neighbours, from_a, from_b, face_taps, partial, reduce_taps, pair_words, mask_two,
-        remain=(0,),
     )
     from_a, from_b = exchange(to_a, to_b)
 
     first_level, inner_two = call(
         inner_kernel,
-        1.2,
+        0.05,
         (shape(features.shape, BF16), planes),
         [sums, sums],
         middle, taps, partial, outer, reduce_taps, pair_words, mask_two,
@@ -673,23 +698,24 @@
         1.0,
         (shape((4 * 16 * count, 128), F32), shape(features.shape, BF16)),
         [DMA(())],
-        outer_two, inner_two, own_two, conv_two, first_level,
+        outer_two, inner_two, own_two, sides_two, from_a, conv_two, first_level,
         store=(1,),
     )
-    second_level, third = call(
+    face = shape((4 * count, 256), BF16)
+    second_level, third, to_a, to_b = call(
         faces_two_kernel,
         0.9,
-        (shape((count, 64, 128), BF16), shape((8 * count, 256), BF16)),
+        (shape((count, 64, 128), BF16), shape((8 * count, 256), BF16), face, face),
         [],
-        low_two, high_two, child_rows(), partial, from_a, from_b, conv_two, second_reduce_kernel,
-        mask_two, mask_three,
-    )
-    from_a, from_b = exchange(third, third)
-
-    own_three, faces_three = call(
+        sides_two, child_rows(), partial, from_b, conv_two, second_reduce_kernel, mask_two,
+        mask_three,
+    )
+    from_a, from_b = exchange(to_a, to_b)
+
+    own_three, far_three = call(
         level_three_tables_kernel,
-        0.4,
-        (shape((27 * 8 * count, 8 * count), BF16), shape((18 * 8 * count, 16 * count), BF16)),
+        0.02,
+        (shape((27 * 8 * count, 12 * count), BF16), shape((9 * 4 * count, 4 * count), BF16)),
         [],
         neighbours, level_three_picks(), third,
     )
@@ -698,7 +724,7 @@
         1.0,
         (shape((8 * count, 256), F32), shape(second_level.shape, BF16)),
         [DMA(())],
-        own_three, third, conv_three, second_level,
+        own_three, third, from_a, conv_three, second_level,
         store=(1,),
     )
     third_level = call(
@@ -706,7 +732,7 @@
         1,
         shape((count, 8, 256), BF16),
         [],
-        faces_three, partial, from_a, from_b, conv_three, mask_three,
+        far_three, partial, from_b, conv_three, mask_three,
     )
     return jnp.swapaxes(first_level, 1, 2), second_level, third_level
 

time: 20.6 us -> 19.2 us (0.932)
  Pallas kernels: 9.88 us -> 9.05 us
  local copies, waits for them, and re-layouts: 1.28 us -> 0.91 us
  waiting for transfers between devices: 0.94 us -> 0.73 us
    pallas_call x11, Pallas kernels: 9.88 us -> 9.05 us  [call(): pl.pallas_call(kernel, out_shape=out_shape, in_specs=[ANY if n in remain...]
    unnamed x22, local copies, waits for them, and re-layouts: 1.28 us -> 0.91 us
    ppermute x3, waiting for transfers between devices: 0.93 us -> 0.72 us  [exchange(): from_b = lax.ppermute(to_b, axes, across)]
  transfers between devices with their start and end apart: 6 -> 6, of which waited for: 1 -> 1; matrix products, arithmetic and copies ran while one was open for 0% -> 0% of each run, Pallas kernels for 28% -> 31%
where the time goes in v2:
time: 19.2 us; the launch traced here: 19.1 us
  Pallas kernels  9.05 us (47%)
  starting transfers between devices  7.51 us (39%)
  local copies, waits for them, and re-layouts  0.91 us (5%)
  between operations  0.85 us (4%)
  waiting for transfers between devices  0.73 us (4%)
    pallas_call x11, Pallas kernels, call(): pl.pallas_call(kernel, out_shape=out_shape, in_specs=[ANY if n in remain...  9.05 us
    ppermute x3, starting transfers between devices, exchange(): from_b = lax.ppermute(to_b, axes, across)  5.94 us
    ppermute x3, starting transfers between devices, exchange(): return (lax.ppermute(to_a, axes, within), from_b)  1.57 us
    unnamed x22, local copies, waits for them, and re-layouts  0.91 us
    ppermute x3, waiting for transfers between devices, exchange(): from_b = lax.ppermute(to_b, axes, across)  0.72 us
  transfers between devices with their start and end apart: 6, of which 1 were waited for; matrix products, arithmetic and copies ran while one was open for 0% of the time, Pallas kernels for 31%

profile of v2, /device:TPU:0, one launch (start us, length us, event | category | flops | bytes accessed | tf_op | source)
XLA Modules:
  0.0 19.1 jit_solution(3810101791280722865)
XLA Ops:
  0.6 0.0 copy-start.2
  0.6 0.0 copy-start.4
  0.7 0.0 copy-start.5
  0.7 0.0 copy-start.6
  0.7 0.8 %copy-done.6 = s32[8,16]{1,0:T(8,128)S(1)} copy-done((s32[8,16]{1,0:T(8,128)S(1)}, s32[8,16]{1,0:T(8,128)}, u32[]{:S(2)}) %copy-start.6) | copy-done | bytes 536
  1.4 0.0 copy-start.7
  1.4 0.1 shard_map.130
  1.6 0.1 copy-done.2
  1.7 0.1 shard_map.131
  1.8 0.5 %collective-permute-start = (bf16[4,64,128]{2,1,0:T(8,128)(2,1)S(1)}, bf16[4,64,128]{2,1,0:T(8,128)(2,1)S(1)}, u32[]{:S(2)}, u32[]{:S(2)}) collective-permute-start(bf16[4,64,128]{2,1,0:T(8,128)(2,1)S(1)} %get-tuple-element.33), channel_id=1, source_target_pairs={{0,1},{1,0},{2,3},{3,2},{4,5},{5,4},{6,7},{7,6},{8,9},{9,8},{10,11... | collective-permute-start | bytes 196616 | tf_op jit(solution)/shard_map/ppermute | solution.py:629
  2.3 0.0 copy-start.9
  2.3 2.6 %collective-permute-start.1 = (bf16[4,64,128]{2,1,0:T(8,128)(2,1)S(1)}, bf16[4,64,128]{2,1,0:T(8,128)(2,1)S(1)}, u32[]{:S(2)}, u32[]{:S(2)}) collective-permute-start(bf16[4,64,128]{2,1,0:T(8,128)(2,1)S(1)} %get-tuple-element.34), channel_id=1, source_target_pairs={{0,16},{1,2},{2,1},{3,4},{4,3},{5,6},{6,5},{7,8},{8,7},{9,10},{10,... | collective-permute-start | bytes 196616 | tf_op jit(solution)/shard_map/ppermute | solution.py:628
  4.9 0.0 copy-done.4
  4.9 0.0 copy-done.5
  4.9 0.0 copy-done.7
  4.9 1.9 %shard_map.132 = (bf16[8,3,6,16,128]{4,3,2,1,0:T(8,128)(2,1)S(1)}, bf16[1152,256]{1,0:T(8,128)(2,1)S(1)}, bf16[1152,128]{1,0:T(8,128)(2,1)S(1)}, bf16[256,256]{1,0:T(8,128)(2,1)S(1)}, f32[4,512,128]{2,1,0:T(8,128)S(1)}) custom-call(s32[8,27]{1,0:T(8,128)S(1)} %copy-done.7, f32[4,8,128]{2,1,0:T(8,128)S(1)} %get-tuple-element.32.bits, ...), custom_call_target="tpu_custom_call" | custom-call | flops 20000000000 | bytes 10000000 | tf_op jit(solution)/shard_map/pallas_call | solution.py:584
  6.8 0.0 copy-done.9
  6.8 0.4 %shard_map.135 = (bf16[1152,128]{1,0:T(8,128)(2,1)S(1)}, bf16[2,1152,128]{2,1,0:T(8,128)(2,1)S(1)}) custom-call(s32[8,27]{1,0:T(8,128)S(1)} %copy-done.7, bf16[432,27]{1,0:T(8,128)(2,1)S(1)} %copy-done.9), custom_call_target="tpu_custom_call" | custom-call | flops 4000000000 | bytes 10000000 | tf_op jit(solution)/shard_map/pallas_call | solution.py:584
  7.2 0.0 collective-permute-done.from_a
  7.2 0.0 collective-permute-done.1.from_b
  7.2 0.0 copy-start.1
  7.3 0.9 %shard_map.133 = (bf16[8,2,64,128]{3,2,1,0:T(8,128)(2,1)S(1)}, bf16[2,128,128]{2,1,0:T(8,128)(2,1)S(1)}, bf16[128,128]{1,0:T(8,128)(2,1)S(1)}, bf16[128,128]{1,0:T(8,128)(2,1)S(1)}) custom-call(s32[8,27]{1,0:T(8,128)S(1)} %copy-done.7, bf16[4,64,128]{2,1,0:T(8,128)(2,1)S(1)} %collective-permute-done.from_a, ...), custom_call_target="tpu_custom_call" | custom-call | flops 15000000512 | bytes 10000000 | tf_op jit(solution)/shard_map/pallas_call | solution.py:584
  8.2 0.2 %collective-permute-start.2 = (bf16[128,128]{1,0:T(8,128)(2,1)S(1)}, bf16[128,128]{1,0:T(8,128)(2,1)S(1)}, u32[]{:S(2)}, u32[]{:S(2)}) collective-permute-start(bf16[128,128]{1,0:T(8,128)(2,1)S(1)} %get-tuple-element.47), channel_id=1, source_target_pairs={{0,1},{1,0},{2,3},{3,2},{4,5},{5,4},{6,7},{7,6},{8,9},{9,8},{10,11... | collective-permute-start | bytes 98312 | tf_op jit(solution)/shard_map/ppermute | solution.py:629
  8.4 1.9 %collective-permute-start.3 = (bf16[128,128]{1,0:T(8,128)(2,1)S(1)}, bf16[128,128]{1,0:T(8,128)(2,1)S(1)}, u32[]{:S(2)}, u32[]{:S(2)}) collective-permute-start(bf16[128,128]{1,0:T(8,128)(2,1)S(1)} %get-tuple-element.51), channel_id=1, source_target_pairs={{0,16},{1,2},{2,1},{3,4},{4,3},{5,6},{6,5},{7,8},{8,7},{9,10},{10,... | collective-permute-start | bytes 98312 | tf_op jit(solution)/shard_map/ppermute | solution.py:628
  10.3 1.0 %shard_map.134 = (bf16[8,64,512]{2,1,0:T(8,128)(2,1)S(1)}, bf16[2,128,128]{2,1,0:T(8,128)(2,1)S(1)}) custom-call(bf16[8,3,6,16,128]{4,3,2,1,0:T(8,128)(2,1)S(1)} %get-tuple-element.41.middle, bf16[1152,256]{1,0:T(8,128)(2,1)S(1)} %get-tuple-element.42.taps, f32[4,512,128]{2,1,0:T(8,128)S(1)} %get-tuple-element.36.partial, ...), custom_call_target="tpu_custom_call" | custom-call | flops 500000000 | bytes 10000000 | tf_op jit(solution)/shard_map/pallas_call | solution.py:584
  11.3 0.0 collective-permute-done.2.from_a
  11.3 0.0 copy-done.1
  11.3 0.0 copy-start.3
  11.3 0.0 copy-start.10
  11.3 1.2 %shard_map.136 = (f32[512,128]{1,0:T(8,128)S(1)}, bf16[8,64,512]{2,1,0:T(8,128)(2,1)}) custom-call(bf16[2,128,128]{2,1,0:T(8,128)(2,1)S(1)} %get-tuple-element.40.outer, bf16[2,128,128]{2,1,0:T(8,128)(2,1)S(1)} %get-tuple-element.44.inner, bf16[1152,128]{1,0:T(8,128)(2,1)S(1)} %get-tuple-element.45.own_gather, ...), custom_call_target="tpu_custom_call" | custom-call | flops 10000000000 | bytes 10000000 | tf_op jit(solution)/shard_map/pallas_call | solution.py:584
  12.5 0.0 collective-permute-done.3.from_b
  12.5 0.0 copy-done.3
  12.5 0.0 copy-done.10
  12.5 0.0 copy-start.8
  12.6 0.0 copy-start
  12.6 0.8 %shard_map.137 = (bf16[8,64,128]{2,1,0:T(8,128)(2,1)S(1)}, bf16[64,256]{1,0:T(8,128)(2,1)S(1)}, bf16[32,256]{1,0:T(8,128)(2,1)S(1)}, bf16[32,256]{1,0:T(8,128)(2,1)S(1)}) custom-call(bf16[2,1152,128]{2,1,0:T(8,128)(2,1)S(1)} %get-tuple-element.46.gathers, bf16[128,128]{1,0:T(8,128)(2,1)S(1)} %copy-done.10, f32[512,128]{1,0:T(8,128)S(1)} %get-tuple-element.50.partial, ...), custom_call_target="tpu_custom_call" | custom-call | flops 8999999488 | bytes 10000000 | tf_op jit(solution)/shard_map/pallas_call | solution.py:584
  13.4 0.8 %collective-permute-start.4 = (bf16[32,256]{1,0:T(8,128)(2,1)S(1)}, bf16[32,256]{1,0:T(8,128)(2,1)S(1)}, u32[]{:S(2)}, u32[]{:S(2)}) collective-permute-start(bf16[32,256]{1,0:T(8,128)(2,1)S(1)} %get-tuple-element.55), channel_id=1, source_target_pairs={{0,1},{1,0},{2,3},{3,2},{4,5},{5,4},{6,7},{7,6},{8,9},{9,8},{10,11... | collective-permute-start | bytes 49160 | tf_op jit(solution)/shard_map/ppermute | solution.py:629
  14.3 1.5 %collective-permute-start.5 = (bf16[32,256]{1,0:T(8,128)(2,1)S(1)}, bf16[32,256]{1,0:T(8,128)(2,1)S(1)}, u32[]{:S(2)}, u32[]{:S(2)}) collective-permute-start(bf16[32,256]{1,0:T(8,128)(2,1)S(1)} %get-tuple-element.60), channel_id=1, source_target_pairs={{0,16},{1,2},{2,1},{3,4},{4,3},{5,6},{6,5},{7,8},{8,7},{9,10},{10,... | collective-permute-start | bytes 49160 | tf_op jit(solution)/shard_map/ppermute | solution.py:628
  15.7 0.0 copy-done.8
  15.7 0.4 %shard_map.138 = (bf16[1728,96]{1,0:T(8,128)(2,1)S(1)}, bf16[288,32]{1,0:T(8,128)(2,1)S(1)}) custom-call(s32[8,27]{1,0:T(8,128)S(1)} %copy-done.7, bf16[432,27]{1,0:T(8,128)(2,1)S(1)} %copy-done.8, bf16[64,256]{1,0:T(8,128)(2,1)S(1)} %get-tuple-element.53.later.third), custom_call_target="tpu_custom_call" | custom-call | flops 200000000 | bytes 10000000 | tf_op jit(solution)/shard_map/pallas_call | solution.py:584
  16.2 0.0 collective-permute-done.4.from_a
  16.2 0.0 copy-done
  16.2 1.1 %shard_map.139 = (f32[64,256]{1,0:T(8,128)S(1)}, bf16[8,64,128]{2,1,0:T(8,128)(2,1)}) custom-call(bf16[1728,96]{1,0:T(8,128)(2,1)S(1)} %get-tuple-element.54.gather, bf16[64,256]{1,0:T(8,128)(2,1)S(1)} %get-tuple-element.53.later.third, bf16[32,256]{1,0:T(8,128)(2,1)S(1)} %collective-permute-done.4.from_a, bf16[27,256,256]{2,1,0:T(8,128)(2,1)S(1)} %copy-done, ...), custom_call_target="tpu_custom_call" | custom-call | flops 10000000000 | bytes 10000000 | tf_op jit(solution)/shard_map/pallas_call | solution.py:584
  17.3 0.7 %collective-permute-done.5.from_b = bf16[32,256]{1,0:T(8,128)(2,1)S(1)} collective-permute-done((bf16[32,256]{1,0:T(8,128)(2,1)S(1)}, bf16[32,256]{1,0:T(8,128)(2,1)S(1)}, u32[]{:S(2)}, u32[]{:S(2)}) %collective-permute-start.5) | collective-permute-done | bytes 16416 | tf_op jit(solution)/shard_map/ppermute | solution.py:628
  18.0 1.1 %shard_map.140 = bf16[8,8,256]{2,1,0:T(8,128)(2,1)} custom-call(bf16[288,32]{1,0:T(8,128)(2,1)S(1)} %get-tuple-element.58.gather, f32[64,256]{1,0:T(8,128)S(1)} %get-tuple-element.59.partial, bf16[32,256]{1,0:T(8,128)(2,1)S(1)} %collective-permute-done.5.from_b, bf16[27,256,256]{2,1,0:T(8,128)(2,1)S(1)} %copy-done, f32[64,256]{1,0:T(8,128)S(1)} %get-tuple-element.52.mask_three), custom_call_target="tpu_custom_call" | custom-call | flops 10000000000 | bytes 10000000 | tf_op jit(solution)/shard_map/pallas_call | solution.py:584
Async XLA Ops:
  0.6 1.1 %copy-start.2 = (bf16[8,512,64]{1,2,0:T(8,128)(2,1)S(1)}, bf16[8,512,64]{1,2,0:T(8,128)(2,1)}, u32[]{:S(2)}) copy-start(bf16[8,512,64]{1,2,0:T(8,128)(2,1)} %param.11) | copy-start | bytes 1572868
  0.6 4.3 %copy-start.4 = (bf16[27,64,64]{2,1,0:T(8,128)(2,1)S(1)}, bf16[27,64,64]{2,1,0:T(8,128)(2,1)}, u32[]{:S(2)}) copy-start(bf16[27,64,64]{2,1,0:T(8,128)(2,1)} %kernel.5) | copy-start | bytes 663556
  0.7 4.3 %copy-start.5 = (bf16[8,64,128]{2,1,0:T(8,128)(2,1)S(1)}, bf16[8,64,128]{2,1,0:T(8,128)(2,1)}, u32[]{:S(2)}) copy-start(bf16[8,64,128]{2,1,0:T(8,128)(2,1)} %reduce.2) | copy-start | bytes 393220
  0.7 0.8 %copy-start.6 = (s32[8,16]{1,0:T(8,128)S(1)}, s32[8,16]{1,0:T(8,128)}, u32[]{:S(2)}) copy-start(s32[8,16]{1,0:T(8,128)} %occupancy.1) | copy-start | bytes 1540
  1.4 3.5 %copy-start.7 = (s32[8,27]{1,0:T(8,128)S(1)}, s32[8,27]{1,0:T(8,128)}, u32[]{:S(2)}) copy-start(s32[8,27]{1,0:T(8,128)} %neighbours.7) | copy-start | bytes 2596
  1.8 5.4 %collective-permute-start = (bf16[4,64,128]{2,1,0:T(8,128)(2,1)S(1)}, bf16[4,64,128]{2,1,0:T(8,128)(2,1)S(1)}, u32[]{:S(2)}, u32[]{:S(2)}) collective-permute-start(bf16[4,64,128]{2,1,0:T(8,128)(2,1)S(1)} %get-tuple-element.33), channel_id=1, source_target_pairs={{0,1},{1,0},{2,3},{3,2},{4,5},{5,4},{6,7},{7,6},{8,9},{9,8},{10,11... | collective-permute-start | bytes 196616 | tf_op jit(solution)/shard_map/ppermute | solution.py:629
  2.3 4.5 %copy-start.9 = (bf16[432,27]{1,0:T(8,128)(2,1)S(1)}, bf16[432,27]{1,0:T(8,128)(2,1)}, u32[]{:S(2)}) copy-start(bf16[432,27]{1,0:T(8,128)(2,1)} %constant.6.clone.pick) | copy-start | bytes 69988
  2.3 4.9 %collective-permute-start.1 = (bf16[4,64,128]{2,1,0:T(8,128)(2,1)S(1)}, bf16[4,64,128]{2,1,0:T(8,128)(2,1)S(1)}, u32[]{:S(2)}, u32[]{:S(2)}) collective-permute-start(bf16[4,64,128]{2,1,0:T(8,128)(2,1)S(1)} %get-tuple-element.34), channel_id=1, source_target_pairs={{0,16},{1,2},{2,1},{3,4},{4,3},{5,6},{6,5},{7,8},{8,7},{9,10},{10,... | collective-permute-start | bytes 196616 | tf_op jit(solution)/shard_map/ppermute | solution.py:628
  7.2 4.0 %copy-start.1 = (bf16[27,128,128]{2,1,0:T(8,128)(2,1)S(1)}, bf16[27,128,128]{2,1,0:T(8,128)(2,1)}, u32[]{:S(2)}) copy-start(bf16[27,128,128]{2,1,0:T(8,128)(2,1)} %kernel.7) | copy-start | bytes 2654212
  8.2 3.1 %collective-permute-start.2 = (bf16[128,128]{1,0:T(8,128)(2,1)S(1)}, bf16[128,128]{1,0:T(8,128)(2,1)S(1)}, u32[]{:S(2)}, u32[]{:S(2)}) collective-permute-start(bf16[128,128]{1,0:T(8,128)(2,1)S(1)} %get-tuple-element.47), channel_id=1, source_target_pairs={{0,1},{1,0},{2,3},{3,2},{4,5},{5,4},{6,7},{7,6},{8,9},{9,8},{10,11... | collective-permute-start | bytes 98312 | tf_op jit(solution)/shard_map/ppermute | solution.py:629
  8.4 4.1 %collective-permute-start.3 = (bf16[128,128]{1,0:T(8,128)(2,1)S(1)}, bf16[128,128]{1,0:T(8,128)(2,1)S(1)}, u32[]{:S(2)}, u32[]{:S(2)}) collective-permute-start(bf16[128,128]{1,0:T(8,128)(2,1)S(1)} %get-tuple-element.51), channel_id=1, source_target_pairs={{0,16},{1,2},{2,1},{3,4},{4,3},{5,6},{6,5},{7,8},{8,7},{9,10},{10,... | collective-permute-start | bytes 98312 | tf_op jit(solution)/shard_map/ppermute | solution.py:628
  11.3 1.3 %copy-start.3 = (bf16[8,128,256]{2,1,0:T(8,128)(2,1)S(1)}, bf16[8,128,256]{2,1,0:T(8,128)(2,1)}, u32[]{:S(2)}) copy-start(bf16[8,128,256]{2,1,0:T(8,128)(2,1)} %reduce.3) | copy-start | bytes 1572868
  11.3 1.3 %copy-start.10 = (bf16[128,128]{1,0:T(8,128)(2,1)S(1)}, bf16[128,128]{1,0:T(8,128)(2,1)}, u32[]{:S(2)}) copy-start(bf16[128,128]{1,0:T(8,128)(2,1)} %constant.7.clone.children) | copy-start | bytes 98308
  12.5 3.2 %copy-start.8 = (bf16[432,27]{1,0:T(8,128)(2,1)S(1)}, bf16[432,27]{1,0:T(8,128)(2,1)}, u32[]{:S(2)}) copy-start(bf16[432,27]{1,0:T(8,128)(2,1)} %constant.8.clone.pick) | copy-start | bytes 69988
  12.6 3.6 %copy-start = (bf16[27,256,256]{2,1,0:T(8,128)(2,1)S(1)}, bf16[27,256,256]{2,1,0:T(8,128)(2,1)}, u32[]{:S(2)}) copy-start(bf16[27,256,256]{2,1,0:T(8,128)(2,1)} %kernel.9) | copy-start | bytes 10616836
  13.4 2.8 %collective-permute-start.4 = (bf16[32,256]{1,0:T(8,128)(2,1)S(1)}, bf16[32,256]{1,0:T(8,128)(2,1)S(1)}, u32[]{:S(2)}, u32[]{:S(2)}) collective-permute-start(bf16[32,256]{1,0:T(8,128)(2,1)S(1)} %get-tuple-element.55), channel_id=1, source_target_pairs={{0,1},{1,0},{2,3},{3,2},{4,5},{5,4},{6,7},{7,6},{8,9},{9,8},{10,11... | collective-permute-start | bytes 49160 | tf_op jit(solution)/shard_map/ppermute | solution.py:629
  14.3 3.7 %collective-permute-start.5 = (bf16[32,256]{1,0:T(8,128)(2,1)S(1)}, bf16[32,256]{1,0:T(8,128)(2,1)S(1)}, u32[]{:S(2)}, u32[]{:S(2)}) collective-permute-start(bf16[32,256]{1,0:T(8,128)(2,1)S(1)} %get-tuple-element.60), channel_id=1, source_target_pairs={{0,16},{1,2},{2,1},{3,4},{4,3},{5,6},{6,5},{7,8},{8,7},{9,10},{10,... | collective-permute-start | bytes 49160 | tf_op jit(solution)/shard_map/ppermute | solution.py:628

commit v3 on v2

--- a/solution.py
+++ b/solution.py
@@ -107,10 +107,10 @@
             mask_three[at : at + 8] = beside([mask, mask])
 
 
-def edges_kernel(features, bits, to_a, to_b):
+def edges_kernel(features, bits, edge, *, near):
     last = features.shape[2] - 128
     lane = iota((64, 128), 1)
-    odd = on_odd_place()
+    low_wanted = on_odd_place() == near
     for q in range(features.shape[0] // 2):
         low, high = [
             [
@@ -122,8 +122,21 @@
         ]
         lows = jnp.where(lane < 64, low[0], pltpu.roll(low[1], 64, 1))
         highs = jnp.where(lane < 64, pltpu.roll(high[0], 64, 1), high[1])
-        to_a[q] = jnp.where(odd, lows, highs).astype(BF16)
-        to_b[q] = jnp.where(odd, highs, lows).astype(BF16)
+        edge[q] = jnp.where(low_wanted, lows, highs).astype(BF16)
+
+
+def far_edge_kernel(features, bits, edge):
+    edges_kernel(features, bits, edge, near=False)
+
+
+def near_edge_kernel(features, bits, earlier, edge):
+    edges_kernel(features, bits, edge, near=True)
+
+
+def near_face_kernel(planes, earlier, face):
+    rows = face.shape[0]
+    begin = pl.multiple_of(jnp.where(on_odd_place(), 0, rows), rows)
+    face[...] = planes[pl.ds(begin, rows), :]
 
 
 def slot_rows(neighbours):
@@ -320,7 +333,7 @@
 
 def faces_one_kernel(
     neighbours, from_a, from_b, face_taps, partial, reduce, pair_words, mask_two,
-    outer, second, to_a, to_b,
+    outer, second, to_b,
     halo, windows, low_sums, high_sums,
 ):
     count = outer.shape[0]
@@ -372,9 +385,8 @@
             (jnp.maximum(sums[2 * b + side], 0.0) * mask_two[3 * side, at]).astype(BF16)
             for side in range(2)
         ]
-        second[0, at] = planes[0]
-        second[1, at] = planes[1]
-        to_a[at] = jnp.where(odd, planes[0], planes[1])
+        second[16 * b : 16 * (b + 1)] = planes[0]
+        second[16 * (count + b) : 16 * (count + b + 1)] = planes[1]
         to_b[at] = jnp.where(odd, planes[1], planes[0])
 
 
@@ -439,8 +451,8 @@
 ):
     copy = pltpu.make_async_copy(first, result, stored)
     copy.start()
-    rows = outer.shape[1]
-    planes = beside([outer[0], inner[0], inner[1], outer[1]])
+    rows = inner.shape[1]
+    planes = beside([outer[:rows], inner[0], inner[1], outer[rows:]])
     moved = dot(own_gather[...], planes).astype(BF16)
     left = beside(
         [
@@ -472,7 +484,7 @@
 
 def faces_two_kernel(
     gathers, children, partial, from_b, kernel, reduce, mask_two, mask_three,
-    second, third, to_a, to_b,
+    second, third, to_b,
 ):
     count = second.shape[0]
     rows = 16 * count
@@ -509,7 +521,6 @@
     value = jnp.maximum(sums, 0.0) * mask_three[...]
     third[...] = value.astype(BF16)
     low, high = value[: 4 * count], value[4 * count :]
-    to_a[...] = jnp.where(odd, low, high).astype(BF16)
     to_b[...] = jnp.where(odd, high, low).astype(BF16)
 
 
@@ -641,7 +652,9 @@
         [],
         occupancy,
     )
-    from_a, from_b = exchange(*call(edges_kernel, 0.02, (face, face), [], features, bits))
+    to_b = call(far_edge_kernel, 0.02, face, [], features, bits)
+    to_a = call(near_edge_kernel, 0.02, face, [], features, bits, to_b)
+    from_a, from_b = exchange(to_a, to_b)
     own_two, sides_two = call(
         level_two_tables_kernel,
         0.4,
@@ -672,10 +685,10 @@
     plane = shape((16 * count, 128), BF16)
     planes = shape((2, 16 * count, 128), BF16)
     sums = pltpu.VMEM((count * 64, 128), F32)
-    outer, outer_two, to_a, to_b = call(
+    outer, outer_two, to_b = call(
         faces_one_kernel,
         1.5,
-        (shape((count, 2, 64, 128), BF16), planes, plane, plane),
+        (shape((count, 2, 64, 128), BF16), shape((2 * 16 * count, 128), BF16), plane),
         [
             pltpu.VMEM((count + 1, 64, 128), F32),
             pltpu.VMEM((count, 3, 6, 16, 128), BF16),
@@ -684,6 +697,7 @@
         ],
         neighbours, from_a, from_b, face_taps, partial, reduce_taps, pair_words, mask_two,
     )
+    to_a = call(near_face_kernel, 0.02, plane, [], outer_two, to_b)
     from_a, from_b = exchange(to_a, to_b)
 
     first_level, inner_two = call(
@@ -702,14 +716,15 @@
         store=(1,),
     )
     face = shape((4 * count, 256), BF16)
-    second_level, third, to_a, to_b = call(
+    second_level, third, to_b = call(
         faces_two_kernel,
         0.9,
-        (shape((count, 64, 128), BF16), shape((8 * count, 256), BF16), face, face),
+        (shape((count, 64, 128), BF16), shape((8 * count, 256), BF16), face),
         [],
         sides_two, child_rows(), partial, from_b, conv_two, second_reduce_kernel, mask_two,
         mask_three,
     )
+    to_a = call(near_face_kernel, 0.02, face, [], third, to_b)
     from_a, from_b = exchange(to_a, to_b)
 
     own_three, far_three = call(

time: 19.2 us -> 18.6 us (0.969)
  starting transfers between devices: 7.51 us -> 6.88 us
    ppermute x3, starting transfers between devices: 1.57 us -> 0.73 us  [exchange(): return (lax.ppermute(to_a, axes, within), from_b)]
    ppermute x3, waiting for transfers between devices: 0.72 us -> 0.01 us  [exchange(): from_b = lax.ppermute(to_b, axes, across)]
    ppermute x3, waiting for transfers between devices: 0.01 us -> 0.62 us  [exchange(): return (lax.ppermute(to_a, axes, within), from_b)]
    ppermute x3, starting transfers between devices: 5.94 us -> 6.15 us  [exchange(): from_b = lax.ppermute(to_b, axes, across)]
    pallas_call x11 -> x14, Pallas kernels: 9.05 us -> 9.16 us  [call(): pl.pallas_call(kernel, out_shape=out_shape, in_specs=[ANY if n in remain...]
  transfers between devices with their start and end apart: 6 -> 6, of which waited for: 1 -> 2; matrix products, arithmetic and copies ran while one was open for 0% -> 0% of each run, Pallas kernels for 31% -> 33%
where the time goes in v3:
time: 18.6 us; the launch traced here: 18.4 us
  Pallas kernels  9.16 us (49%)
  starting transfers between devices  6.88 us (37%)
  local copies, waits for them, and re-layouts  0.91 us (5%)
  between operations  0.83 us (4%)
  waiting for transfers between devices  0.62 us (3%)
    pallas_call x14, Pallas kernels, call(): pl.pallas_call(kernel, out_shape=out_shape, in_specs=[ANY if n in remain...  9.16 us
    ppermute x3, starting transfers between devices, exchange(): from_b = lax.ppermute(to_b, axes, across)  6.15 us
    unnamed x22, local copies, waits for them, and re-layouts  0.91 us
    ppermute x3, starting transfers between devices, exchange(): return (lax.ppermute(to_a, axes, within), from_b)  0.73 us
    ppermute x3, waiting for transfers between devices, exchange(): return (lax.ppermute(to_a, axes, within), from_b)  0.62 us
  transfers between devices with their start and end apart: 6, of which 2 were waited for; matrix products, arithmetic and copies ran while one was open for 0% of the time, Pallas kernels for 33%

profile of v3, /device:TPU:0, one launch (start us, length us, event | category | flops | bytes accessed | tf_op | source)
XLA Modules:
  0.0 18.4 jit_solution(10616201087887897535)
XLA Ops:
  0.6 0.0 copy-start.2
  0.6 0.0 copy-start.4
  0.7 0.0 copy-start.5
  0.7 0.0 copy-start.6
  0.7 0.8 %copy-done.6 = s32[8,16]{1,0:T(8,128)S(1)} copy-done((s32[8,16]{1,0:T(8,128)S(1)}, s32[8,16]{1,0:T(8,128)}, u32[]{:S(2)}) %copy-start.6) | copy-done | bytes 536
  1.4 0.0 copy-start.7
  1.4 0.1 shard_map.130
  1.6 0.1 copy-done.2
  1.7 0.1 shard_map.131.earlier
  1.8 3.0 %collective-permute-start.1 = (bf16[4,64,128]{2,1,0:T(8,128)(2,1)S(1)}, bf16[4,64,128]{2,1,0:T(8,128)(2,1)S(1)}, u32[]{:S(2)}, u32[]{:S(2)}) collective-permute-start(bf16[4,64,128]{2,1,0:T(8,128)(2,1)S(1)} %shard_map.131.earlier), channel_id=1, source_target_pairs={{0,16},{1,2},{2,1},{3,4},{4,3},{5,6},{6,5},{7,8},{8,7},{9,10},{10,... | collective-permute-start | bytes 196616 | tf_op jit(solution)/shard_map/ppermute | solution.py:639
  4.8 0.1 shard_map.132
  4.9 0.0 copy-start.9
  4.9 0.2 %collective-permute-start = (bf16[4,64,128]{2,1,0:T(8,128)(2,1)S(1)}, bf16[4,64,128]{2,1,0:T(8,128)(2,1)S(1)}, u32[]{:S(2)}, u32[]{:S(2)}) collective-permute-start(bf16[4,64,128]{2,1,0:T(8,128)(2,1)S(1)} %shard_map.132), channel_id=1, source_target_pairs={{0,1},{1,0},{2,3},{3,2},{4,5},{5,4},{6,7},{7,6},{8,9},{9,8},{10,11... | collective-permute-start | bytes 196616 | tf_op jit(solution)/shard_map/ppermute | solution.py:640
  5.1 0.0 copy-done.4
  5.1 0.0 copy-done.5
  5.1 0.0 copy-done.7
  5.1 1.9 %shard_map.133 = (bf16[8,3,6,16,128]{4,3,2,1,0:T(8,128)(2,1)S(1)}, bf16[1152,256]{1,0:T(8,128)(2,1)S(1)}, bf16[1152,128]{1,0:T(8,128)(2,1)S(1)}, bf16[256,256]{1,0:T(8,128)(2,1)S(1)}, f32[4,512,128]{2,1,0:T(8,128)S(1)}) custom-call(s32[8,27]{1,0:T(8,128)S(1)} %copy-done.7, f32[4,8,128]{2,1,0:T(8,128)S(1)} %get-tuple-element.28.bits, ...), custom_call_target="tpu_custom_call" | custom-call | flops 20000000000 | bytes 10000000 | tf_op jit(solution)/shard_map/pallas_call | solution.py:595
  7.0 0.0 copy-done.9
  7.1 0.4 %shard_map.136 = (bf16[1152,128]{1,0:T(8,128)(2,1)S(1)}, bf16[2,1152,128]{2,1,0:T(8,128)(2,1)S(1)}) custom-call(s32[8,27]{1,0:T(8,128)S(1)} %copy-done.7, bf16[432,27]{1,0:T(8,128)(2,1)S(1)} %copy-done.9), custom_call_target="tpu_custom_call" | custom-call | flops 4000000000 | bytes 10000000 | tf_op jit(solution)/shard_map/pallas_call | solution.py:595
  7.5 0.0 collective-permute-done.from_a
  7.5 0.0 collective-permute-done.1.from_b
  7.5 1.0 %shard_map.134 = (bf16[8,2,64,128]{3,2,1,0:T(8,128)(2,1)S(1)}, bf16[256,128]{1,0:T(8,128)(2,1)S(1)}, bf16[128,128]{1,0:T(8,128)(2,1)S(1)}) custom-call(s32[8,27]{1,0:T(8,128)S(1)} %copy-done.7, bf16[4,64,128]{2,1,0:T(8,128)(2,1)S(1)} %collective-permute-done.from_a, bf16[4,64,128]{2,1,0:T(8,128)(2,1)S(1)} %collective-permute-done.1.from_b, ...), custom_call_target="tpu_custom_call" | custom-call | flops 15000000512 | bytes 10000000 | tf_op jit(solution)/shard_map/pallas_call | solution.py:595
  8.4 0.0 copy-start.1
  8.4 1.6 %collective-permute-start.3 = (bf16[128,128]{1,0:T(8,128)(2,1)S(1)}, bf16[128,128]{1,0:T(8,128)(2,1)S(1)}, u32[]{:S(2)}, u32[]{:S(2)}) collective-permute-start(bf16[128,128]{1,0:T(8,128)(2,1)S(1)} %get-tuple-element.41.earlier), channel_id=1, source_target_pairs={{0,16},{1,2},{2,1},{3,4},{4,3},{5,6},{6,5},{7,8},{8,7},{9,10},{10,... | collective-permute-start | bytes 98312 | tf_op jit(solution)/shard_map/ppermute | solution.py:639
  10.1 0.1 collective-permute-start.2
  10.2 1.0 %shard_map.135 = (bf16[8,64,512]{2,1,0:T(8,128)(2,1)S(1)}, bf16[2,128,128]{2,1,0:T(8,128)(2,1)S(1)}) custom-call(bf16[8,3,6,16,128]{4,3,2,1,0:T(8,128)(2,1)S(1)} %get-tuple-element.35.middle, bf16[1152,256]{1,0:T(8,128)(2,1)S(1)} %get-tuple-element.36.taps, f32[4,512,128]{2,1,0:T(8,128)S(1)} %get-tuple-element.30.partial, ...), custom_call_target="tpu_custom_call" | custom-call | flops 500000000 | bytes 10000000 | tf_op jit(solution)/shard_map/pallas_call | solution.py:595
  11.1 0.2 %collective-permute-done.2.from_a = bf16[128,128]{1,0:T(8,128)(2,1)S(1)} collective-permute-done((bf16[128,128]{1,0:T(8,128)(2,1)S(1)}, bf16[128,128]{1,0:T(8,128)(2,1)S(1)}, u32[]{:S(2)}, u32[]{:S(2)}) %collective-permute-start.2) | collective-permute-done | bytes 32800 | tf_op jit(solution)/shard_map/ppermute | solution.py:640
  11.3 0.0 copy-done.1
  11.3 0.0 copy-start.3
  11.3 0.0 copy-start.10
  11.3 1.2 %shard_map.138 = (f32[512,128]{1,0:T(8,128)S(1)}, bf16[8,64,512]{2,1,0:T(8,128)(2,1)}) custom-call(bf16[256,128]{1,0:T(8,128)(2,1)S(1)} %get-tuple-element.34.planes.outer, bf16[2,128,128]{2,1,0:T(8,128)(2,1)S(1)} %get-tuple-element.38.inner, bf16[1152,128]{1,0:T(8,128)(2,1)S(1)} %get-tuple-element.39.own_gather, ...), custom_call_target="tpu_custom_call" | custom-call | flops 10000000000 | bytes 10000000 | tf_op jit(solution)/shard_map/pallas_call | solution.py:595
  12.5 0.0 collective-permute-done.3.from_b
  12.5 0.0 copy-done.3
  12.6 0.0 copy-done.10
  12.6 0.0 copy-start.8
  12.6 0.0 copy-start
  12.6 0.8 %shard_map.139 = (bf16[8,64,128]{2,1,0:T(8,128)(2,1)S(1)}, bf16[64,256]{1,0:T(8,128)(2,1)S(1)}, bf16[32,256]{1,0:T(8,128)(2,1)S(1)}) custom-call(bf16[2,1152,128]{2,1,0:T(8,128)(2,1)S(1)} %get-tuple-element.40.gathers, bf16[128,128]{1,0:T(8,128)(2,1)S(1)} %copy-done.10, f32[512,128]{1,0:T(8,128)S(1)} %get-tuple-element.44.partial, ...), custom_call_target="tpu_custom_call" | custom-call | flops 8999999488 | bytes 10000000 | tf_op jit(solution)/shard_map/pallas_call | solution.py:595
  13.4 1.5 %collective-permute-start.5 = (bf16[32,256]{1,0:T(8,128)(2,1)S(1)}, bf16[32,256]{1,0:T(8,128)(2,1)S(1)}, u32[]{:S(2)}, u32[]{:S(2)}) collective-permute-start(bf16[32,256]{1,0:T(8,128)(2,1)S(1)} %get-tuple-element.48.earlier), channel_id=1, source_target_pairs={{0,16},{1,2},{2,1},{3,4},{4,3},{5,6},{6,5},{7,8},{8,7},{9,10},{10,... | collective-permute-start | bytes 49160 | tf_op jit(solution)/shard_map/ppermute | solution.py:639
  14.9 0.5 %collective-permute-start.4 = (bf16[32,256]{1,0:T(8,128)(2,1)S(1)}, bf16[32,256]{1,0:T(8,128)(2,1)S(1)}, u32[]{:S(2)}, u32[]{:S(2)}) collective-permute-start(bf16[32,256]{1,0:T(8,128)(2,1)S(1)} %shard_map.141), channel_id=1, source_target_pairs={{0,1},{1,0},{2,3},{3,2},{4,5},{5,4},{6,7},{7,6},{8,9},{9,8},{10,11... | collective-permute-start | bytes 49160 | tf_op jit(solution)/shard_map/ppermute | solution.py:640
  15.4 0.0 copy-done.8
  15.4 0.4 %shard_map.140 = (bf16[1728,96]{1,0:T(8,128)(2,1)S(1)}, bf16[288,32]{1,0:T(8,128)(2,1)S(1)}) custom-call(s32[8,27]{1,0:T(8,128)S(1)} %copy-done.7, bf16[432,27]{1,0:T(8,128)(2,1)S(1)} %copy-done.8, bf16[64,256]{1,0:T(8,128)(2,1)S(1)} %get-tuple-element.46.later.planes.third), custom_call_target="tpu_custom_call" | custom-call | flops 200000000 | bytes 10000000 | tf_op jit(solution)/shard_map/pallas_call | solution.py:595
  15.8 0.4 %collective-permute-done.4.from_a = bf16[32,256]{1,0:T(8,128)(2,1)S(1)} collective-permute-done((bf16[32,256]{1,0:T(8,128)(2,1)S(1)}, bf16[32,256]{1,0:T(8,128)(2,1)S(1)}, u32[]{:S(2)}, u32[]{:S(2)}) %collective-permute-start.4) | collective-permute-done | bytes 16416 | tf_op jit(solution)/shard_map/ppermute | solution.py:640
  16.2 0.0 copy-done
  16.2 1.1 %shard_map.142 = (f32[64,256]{1,0:T(8,128)S(1)}, bf16[8,64,128]{2,1,0:T(8,128)(2,1)}) custom-call(bf16[1728,96]{1,0:T(8,128)(2,1)S(1)} %get-tuple-element.47.gather, bf16[64,256]{1,0:T(8,128)(2,1)S(1)} %get-tuple-element.46.later.planes.third, bf16[32,256]{1,0:T(8,128)(2,1)S(1)} %collective-permute-done.4.from_a, bf16[27,256,256]{2,1,0:T(8,128)(2,1)S(1)} %copy-done, ...), custom_call_target="tpu_custom_call" | custom-call | flops 10000000000 | bytes 10000000 | tf_op jit(solution)/shard_map/pallas_call | solution.py:595
  17.3 0.0 collective-permute-done.5.from_b
  17.3 1.1 %shard_map.143 = bf16[8,8,256]{2,1,0:T(8,128)(2,1)} custom-call(bf16[288,32]{1,0:T(8,128)(2,1)S(1)} %get-tuple-element.51.gather, f32[64,256]{1,0:T(8,128)S(1)} %get-tuple-element.52.partial, bf16[32,256]{1,0:T(8,128)(2,1)S(1)} %collective-permute-done.5.from_b, bf16[27,256,256]{2,1,0:T(8,128)(2,1)S(1)} %copy-done, f32[64,256]{1,0:T(8,128)S(1)} %get-tuple-element.45.mask_three), custom_call_target="tpu_custom_call" | custom-call | flops 10000000000 | bytes 10000000 | tf_op jit(solution)/shard_map/pallas_call | solution.py:595
  (2 shorter events, 0.0 us)
Async XLA Ops:
  0.6 1.1 %copy-start.2 = (bf16[8,512,64]{1,2,0:T(8,128)(2,1)S(1)}, bf16[8,512,64]{1,2,0:T(8,128)(2,1)}, u32[]{:S(2)}) copy-start(bf16[8,512,64]{1,2,0:T(8,128)(2,1)} %param.11) | copy-start | bytes 1572868
  0.6 4.5 %copy-start.4 = (bf16[27,64,64]{2,1,0:T(8,128)(2,1)S(1)}, bf16[27,64,64]{2,1,0:T(8,128)(2,1)}, u32[]{:S(2)}) copy-start(bf16[27,64,64]{2,1,0:T(8,128)(2,1)} %kernel.5) | copy-start | bytes 663556
  0.7 4.5 %copy-start.5 = (bf16[8,64,128]{2,1,0:T(8,128)(2,1)S(1)}, bf16[8,64,128]{2,1,0:T(8,128)(2,1)}, u32[]{:S(2)}) copy-start(bf16[8,64,128]{2,1,0:T(8,128)(2,1)} %reduce.2) | copy-start | bytes 393220
  0.7 0.8 %copy-start.6 = (s32[8,16]{1,0:T(8,128)S(1)}, s32[8,16]{1,0:T(8,128)}, u32[]{:S(2)}) copy-start(s32[8,16]{1,0:T(8,128)} %occupancy.1) | copy-start | bytes 1540
  1.4 3.7 %copy-start.7 = (s32[8,27]{1,0:T(8,128)S(1)}, s32[8,27]{1,0:T(8,128)}, u32[]{:S(2)}) copy-start(s32[8,27]{1,0:T(8,128)} %neighbours.7) | copy-start | bytes 2596
  1.8 5.7 %collective-permute-start.1 = (bf16[4,64,128]{2,1,0:T(8,128)(2,1)S(1)}, bf16[4,64,128]{2,1,0:T(8,128)(2,1)S(1)}, u32[]{:S(2)}, u32[]{:S(2)}) collective-permute-start(bf16[4,64,128]{2,1,0:T(8,128)(2,1)S(1)} %shard_map.131.earlier), channel_id=1, source_target_pairs={{0,16},{1,2},{2,1},{3,4},{4,3},{5,6},{6,5},{7,8},{8,7},{9,10},{10,... | collective-permute-start | bytes 196616 | tf_op jit(solution)/shard_map/ppermute | solution.py:639
  4.9 2.1 %copy-start.9 = (bf16[432,27]{1,0:T(8,128)(2,1)S(1)}, bf16[432,27]{1,0:T(8,128)(2,1)}, u32[]{:S(2)}) copy-start(bf16[432,27]{1,0:T(8,128)(2,1)} %constant.6.clone.pick) | copy-start | bytes 69988
  4.9 2.5 %collective-permute-start = (bf16[4,64,128]{2,1,0:T(8,128)(2,1)S(1)}, bf16[4,64,128]{2,1,0:T(8,128)(2,1)S(1)}, u32[]{:S(2)}, u32[]{:S(2)}) collective-permute-start(bf16[4,64,128]{2,1,0:T(8,128)(2,1)S(1)} %shard_map.132), channel_id=1, source_target_pairs={{0,1},{1,0},{2,3},{3,2},{4,5},{5,4},{6,7},{7,6},{8,9},{9,8},{10,11... | collective-permute-start | bytes 196616 | tf_op jit(solution)/shard_map/ppermute | solution.py:640
  8.4 2.9 %copy-start.1 = (bf16[27,128,128]{2,1,0:T(8,128)(2,1)S(1)}, bf16[27,128,128]{2,1,0:T(8,128)(2,1)}, u32[]{:S(2)}) copy-start(bf16[27,128,128]{2,1,0:T(8,128)(2,1)} %kernel.7) | copy-start | bytes 2654212
  8.4 4.1 %collective-permute-start.3 = (bf16[128,128]{1,0:T(8,128)(2,1)S(1)}, bf16[128,128]{1,0:T(8,128)(2,1)S(1)}, u32[]{:S(2)}, u32[]{:S(2)}) collective-permute-start(bf16[128,128]{1,0:T(8,128)(2,1)S(1)} %get-tuple-element.41.earlier), channel_id=1, source_target_pairs={{0,16},{1,2},{2,1},{3,4},{4,3},{5,6},{6,5},{7,8},{8,7},{9,10},{10,... | collective-permute-start | bytes 98312 | tf_op jit(solution)/shard_map/ppermute | solution.py:639
  10.1 1.2 %collective-permute-start.2 = (bf16[128,128]{1,0:T(8,128)(2,1)S(1)}, bf16[128,128]{1,0:T(8,128)(2,1)S(1)}, u32[]{:S(2)}, u32[]{:S(2)}) collective-permute-start(bf16[128,128]{1,0:T(8,128)(2,1)S(1)} %shard_map.137), channel_id=1, source_target_pairs={{0,1},{1,0},{2,3},{3,2},{4,5},{5,4},{6,7},{7,6},{8,9},{9,8},{10,11... | collective-permute-start | bytes 98312 | tf_op jit(solution)/shard_map/ppermute | solution.py:640
  11.3 1.2 %copy-start.3 = (bf16[8,128,256]{2,1,0:T(8,128)(2,1)S(1)}, bf16[8,128,256]{2,1,0:T(8,128)(2,1)}, u32[]{:S(2)}) copy-start(bf16[8,128,256]{2,1,0:T(8,128)(2,1)} %reduce.3) | copy-start | bytes 1572868
  11.3 1.2 %copy-start.10 = (bf16[128,128]{1,0:T(8,128)(2,1)S(1)}, bf16[128,128]{1,0:T(8,128)(2,1)}, u32[]{:S(2)}) copy-start(bf16[128,128]{1,0:T(8,128)(2,1)} %constant.7.clone.children) | copy-start | bytes 98308
  12.6 2.8 %copy-start.8 = (bf16[432,27]{1,0:T(8,128)(2,1)S(1)}, bf16[432,27]{1,0:T(8,128)(2,1)}, u32[]{:S(2)}) copy-start(bf16[432,27]{1,0:T(8,128)(2,1)} %constant.8.clone.pick) | copy-start | bytes 69988
  12.6 3.7 %copy-start = (bf16[27,256,256]{2,1,0:T(8,128)(2,1)S(1)}, bf16[27,256,256]{2,1,0:T(8,128)(2,1)}, u32[]{:S(2)}) copy-start(bf16[27,256,256]{2,1,0:T(8,128)(2,1)} %kernel.9) | copy-start | bytes 10616836
  13.4 3.9 %collective-permute-start.5 = (bf16[32,256]{1,0:T(8,128)(2,1)S(1)}, bf16[32,256]{1,0:T(8,128)(2,1)S(1)}, u32[]{:S(2)}, u32[]{:S(2)}) collective-permute-start(bf16[32,256]{1,0:T(8,128)(2,1)S(1)} %get-tuple-element.48.earlier), channel_id=1, source_target_pairs={{0,16},{1,2},{2,1},{3,4},{4,3},{5,6},{6,5},{7,8},{8,7},{9,10},{10,... | collective-permute-start | bytes 49160 | tf_op jit(solution)/shard_map/ppermute | solution.py:639
  14.9 1.3 %collective-permute-start.4 = (bf16[32,256]{1,0:T(8,128)(2,1)S(1)}, bf16[32,256]{1,0:T(8,128)(2,1)S(1)}, u32[]{:S(2)}, u32[]{:S(2)}) collective-permute-start(bf16[32,256]{1,0:T(8,128)(2,1)S(1)} %shard_map.141), channel_id=1, source_target_pairs={{0,1},{1,0},{2,3},{3,2},{4,5},{5,4},{6,7},{7,6},{8,9},{9,8},{10,11... | collective-permute-start | bytes 49160 | tf_op jit(solution)/shard_map/ppermute | solution.py:640

commit v4 on v3

--- a/solution.py
+++ b/solution.py
@@ -60,7 +60,11 @@
     return jnp.where(number < 0, count, number + shift - lax.axis_index(LINE) * count)
 
 
-def masks_kernel(occupancy, bits, pair_words, mask_two, mask_three):
+def blank_kernel(notes):
+    notes[...] = jnp.zeros(notes.shape, F32)
+
+
+def masks_kernel(occupancy, blank, bits, edge_bits, pair_words, mask_two, mask_three):
     count = occupancy.shape[0]
     for q in range(4):
         bits[q] = column_bits(occupancy[...], q)
@@ -86,6 +90,13 @@
                     for half in range(2)
                 ]
             )
+    plane, half, m = [jnp.bitwise_and(lax.shift_right_logical(lane, n), 1) for n in (4, 3, 2)]
+    for side in range(2):
+        word = [any_two[4 * side + n] for n in range(4)]
+        word = jnp.where(
+            plane == 0, jnp.where(half == 0, word[0], word[1]), jnp.where(half == 0, word[2], word[3])
+        )
+        edge_bits[side] = bits_of(word, 16 * m + 2 * jnp.bitwise_and(lane, 3))
     any_three = []
     for i in range(2):
         for j in range(2):
@@ -107,10 +118,10 @@
             mask_three[at : at + 8] = beside([mask, mask])
 
 
-def edges_kernel(features, bits, edge, *, near):
+def edge_planes(features, bits, low_wanted):
     last = features.shape[2] - 128
     lane = iota((64, 128), 1)
-    low_wanted = on_odd_place() == near
+    planes = []
     for q in range(features.shape[0] // 2):
         low, high = [
             [
@@ -122,15 +133,26 @@
         ]
         lows = jnp.where(lane < 64, low[0], pltpu.roll(low[1], 64, 1))
         highs = jnp.where(lane < 64, pltpu.roll(high[0], 64, 1), high[1])
-        edge[q] = jnp.where(low_wanted, lows, highs).astype(BF16)
-
-
-def far_edge_kernel(features, bits, edge):
-    edges_kernel(features, bits, edge, near=False)
+        planes.append(jnp.where(low_wanted, lows, highs).astype(BF16))
+    return planes
+
+
+def far_edge_kernel(features, bits, neighbours, edge_bits, blank, edge, notes):
+    count = features.shape[0]
+    odd = on_odd_place()
+    for q, plane in enumerate(edge_planes(features, bits, jnp.logical_not(odd))):
+        edge[64 * q : 64 * (q + 1), :] = plane
+    notes[...] = blank[...]
+    notes[:count, : neighbours.shape[1]] = jnp.where(
+        neighbours[...] < 0, 4 * count, slot_numbers(neighbours)
+    ).astype(F32)
+    notes[count:, :] = edge_bits[jnp.where(odd, 1, 0)]
+    edge[32 * count :, :] = notes[...].astype(BF16)
 
 
 def near_edge_kernel(features, bits, earlier, edge):
-    edges_kernel(features, bits, edge, near=True)
+    for q, plane in enumerate(edge_planes(features, bits, on_odd_place())):
+        edge[q] = plane
 
 
 def near_face_kernel(planes, earlier, face):
@@ -139,28 +161,29 @@
     face[...] = planes[pl.ds(begin, rows), :]
 
 
-def slot_rows(neighbours):
-    count = neighbours.shape[0]
-    slot = jnp.where(neighbours[...] < 0, 4 * count, slot_numbers(neighbours)).astype(F32)
+def slot_rows(slot):
     return stack(
-        [jnp.broadcast_to(slot[b : b + 1], (128, slot.shape[1])) for b in range(count)]
+        [jnp.broadcast_to(slot[b : b + 1], (128, slot.shape[1])) for b in range(slot.shape[0])]
     ).astype(BF16)
+
+
+def own_slot_rows(neighbours):
+    slot = jnp.where(neighbours[...] < 0, 4 * neighbours.shape[0], slot_numbers(neighbours))
+    return slot_rows(slot.astype(F32))
 
 
 def times_transposed(x, y):
     return lax.dot_general(x, y, (((1,), (1,)), ((), ())), preferred_element_type=F32)
 
 
-def level_two_tables_kernel(neighbours, pick, own_two, sides_two):
-    count = neighbours.shape[0]
-    rows = times_transposed(pick[...], slot_rows(neighbours))
+def fill_level_two_tables(tables, rows, count):
     lane = iota((16, 16 * count), 1)
     row = iota((16, 16 * count), 0)
     j, k = lax.shift_right_logical(row, 2), jnp.bitwise_and(row, 3)
     for q in range(9):
         source = 4 * jnp.bitwise_and(j + q // 3 + 3, 3) + jnp.bitwise_and(k + q % 3 + 3, 3)
         wanted = (lane - source).astype(F32)
-        for a, table in enumerate((sides_two.at[0], own_two, sides_two.at[1])):
+        for a, table in enumerate(tables):
             at = 16 * (9 * a + q)
             for b in range(count):
                 table[16 * (count * q + b) : 16 * (count * q + b + 1), :] = jnp.where(
@@ -168,10 +191,56 @@
                 ).astype(BF16)
 
 
-def level_three_tables_kernel(neighbours, pick, later, own_three, far_three):
+def level_two_tables_kernel(neighbours, pick, later, own_two, sides_two):
+    rows = times_transposed(pick[...], own_slot_rows(neighbours))
+    fill_level_two_tables(
+        (sides_two.at[0], own_two, sides_two.at[1]), rows, neighbours.shape[0]
+    )
+
+
+def far_tables_kernel(message, pick, later, own_two, toward_two, mask_two, mask_three):
+    count = own_two.shape[1] // 16
+    notes = message[32 * count :, :].astype(F32)
+    slots = slot_rows(notes[:count, : pick.shape[1]])
+    begin = pl.multiple_of(jnp.where(on_odd_place(), 0, 288), 16)
+    rows = stack(
+        [
+            times_transposed(pick[pl.ds(begin, 144), :], slots),
+            times_transposed(pick[144:288, :], slots),
+        ]
+    )
+    fill_level_two_tables((toward_two, own_two), rows, count)
+
+    every = jnp.ones((128, 256), BF16)
+    lane = iota((16, 128), 1)
+    row = iota((16, 128), 0)
+    bits = [notes[count + b : count + b + 1] for b in range(count)]
+    chosen = stack(
+        [
+            jnp.where(lane == 16 * plane + row, jnp.broadcast_to(bits[b], (16, 128)), 0.0)
+            for plane in range(2)
+            for b in range(count)
+        ]
+    ).astype(BF16)
+    mask_two[...] = dot(chosen, every[:, :128])
+    lane, row = lane[:8], row[:8]
+    child = jnp.bitwise_and(lax.shift_right_logical(lane, 2), 2) + jnp.bitwise_and(
+        lax.shift_right_logical(lane, 1), 1
+    )
+    wanted = (child == jnp.bitwise_and(row, 3)) & (lane < 32)
+    chosen = stack(
+        [
+            jnp.where(wanted, jnp.where(row < 4, bits[b], bits[b + 1]), 0.0)
+            for b in range(0, count, 2)
+        ]
+    ).astype(BF16)
+    mask_three[...] = jnp.where(dot(chosen, every) > 0.5, 1.0, 0.0)
+
+
+def level_three_tables_kernel(neighbours, pick, later, own_three, near_three):
     count = neighbours.shape[0]
     odd = on_odd_place()
-    rows = times_transposed(pick[...], slot_rows(neighbours))
+    rows = times_transposed(pick[...], own_slot_rows(neighbours))
     row = iota((8, 128), 0)
     lane = iota((8, 128), 1)
     j, k = [jnp.bitwise_and(lax.shift_right_logical(row, n), 1) for n in (1, 0)]
@@ -193,16 +262,16 @@
         for i in range(2):
             x = i + tap // 9 - 1
             if x < 0:
+                begin = jnp.where(odd, nowhere, 8 * count)
+            elif x > 1:
                 begin = jnp.where(odd, 8 * count, nowhere)
-            elif x > 1:
-                begin = jnp.where(odd, nowhere, 8 * count)
             else:
                 begin = 4 * count * x
             at = 8 * count * tap + 4 * count * i
             own_three[at : at + 4 * count, :] = block(tap, i, begin)[:, : 12 * count].astype(BF16)
     for q in range(9):
-        tile = jnp.where(odd, block(18 + q, 1, 0), block(q, 0, 0))
-        far_three[4 * count * q : 4 * count * (q + 1), :] = tile[:, : 4 * count].astype(BF16)
+        tile = jnp.where(odd, block(q, 0, 0), block(18 + q, 1, 0))
+        near_three[4 * count * q : 4 * count * (q + 1), :] = tile[:, : 4 * count].astype(BF16)
 
 
 def shifted_windows(source, row):
@@ -332,7 +401,7 @@
 
 
 def faces_one_kernel(
-    neighbours, from_a, from_b, face_taps, partial, reduce, pair_words, mask_two,
+    neighbours, from_a, from_b, face_taps, partial, reduce, pair_words, mask_two, inner,
     outer, second, to_b,
     halo, windows, low_sums, high_sums,
 ):
@@ -344,7 +413,7 @@
     slot = slot_numbers(neighbours)
     halo[count] = jnp.zeros((64, 128), F32)
     for q in range(count // 2):
-        one, two = from_a[q].astype(F32), from_b[q].astype(F32)
+        one, two = from_a[q].astype(F32), from_b[64 * q : 64 * (q + 1), :].astype(F32)
         m = stack([jnp.where(odd, one, two), jnp.where(odd, two, one)]).T
         halo[2 * q] = m[:64]
         halo[2 * q + 1] = m[64:]
@@ -388,15 +457,17 @@
         second[16 * b : 16 * (b + 1)] = planes[0]
         second[16 * (count + b) : 16 * (count + b + 1)] = planes[1]
         to_b[at] = jnp.where(odd, planes[1], planes[0])
+    rows = 16 * count
+    to_b[rows : 2 * rows] = jnp.where(odd, inner[1], inner[0])
+    to_b[2 * rows :] = jnp.where(odd, inner[0], inner[1])
 
 
 def inner_kernel(
-    middle, taps, partial, outer, reduce, pair_words, mask_two,
-    out, second,
+    middle, taps, partial, reduce, pair_words, mask_two,
+    inner, second,
     low_sums, high_sums,
 ):
     count = middle.shape[0]
-    lane = iota((64, 128), 1)
     added = dot(
         beside(
             [
@@ -409,31 +480,32 @@
     )
     groups = []
     for b in range(count):
+        at = slice(64 * b, 64 * (b + 1))
         for i in (1, 2):
-            at = slice(64 * b, 64 * (b + 1))
             sums = partial[i, at] + added[at, 128 * (i - 1) : 128 * i]
             groups.append(masked_tiles(sums, pair_words, b, i))
-        ordered = [
-            outer[b, 0].astype(F32),
-            stack(groups[2 * b]),
-            stack(groups[2 * b + 1]),
-            outer[b, 1].astype(F32),
-        ]
+            inner[b, i - 1] = stack(groups[-1]).astype(BF16)
+    sums = reduce_planes(groups, reduce, low_sums, high_sums)
+    for b in range(count):
+        at = slice(16 * b, 16 * (b + 1))
+        for i in (1, 2):
+            second[i - 1, at] = (
+                jnp.maximum(sums[2 * b + i - 1], 0.0) * mask_two[i, at]
+            ).astype(BF16)
+
+
+def output_kernel(outer, inner, out):
+    lane = iota((64, 128), 1)
+    for b in range(outer.shape[0]):
+        ordered = [outer[b, 0], inner[b, 0], inner[b, 1], outer[b, 1]]
         for i in (0, 2):
-            m = stack(ordered[i : i + 2]).T
+            m = stack(ordered[i : i + 2]).astype(F32).T
             top, bottom = m[:64], m[64:]
             out[b, :, 128 * i : 128 * (i + 1)] = jnp.where(
                 lane < 64, top, pltpu.roll(bottom, 64, 1)
             ).astype(BF16)
             out[b, :, 128 * (i + 1) : 128 * (i + 2)] = jnp.where(
                 lane < 64, pltpu.roll(top, 64, 1), bottom
-            ).astype(BF16)
-    sums = reduce_planes(groups, reduce, low_sums, high_sums)
-    for b in range(count):
-        at = slice(16 * b, 16 * (b + 1))
-        for i in (1, 2):
-            second[i - 1, at] = (
-                jnp.maximum(sums[2 * b + i - 1], 0.0) * mask_two[i, at]
             ).astype(BF16)
 
 
@@ -482,15 +554,36 @@
     copy.wait()
 
 
+def own_for_far_kernel(gather, to_b, kernel, part):
+    rows = part.shape[0]
+    part[...] = face_part(gather[...], to_b[:rows], kernel, jnp.where(on_odd_place(), 0, 1))
+
+
+def child_columns(picked, pairs, planes):
+    return beside(
+        [
+            stack(
+                [
+                    picked[8 * (planes * q + i) : 8 * (planes * q + i + 1), 128 * n : 128 * (n + 1)]
+                    for i in range(planes)
+                    for n in range(pairs)
+                ]
+            )
+            for q in range(8)
+        ]
+    )
+
+
 def faces_two_kernel(
-    gathers, children, partial, from_b, kernel, reduce, mask_two, mask_three,
-    second, third, to_b,
+    gathers, far_gather, children, far_children, partial, own_for_far, from_b, kernel, reduce,
+    mask_two, mask_three, far_mask_two, far_mask_three,
+    second, third, far_third,
 ):
     count = second.shape[0]
     rows = 16 * count
     odd = on_odd_place()
     high = jnp.where(odd, 1, 0)
-    far = face_part(gathers[high], from_b[...], kernel, high)
+    far = face_part(gathers[high], from_b[:rows], kernel, high)
     planes = []
     for i in range(4):
         sums = partial[i * rows : (i + 1) * rows]
@@ -502,44 +595,67 @@
     ]
     for b in range(count):
         second[b] = bricks[b]
+    picked = dot(
+        children[...], beside([stack(bricks[b : b + 2]) for b in range(0, count, 2)])
+    )
+
     moved = dot(
-        children[...], beside([stack(bricks[b : b + 2]) for b in range(0, count, 2)])
-    )
-    left = beside(
-        [
-            stack(
-                [
-                    moved[16 * q + 8 * i : 16 * q + 8 * (i + 1), 128 * n : 128 * (n + 1)]
-                    for i in range(2)
-                    for n in range(count // 2)
-                ]
-            )
-            for q in range(8)
-        ]
+        far_gather[...], beside([from_b[d * rows : (d + 1) * rows] for d in range(3)])
     ).astype(BF16)
-    sums = dot(left, reduce[...].reshape(8 * 128, 256))
-    value = jnp.maximum(sums, 0.0) * mask_three[...]
-    third[...] = value.astype(BF16)
-    low, high = value[: 4 * count], value[4 * count :]
-    to_b[...] = jnp.where(odd, high, low).astype(BF16)
-
-
-def own_three_kernel(gather, third, from_a, kernel, second, partial, result, stored):
+    left = [
+        beside([moved[q * rows : (q + 1) * rows, 128 * d : 128 * (d + 1)] for q in range(9)])
+        for d in range(3)
+    ]
+    toward, same, away = [
+        kernel[pl.ds(begin, 9)].reshape(9 * 128, 128) for begin in (18 - 18 * high, 9, 18 * high)
+    ]
+    zero = dot(left[0], beside([same, toward]))
+    one = dot(left[1], beside([away, same]))
+    near = own_for_far[...] + zero[:, :128] + one[:, :128]
+    past = zero[:, 128:] + one[:, 128:] + dot(left[2], away)
+    far_planes = [
+        (jnp.maximum(sums, 0.0) * far_mask_two[n * rows : (n + 1) * rows]).astype(BF16)
+        for n, sums in enumerate((jnp.where(odd, near, past), jnp.where(odd, past, near)))
+    ]
+    far_picked = dot(
+        far_children[...],
+        beside(
+            [
+                stack(
+                    [
+                        plane[16 * b : 16 * (b + 1)]
+                        for b in (n, n + 1)
+                        for plane in far_planes
+                    ]
+                )
+                for n in range(0, count, 2)
+            ]
+        ),
+    )
+    left = stack(
+        [child_columns(picked, count // 2, 2), child_columns(far_picked, count // 2, 1)]
+    ).astype(BF16)
+    sums = jnp.maximum(dot(left, reduce[...].reshape(8 * 128, 256)), 0.0)
+    third[...] = (sums[: 8 * count] * mask_three[...]).astype(BF16)
+    far_third[...] = (sums[8 * count :] * far_mask_three[...]).astype(BF16)
+
+
+def own_three_kernel(gather, third, far, kernel, second, partial, result, stored):
     copy = pltpu.make_async_copy(second, result, stored)
     copy.start()
     rows = third.shape[0]
-    moved = dot(gather[...], stack([third[...], from_a[...]])).astype(BF16)
+    moved = dot(gather[...], stack([third[...], far[...]])).astype(BF16)
     left = beside([moved[q * rows : (q + 1) * rows] for q in range(27)])
     partial[...] = dot(left, kernel[...].reshape(27 * 256, 256))
     copy.wait()
 
 
-def faces_three_kernel(gather, partial, from_b, kernel, mask_three, out):
-    rows = from_b.shape[0]
+def faces_three_kernel(gather, partial, from_a, kernel, mask_three, out):
+    rows = from_a.shape[0]
     odd = on_odd_place()
-    far = face_part(gather[...], from_b[...], kernel, jnp.where(odd, 1, 0))
-    low = partial[:rows] + jnp.where(odd, 0.0, far)
-    high = partial[rows:] + jnp.where(odd, far, 0.0)
+    near = face_part(gather[...], from_a[...], kernel, jnp.where(odd, 0, 1))
+    low = partial[:rows] + jnp.where(odd, near, 0.0)
+    high = partial[rows:] + jnp.where(odd, 0.0, near)
     low = jnp.maximum(low, 0.0) * mask_three[:rows]
     high = jnp.maximum(high, 0.0) * mask_three[rows:]
     row = iota((8, 256), 0)
@@ -572,14 +688,15 @@
     return jnp.asarray(pick, BF16)
 
 
-def child_rows():
-    pick = np.zeros((128, 128), np.float32)
+def child_rows(planes):
+    pick = np.zeros((8 * planes * 8, 2 * 2 * planes * 16), np.float32)
     for q in range(8):
-        for r in range(16):
+        for r in range(8 * planes):
             x, y, z = [
                 2 * n + (q >> s & 1) for n, s in ((r // 8, 2), (r // 2 % 2, 1), (r % 2, 0))
             ]
-            pick[16 * q + r, 64 * (r // 4 % 2) + 16 * x + 4 * y + z] = 1
+            at = 2 * planes * 16 * (r // 4 % 2) + 16 * x + 4 * y + z
+            pick[8 * planes * q + r, at] = 1
     return jnp.asarray(pick, BF16)
 
 
@@ -639,32 +756,30 @@
         from_b = lax.ppermute(to_b, axes, across)
         return lax.ppermute(to_a, axes, within), from_b
 
-    face = shape((count // 2, 64, 128), BF16)
-    bits, pair_words, mask_two, mask_three = call(
+    blank = call(blank_kernel, 1.0, shape((2 * count, 128), F32), [])
+    bits, edge_bits, pair_words, mask_two, mask_three = call(
         masks_kernel,
-        0.3,
+        0.01,
         (
             shape((4, count, 128), F32),
+            shape((2, count, 128), F32),
             shape((8, count, 128), jnp.int32),
             shape((4, 16 * count, 128), F32),
             shape((8 * count, 256), F32),
         ),
         [],
-        occupancy,
-    )
-    to_b = call(far_edge_kernel, 0.02, face, [], features, bits)
+        occupancy, blank,
+    )
+    to_b = call(
+        far_edge_kernel,
+        0.02,
+        shape((32 * count + 2 * count, 128), BF16),
+        [pltpu.VMEM((2 * count, 128), F32)],
+        features, bits, neighbours, edge_bits, blank,
+    )
+    face = shape((count // 2, 64, 128), BF16)
     to_a = call(near_edge_kernel, 0.02, face, [], features, bits, to_b)
-    from_a, from_b = exchange(to_a, to_b)
-    own_two, sides_two = call(
-        level_two_tables_kernel,
-        0.4,
-        (
-            shape((9 * 16 * count, 16 * count), BF16),
-            shape((2, 9 * 16 * count, 16 * count), BF16),
-        ),
-        [],
-        neighbours, level_two_picks(),
-    )
+    from_a, message = exchange(to_a, to_b)
     middle, taps, face_taps, reduce_taps, partial = call(
         outer_kernel,
         2.0,
@@ -683,29 +798,54 @@
         neighbours, bits, features, conv_one, first_reduce_kernel,
     )
     plane = shape((16 * count, 128), BF16)
-    planes = shape((2, 16 * count, 128), BF16)
+    rows = shape((count, 2, 64, 128), BF16)
     sums = pltpu.VMEM((count * 64, 128), F32)
+    inner, inner_two = call(
+        inner_kernel,
+        0.05,
+        (rows, shape((2, 16 * count, 128), BF16)),
+        [sums, sums],
+        middle, taps, partial, reduce_taps, pair_words, mask_two,
+    )
     outer, outer_two, to_b = call(
         faces_one_kernel,
         1.5,
-        (shape((count, 2, 64, 128), BF16), shape((2 * 16 * count, 128), BF16), plane),
+        (rows, shape((2 * 16 * count, 128), BF16), shape((3 * 16 * count, 128), BF16)),
         [
             pltpu.VMEM((count + 1, 64, 128), F32),
             pltpu.VMEM((count, 3, 6, 16, 128), BF16),
             sums,
             sums,
         ],
-        neighbours, from_a, from_b, face_taps, partial, reduce_taps, pair_words, mask_two,
+        neighbours, from_a, message, face_taps, partial, reduce_taps, pair_words, mask_two,
+        inner_two,
     )
     to_a = call(near_face_kernel, 0.02, plane, [], outer_two, to_b)
     from_a, from_b = exchange(to_a, to_b)
 
-    first_level, inner_two = call(
-        inner_kernel,
+    pick = level_two_picks()
+    table = shape((9 * 16 * count, 16 * count), BF16)
+    own_two, sides_two = call(
+        level_two_tables_kernel,
         0.05,
-        (shape(features.shape, BF16), planes),
-        [sums, sums],
-        middle, taps, partial, outer, reduce_taps, pair_words, mask_two,
+        (table, shape((2, 9 * 16 * count, 16 * count), BF16)),
+        [],
+        neighbours, pick, to_a,
+    )
+    far_two, toward_two, far_mask_two, far_mask_three = call(
+        far_tables_kernel,
+        0.05,
+        (table, table, shape((2 * 16 * count, 128), F32), shape((4 * count, 256), F32)),
+        [],
+        message, pick, to_a,
+    )
+    first_level = call(output_kernel, 0.05, shape(features.shape, BF16), [], outer, inner)
+    own_for_far = call(
+        own_for_far_kernel,
+        0.05,
+        shape((16 * count, 128), F32),
+        [],
+        toward_two, to_b, conv_two,
     )
     partial, first_level = call(
         own_two_kernel,
@@ -715,31 +855,30 @@
         outer_two, inner_two, own_two, sides_two, from_a, conv_two, first_level,
         store=(1,),
     )
+    own_three, near_three = call(
+        level_three_tables_kernel,
+        0.05,
+        (shape((27 * 8 * count, 12 * count), BF16), shape((9 * 4 * count, 4 * count), BF16)),
+        [],
+        neighbours, level_three_picks(), to_a,
+    )
     face = shape((4 * count, 256), BF16)
-    second_level, third, to_b = call(
+    second_level, third, far_third = call(
         faces_two_kernel,
-        0.9,
+        1.5,
         (shape((count, 64, 128), BF16), shape((8 * count, 256), BF16), face),
         [],
-        sides_two, child_rows(), partial, from_b, conv_two, second_reduce_kernel, mask_two,
-        mask_three,
-    )
-    to_a = call(near_face_kernel, 0.02, face, [], third, to_b)
-    from_a, from_b = exchange(to_a, to_b)
-
-    own_three, far_three = call(
-        level_three_tables_kernel,
-        0.02,
-        (shape((27 * 8 * count, 12 * count), BF16), shape((9 * 4 * count, 4 * count), BF16)),
-        [],
-        neighbours, level_three_picks(), third,
-    )
+        sides_two, far_two, child_rows(2), child_rows(1), partial, own_for_far, from_b, conv_two,
+        second_reduce_kernel, mask_two, mask_three, far_mask_two, far_mask_three,
+    )
+    to_a = call(near_face_kernel, 0.02, face, [], third, far_third)
+    from_a = lax.ppermute(to_a, axes, within)
     partial, second_level = call(
         own_three_kernel,
         1.0,
         (shape((8 * count, 256), F32), shape(second_level.shape, BF16)),
         [DMA(())],
-        own_three, third, from_a, conv_three, second_level,
+        own_three, third, far_third, conv_three, second_level,
         store=(1,),
     )
     third_level = call(
@@ -747,7 +886,7 @@
         1,
         shape((count, 8, 256), BF16),
         [],
-        far_three, partial, from_b, conv_three, mask_three,
+        near_three, partial, from_a, conv_three, mask_three,
     )
     return jnp.swapaxes(first_level, 1, 2), second_level, third_level
 

time: 18.6 us -> 18.3 us (0.984)
  Pallas kernels: 9.16 us -> 11 us
  starting transfers between devices: 6.88 us -> 5.34 us
  waiting for transfers between devices: 0.62 us -> 0.01 us
    pallas_call x14 -> x18, Pallas kernels: 9.16 us -> 11 us  [call(): pl.pallas_call(kernel, out_shape=out_shape, in_specs=[ANY if n in remain...]
    ppermute x3 -> x2, starting transfers between devices: 6.15 us -> 4.56 us  [exchange(): from_b = lax.ppermute(to_b, axes, across)]
    ppermute x3 -> x2, waiting for transfers between devices: 0.62 us -> 0.01 us  [exchange(): return (lax.ppermute(to_a, axes, within), from_b)]
    ppermute x0 -> x1, starting transfers between devices: none -> 0.43 us  [on_device(): from_a = lax.ppermute(to_a, axes, within)]
    ppermute x3 -> x2, starting transfers between devices: 0.73 us -> 0.35 us  [exchange(): return (lax.ppermute(to_a, axes, within), from_b)]
    unnamed x22 -> x24, local copies, waits for them, and re-layouts: 0.91 us -> 0.9 us
  transfers between devices with their start and end apart: 6 -> 5, of which waited for: 2 -> 0; matrix products, arithmetic and copies ran while one was open for 0% -> 0% of each run, Pallas kernels for 33% -> 39%
where the time goes in v4:
time: 18.3 us; the launch traced here: 18.1 us
  Pallas kernels  11 us (60%)
  starting transfers between devices  5.34 us (29%)
  between operations  0.91 us (5%)
  local copies, waits for them, and re-layouts  0.9 us (5%)
    pallas_call x18, Pallas kernels, call(): pl.pallas_call(kernel, out_shape=out_shape, in_specs=[ANY if n in remain...  11 us
    ppermute x2, starting transfers between devices, exchange(): from_b = lax.ppermute(to_b, axes, across)  4.56 us
    unnamed x24, local copies, waits for them, and re-layouts  0.9 us
    ppermute x1, starting transfers between devices, on_device(): from_a = lax.ppermute(to_a, axes, within)  0.43 us
  transfers between devices with their start and end apart: 5, of which 0 were waited for; matrix products, arithmetic and copies ran while one was open for 0% of the time, Pallas kernels for 39%

profile of v4, /device:TPU:0, one launch (start us, length us, event | category | flops | bytes accessed | tf_op | source)
XLA Modules:
  0.0 18.1 jit_solution(6377986776343606129)
XLA Ops:
  0.6 0.0 copy-start.6
  0.6 0.0 copy-start.2
  0.7 0.0 copy-start.7
  0.7 0.0 copy-start.4
  0.7 0.0 copy-start.5
  0.7 0.6 %copy-done.6 = s32[8,16]{1,0:T(8,128)S(1)} copy-done((s32[8,16]{1,0:T(8,128)S(1)}, s32[8,16]{1,0:T(8,128)}, u32[]{:S(2)}) %copy-start.6) | copy-done | bytes 536
  1.3 0.1 shard_map.140
  1.5 0.2 %copy-done.2 = bf16[8,512,64]{1,2,0:T(8,128)(2,1)S(1)} copy-done((bf16[8,512,64]{1,2,0:T(8,128)(2,1)S(1)}, bf16[8,512,64]{1,2,0:T(8,128)(2,1)}, u32[]{:S(2)}) %copy-start.2) | copy-done | bytes 524312
  1.7 0.0 copy-done.7
  1.7 0.1 shard_map.141.earlier
  1.8 3.0 %collective-permute-start.1 = (bf16[272,128]{1,0:T(8,128)(2,1)S(1)}, bf16[272,128]{1,0:T(8,128)(2,1)S(1)}, u32[]{:S(2)}, u32[]{:S(2)}) collective-permute-start(bf16[272,128]{1,0:T(8,128)(2,1)S(1)} %shard_map.141.earlier), channel_id=1, source_target_pairs={{0,16},{1,2},{2,1},{3,4},{4,3},{5,6},{6,5},{7,8},{8,7},{9,10},{10,... | collective-permute-start | bytes 208904 | tf_op jit(solution)/shard_map/ppermute | solution.py:756
  4.8 0.1 shard_map.142
  4.9 0.2 %collective-permute-start = (bf16[4,64,128]{2,1,0:T(8,128)(2,1)S(1)}, bf16[4,64,128]{2,1,0:T(8,128)(2,1)S(1)}, u32[]{:S(2)}, u32[]{:S(2)}) collective-permute-start(bf16[4,64,128]{2,1,0:T(8,128)(2,1)S(1)} %shard_map.142), channel_id=1, source_target_pairs={{0,1},{1,0},{2,3},{3,2},{4,5},{5,4},{6,7},{7,6},{8,9},{9,8},{10,11... | collective-permute-start | bytes 196616 | tf_op jit(solution)/shard_map/ppermute | solution.py:757
  5.1 0.0 copy-done.4
  5.1 0.0 copy-done.5
  5.1 1.9 %shard_map.143 = (bf16[8,3,6,16,128]{4,3,2,1,0:T(8,128)(2,1)S(1)}, bf16[1152,256]{1,0:T(8,128)(2,1)S(1)}, bf16[1152,128]{1,0:T(8,128)(2,1)S(1)}, bf16[256,256]{1,0:T(8,128)(2,1)S(1)}, f32[4,512,128]{2,1,0:T(8,128)S(1)}) custom-call(s32[8,27]{1,0:T(8,128)S(1)} %copy-done.7, f32[4,8,128]{2,1,0:T(8,128)S(1)} %get-tuple-element.33.bits, ...), custom_call_target="tpu_custom_call" | custom-call | flops 20000000000 | bytes 10000000 | tf_op jit(solution)/shard_map/pallas_call | solution.py:712
  7.0 0.8 %shard_map.144 = (bf16[8,2,64,128]{3,2,1,0:T(8,128)(2,1)S(1)}, bf16[2,128,128]{2,1,0:T(8,128)(2,1)S(1)}) custom-call(bf16[8,3,6,16,128]{4,3,2,1,0:T(8,128)(2,1)S(1)} %get-tuple-element.40.middle, bf16[1152,256]{1,0:T(8,128)(2,1)S(1)} %get-tuple-element.41.taps, f32[4,512,128]{2,1,0:T(8,128)S(1)} %get-tuple-element.36.partial, ...), custom_call_target="tpu_custom_call" | custom-call | flops 500000000 | bytes 10000000 | tf_op jit(solution)/shard_map/pallas_call | solution.py:712
  7.8 0.0 collective-permute-done.from_a
  7.8 0.0 collective-permute-done.1.from_b.message
  7.8 0.0 copy-start.8
  7.8 0.0 copy-start.9
  7.8 0.9 %shard_map.145 = (bf16[8,2,64,128]{3,2,1,0:T(8,128)(2,1)S(1)}, bf16[256,128]{1,0:T(8,128)(2,1)S(1)}, bf16[384,128]{1,0:T(8,128)(2,1)S(1)}) custom-call(s32[8,27]{1,0:T(8,128)S(1)} %copy-done.7, bf16[4,64,128]{2,1,0:T(8,128)(2,1)S(1)} %collective-permute-done.from_a, bf16[272,128]{1,0:T(8,128)(2,1)S(1)} %collective-permute-done.1.from_b.message, ...), custom_call_target="tpu_custom_call" | custom-call | flops 15000000512 | bytes 10000000 | tf_op jit(solution)/shard_map/pallas_call | solution.py:712
  8.8 0.0 copy-start.1
  8.8 1.6 %collective-permute-start.3 = (bf16[384,128]{1,0:T(8,128)(2,1)S(1)}, bf16[384,128]{1,0:T(8,128)(2,1)S(1)}, u32[]{:S(2)}, u32[]{:S(2)}) collective-permute-start(bf16[384,128]{1,0:T(8,128)(2,1)S(1)} %get-tuple-element.44.earlier.to_b), channel_id=1, source_target_pairs={{0,16},{1,2},{2,1},{3,4},{4,3},{5,6},{6,5},{7,8},{8,7},{9,10},{10,... | collective-permute-start | bytes 294920 | tf_op jit(solution)/shard_map/ppermute | solution.py:756
  10.4 0.1 collective-permute-start.2
  10.5 0.0 copy-done.8
  10.5 0.4 %shard_map.147 = (bf16[1152,128]{1,0:T(8,128)(2,1)S(1)}, bf16[2,1152,128]{2,1,0:T(8,128)(2,1)S(1)}) custom-call(s32[8,27]{1,0:T(8,128)S(1)} %copy-done.7, bf16[432,27]{1,0:T(8,128)(2,1)S(1)} %copy-done.8, bf16[128,128]{1,0:T(8,128)(2,1)S(1)} %shard_map.146.later), custom_call_target="tpu_custom_call" | custom-call | flops 500000000 | bytes 10000000 | tf_op jit(solution)/shard_map/pallas_call | solution.py:712
  10.9 0.0 copy-done.9
  10.9 0.4 %shard_map.150 = (bf16[1728,96]{1,0:T(8,128)(2,1)S(1)}, bf16[288,32]{1,0:T(8,128)(2,1)S(1)}) custom-call(s32[8,27]{1,0:T(8,128)S(1)} %copy-done.7, bf16[432,27]{1,0:T(8,128)(2,1)S(1)} %copy-done.9, bf16[128,128]{1,0:T(8,128)(2,1)S(1)} %shard_map.146.later), custom_call_target="tpu_custom_call" | custom-call | flops 500000000 | bytes 10000000 | tf_op jit(solution)/shard_map/pallas_call | solution.py:712
  11.3 0.4 %shard_map.151 = (bf16[1152,128]{1,0:T(8,128)(2,1)S(1)}, bf16[1152,128]{1,0:T(8,128)(2,1)S(1)}, f32[256,128]{1,0:T(8,128)S(1)}, f32[32,256]{1,0:T(8,128)S(1)}) custom-call(bf16[272,128]{1,0:T(8,128)(2,1)S(1)} %collective-permute-done.1.from_b.message, bf16[432,27]{1,0:T(8,128)(2,1)S(1)} %copy-done.8, bf16[128,128]{1,0:T(8,128)(2,1)S(1)} %shard_map.146.later), custom_call_target="tpu_custom_call" | custom-call | flops 500000000 | bytes 10000000 | tf_op jit(solution)/shard_map/pallas_call | solution.py:712
  11.7 0.0 copy-done.1
  11.7 0.4 %shard_map.152.own_for_far = f32[128,128]{1,0:T(8,128)S(1)} custom-call(bf16[1152,128]{1,0:T(8,128)(2,1)S(1)} %get-tuple-element.53.gather, bf16[384,128]{1,0:T(8,128)(2,1)S(1)} %get-tuple-element.44.earlier.to_b, bf16[27,128,128]{2,1,0:T(8,128)(2,1)S(1)} %copy-done.1), custom_call_target="tpu_custom_call" | custom-call | flops 500000000 | bytes 10000000 | tf_op jit(solution)/shard_map/pallas_call | solution.py:712
  12.1 0.5 %shard_map.148.first = bf16[8,64,512]{2,1,0:T(8,128)(2,1)S(1)} custom-call(bf16[8,2,64,128]{3,2,1,0:T(8,128)(2,1)S(1)} %get-tuple-element.47.outer, bf16[8,2,64,128]{3,2,1,0:T(8,128)(2,1)S(1)} %get-tuple-element.48.inner), custom_call_target="tpu_custom_call" | custom-call | flops 500000000 | bytes 10000000 | tf_op jit(solution)/shard_map/pallas_call | solution.py:712
  12.6 0.0 collective-permute-done.2.from_a
  12.6 0.0 copy-start.3
  12.6 0.0 copy-start.10
  12.6 0.0 copy-start.11
  12.7 1.2 %shard_map.149 = (f32[512,128]{1,0:T(8,128)S(1)}, bf16[8,64,512]{2,1,0:T(8,128)(2,1)}) custom-call(bf16[256,128]{1,0:T(8,128)(2,1)S(1)} %get-tuple-element.43.planes.outer, bf16[2,128,128]{2,1,0:T(8,128)(2,1)S(1)} %get-tuple-element.42.inner, bf16[1152,128]{1,0:T(8,128)(2,1)S(1)} %get-tuple-element.45.own_gather, ...), custom_call_target="tpu_custom_call" | custom-call | flops 10000000000 | bytes 10000000 | tf_op jit(solution)/shard_map/pallas_call | solution.py:712
  13.9 0.0 collective-permute-done.3.from_b
  13.9 0.0 copy-done.3
  13.9 0.0 copy-done.10
  13.9 0.0 copy-done.11
  13.9 0.0 copy-start
  13.9 1.6 %shard_map.153 = (bf16[8,64,128]{2,1,0:T(8,128)(2,1)S(1)}, bf16[64,256]{1,0:T(8,128)(2,1)S(1)}, bf16[32,256]{1,0:T(8,128)(2,1)S(1)}) custom-call(bf16[2,1152,128]{2,1,0:T(8,128)(2,1)S(1)} %get-tuple-element.46.gathers, bf16[1152,128]{1,0:T(8,128)(2,1)S(1)} %get-tuple-element.51.far_gather, bf16[128,128]{1,0:T(8,128)(2,1)S(1)} %copy-done.10, ...), custom_call_target="tpu_custom_call" | custom-call | flops 15000000512 | bytes 10000000 | tf_op jit(solution)/shard_map/pallas_call | solution.py:712
  15.5 0.4 %collective-permute-start.4 = (bf16[32,256]{1,0:T(8,128)(2,1)S(1)}, bf16[32,256]{1,0:T(8,128)(2,1)S(1)}, u32[]{:S(2)}, u32[]{:S(2)}) collective-permute-start(bf16[32,256]{1,0:T(8,128)(2,1)S(1)} %shard_map.155), channel_id=1, source_target_pairs={{0,1},{1,0},{2,3},{3,2},{4,5},{5,4},{6,7},{7,6},{8,9},{9,8},{10,11... | collective-permute-start | bytes 49160 | tf_op jit(solution)/shard_map/ppermute | solution.py:875
  16.0 1.1 %shard_map.154 = (f32[64,256]{1,0:T(8,128)S(1)}, bf16[8,64,128]{2,1,0:T(8,128)(2,1)}) custom-call(bf16[1728,96]{1,0:T(8,128)(2,1)S(1)} %get-tuple-element.50.gather, bf16[64,256]{1,0:T(8,128)(2,1)S(1)} %get-tuple-element.57.third.planes, bf16[32,256]{1,0:T(8,128)(2,1)S(1)} %get-tuple-element.58.far.earlier, bf16[27,256,256]{2,1,0:T(8,128)(2,1)S(1)} %copy-done, ...), custom_call_target="tpu_custom_call" | custom-call | flops 10000000000 | bytes 10000000 | tf_op jit(solution)/shard_map/pallas_call | solution.py:712
  17.0 0.0 collective-permute-done.4.from_a
  17.1 1.1 %shard_map.156 = bf16[8,8,256]{2,1,0:T(8,128)(2,1)} custom-call(bf16[288,32]{1,0:T(8,128)(2,1)S(1)} %get-tuple-element.61.gather, f32[64,256]{1,0:T(8,128)S(1)} %get-tuple-element.62.partial, bf16[32,256]{1,0:T(8,128)(2,1)S(1)} %collective-permute-done.4.from_a, bf16[27,256,256]{2,1,0:T(8,128)(2,1)S(1)} %copy-done, f32[64,256]{1,0:T(8,128)S(1)} %get-tuple-element.54.mask_three), custom_call_target="tpu_custom_call" | custom-call | flops 10000000000 | bytes 10000000 | tf_op jit(solution)/shard_map/pallas_call | solution.py:712
  (4 shorter events, 0.0 us)
Async XLA Ops:
  0.6 0.7 %copy-start.6 = (s32[8,16]{1,0:T(8,128)S(1)}, s32[8,16]{1,0:T(8,128)}, u32[]{:S(2)}) copy-start(s32[8,16]{1,0:T(8,128)} %occupancy.1) | copy-start | bytes 1540
  0.6 1.0 %copy-start.2 = (bf16[8,512,64]{1,2,0:T(8,128)(2,1)S(1)}, bf16[8,512,64]{1,2,0:T(8,128)(2,1)}, u32[]{:S(2)}) copy-start(bf16[8,512,64]{1,2,0:T(8,128)(2,1)} %param.12) | copy-start | bytes 1572868
  0.7 1.0 %copy-start.7 = (s32[8,27]{1,0:T(8,128)S(1)}, s32[8,27]{1,0:T(8,128)}, u32[]{:S(2)}) copy-start(s32[8,27]{1,0:T(8,128)} %neighbours.9) | copy-start | bytes 2596
  0.7 4.5 %copy-start.4 = (bf16[27,64,64]{2,1,0:T(8,128)(2,1)S(1)}, bf16[27,64,64]{2,1,0:T(8,128)(2,1)}, u32[]{:S(2)}) copy-start(bf16[27,64,64]{2,1,0:T(8,128)(2,1)} %kernel.6) | copy-start | bytes 663556
  0.7 4.5 %copy-start.5 = (bf16[8,64,128]{2,1,0:T(8,128)(2,1)S(1)}, bf16[8,64,128]{2,1,0:T(8,128)(2,1)}, u32[]{:S(2)}) copy-start(bf16[8,64,128]{2,1,0:T(8,128)(2,1)} %reduce.2) | copy-start | bytes 393220
  1.8 6.0 %collective-permute-start.1 = (bf16[272,128]{1,0:T(8,128)(2,1)S(1)}, bf16[272,128]{1,0:T(8,128)(2,1)S(1)}, u32[]{:S(2)}, u32[]{:S(2)}) collective-permute-start(bf16[272,128]{1,0:T(8,128)(2,1)S(1)} %shard_map.141.earlier), channel_id=1, source_target_pairs={{0,16},{1,2},{2,1},{3,4},{4,3},{5,6},{6,5},{7,8},{8,7},{9,10},{10,... | collective-permute-start | bytes 208904 | tf_op jit(solution)/shard_map/ppermute | solution.py:756
  4.9 2.9 %collective-permute-start = (bf16[4,64,128]{2,1,0:T(8,128)(2,1)S(1)}, bf16[4,64,128]{2,1,0:T(8,128)(2,1)S(1)}, u32[]{:S(2)}, u32[]{:S(2)}) collective-permute-start(bf16[4,64,128]{2,1,0:T(8,128)(2,1)S(1)} %shard_map.142), channel_id=1, source_target_pairs={{0,1},{1,0},{2,3},{3,2},{4,5},{5,4},{6,7},{7,6},{8,9},{9,8},{10,11... | collective-permute-start | bytes 196616 | tf_op jit(solution)/shard_map/ppermute | solution.py:757
  7.8 2.7 %copy-start.8 = (bf16[432,27]{1,0:T(8,128)(2,1)S(1)}, bf16[432,27]{1,0:T(8,128)(2,1)}, u32[]{:S(2)}) copy-start(bf16[432,27]{1,0:T(8,128)(2,1)} %constant.8.clone.pick) | copy-start | bytes 69988
  7.8 3.1 %copy-start.9 = (bf16[432,27]{1,0:T(8,128)(2,1)S(1)}, bf16[432,27]{1,0:T(8,128)(2,1)}, u32[]{:S(2)}) copy-start(bf16[432,27]{1,0:T(8,128)(2,1)} %constant.9.clone.pick) | copy-start | bytes 69988
  8.8 2.9 %copy-start.1 = (bf16[27,128,128]{2,1,0:T(8,128)(2,1)S(1)}, bf16[27,128,128]{2,1,0:T(8,128)(2,1)}, u32[]{:S(2)}) copy-start(bf16[27,128,128]{2,1,0:T(8,128)(2,1)} %kernel.9) | copy-start | bytes 2654212
  8.8 5.1 %collective-permute-start.3 = (bf16[384,128]{1,0:T(8,128)(2,1)S(1)}, bf16[384,128]{1,0:T(8,128)(2,1)S(1)}, u32[]{:S(2)}, u32[]{:S(2)}) collective-permute-start(bf16[384,128]{1,0:T(8,128)(2,1)S(1)} %get-tuple-element.44.earlier.to_b), channel_id=1, source_target_pairs={{0,16},{1,2},{2,1},{3,4},{4,3},{5,6},{6,5},{7,8},{8,7},{9,10},{10,... | collective-permute-start | bytes 294920 | tf_op jit(solution)/shard_map/ppermute | solution.py:756
  10.4 2.3 %collective-permute-start.2 = (bf16[128,128]{1,0:T(8,128)(2,1)S(1)}, bf16[128,128]{1,0:T(8,128)(2,1)S(1)}, u32[]{:S(2)}, u32[]{:S(2)}) collective-permute-start(bf16[128,128]{1,0:T(8,128)(2,1)S(1)} %shard_map.146.later), channel_id=1, source_target_pairs={{0,1},{1,0},{2,3},{3,2},{4,5},{5,4},{6,7},{7,6},{8,9},{9,8},{10,11... | collective-permute-start | bytes 98312 | tf_op jit(solution)/shard_map/ppermute | solution.py:757
  12.6 1.3 %copy-start.3 = (bf16[8,128,256]{2,1,0:T(8,128)(2,1)S(1)}, bf16[8,128,256]{2,1,0:T(8,128)(2,1)}, u32[]{:S(2)}) copy-start(bf16[8,128,256]{2,1,0:T(8,128)(2,1)} %reduce.3) | copy-start | bytes 1572868
  12.6 1.3 %copy-start.10 = (bf16[128,128]{1,0:T(8,128)(2,1)S(1)}, bf16[128,128]{1,0:T(8,128)(2,1)}, u32[]{:S(2)}) copy-start(bf16[128,128]{1,0:T(8,128)(2,1)} %constant.10.clone.children) | copy-start | bytes 98308
  12.6 1.3 %copy-start.11 = (bf16[64,64]{1,0:T(8,128)(2,1)S(1)}, bf16[64,64]{1,0:T(8,128)(2,1)}, u32[]{:S(2)}) copy-start(bf16[64,64]{1,0:T(8,128)(2,1)} %constant.11.clone.far_children) | copy-start | bytes 24580
  13.9 2.0 %copy-start = (bf16[27,256,256]{2,1,0:T(8,128)(2,1)S(1)}, bf16[27,256,256]{2,1,0:T(8,128)(2,1)}, u32[]{:S(2)}) copy-start(bf16[27,256,256]{2,1,0:T(8,128)(2,1)} %kernel.11) | copy-start | bytes 10616836
  15.5 1.5 %collective-permute-start.4 = (bf16[32,256]{1,0:T(8,128)(2,1)S(1)}, bf16[32,256]{1,0:T(8,128)(2,1)S(1)}, u32[]{:S(2)}, u32[]{:S(2)}) collective-permute-start(bf16[32,256]{1,0:T(8,128)(2,1)S(1)} %shard_map.155), channel_id=1, source_target_pairs={{0,1},{1,0},{2,3},{3,2},{4,5},{5,4},{6,7},{7,6},{8,9},{9,8},{10,11... | collective-permute-start | bytes 49160 | tf_op jit(solution)/shard_map/ppermute | solution.py:875

commit v5 on v4

--- a/solution.py
+++ b/solution.py
@@ -120,20 +120,19 @@
 
 def edge_planes(features, bits, low_wanted):
     last = features.shape[2] - 128
-    lane = iota((64, 128), 1)
     planes = []
     for q in range(features.shape[0] // 2):
         low, high = [
             [
-                features[b, :, column * last : column * last + 128].astype(F32)
-                * bits[3 * column, b : b + 1]
+                features[b, :, column * last : column * last + 128]
+                * bits[3 * column, b : b + 1].astype(BF16)
                 for b in (2 * q, 2 * q + 1)
             ]
             for column in range(2)
         ]
-        lows = jnp.where(lane < 64, low[0], pltpu.roll(low[1], 64, 1))
-        highs = jnp.where(lane < 64, pltpu.roll(high[0], 64, 1), high[1])
-        planes.append(jnp.where(low_wanted, lows, highs).astype(BF16))
+        lows = beside([low[0][:, :64], low[1][:, :64]])
+        highs = beside([high[0][:, 64:], high[1][:, 64:]])
+        planes.append(jnp.where(low_wanted, lows, highs))
     return planes
 
 
@@ -198,8 +197,8 @@
     )
 
 
-def far_tables_kernel(message, pick, later, own_two, toward_two, mask_two, mask_three):
-    count = own_two.shape[1] // 16
+def far_tables_kernel(message, pick, later, gather, mask_two, mask_three):
+    count = gather.shape[1] // 32
     notes = message[32 * count :, :].astype(F32)
     slots = slot_rows(notes[:count, : pick.shape[1]])
     begin = pl.multiple_of(jnp.where(on_odd_place(), 0, 288), 16)
@@ -209,7 +208,8 @@
             times_transposed(pick[144:288, :], slots),
         ]
     )
-    fill_level_two_tables((toward_two, own_two), rows, count)
+    width = 16 * count
+    fill_level_two_tables((gather.at[:, width:], gather.at[:, :width]), rows, count)
 
     every = jnp.ones((128, 256), BF16)
     lane = iota((16, 128), 1)
@@ -298,21 +298,20 @@
     tables, windows, wrap_taps,
 ):
     count = features.shape[0]
-    lane = iota((64, 128), 1)
     row = iota((8, 128), 0)
     numbers = slot_numbers(neighbours)
 
-    none = jnp.zeros((64, 64), F32)
+    none = jnp.zeros((64, 64), BF16)
     for q in range(9):
-        w = [kernel[9 * a + q].astype(F32) for a in range(3)]
+        w = [kernel[9 * a + q] for a in range(3)]
         rows = slice(q * 128, (q + 1) * 128)
         taps[rows, :] = stack(
             [beside([w[2], w[1], w[0], none]), beside([none, w[2], w[1], w[0]])]
-        ).astype(BF16)
+        )
         wrap_taps[rows, :] = stack(
             [beside([w[2], w[1], none, none]), beside([none, none, w[1], w[0]])]
-        ).astype(BF16)
-        face_taps[rows, :] = stack([beside([w[0], none]), beside([none, w[2]])]).astype(BF16)
+        )
+        face_taps[rows, :] = stack([beside([w[0], none]), beside([none, w[2]])])
 
     reduce_taps[...] = stack(
         [
@@ -326,19 +325,18 @@
         tables[pair, count] = jnp.zeros((64, 128), F32)
     for b in range(count):
         cols = [
-            features[b, :, 128 * q : 128 * (q + 1)].astype(F32) * bits[q, b : b + 1]
+            features[b, :, 128 * q : 128 * (q + 1)] * bits[q, b : b + 1].astype(BF16)
             for q in range(4)
         ]
-        rolled = [pltpu.roll(col, 64, 1) for col in cols]
         for p in (0, 2):
             m = stack(
                 [
-                    jnp.where(lane < 64, rolled[p], cols[p + 1]),
-                    jnp.where(lane < 64, cols[p + 1], rolled[(p + 2) % 4]),
+                    beside([cols[p][:, 64:], cols[p + 1][:, 64:]]),
+                    beside([cols[p + 1][:, :64], cols[(p + 2) % 4][:, :64]]),
                 ]
             ).T
-            tables[p, b] = m[:64]
-            tables[p + 1, b] = m[64:]
+            tables[p, b] = m[:64].astype(F32)
+            tables[p + 1, b] = m[64:].astype(F32)
 
     for b in range(count):
         slot = [numbers[b, 9 + q] for q in range(9)]
@@ -413,10 +411,10 @@
     slot = slot_numbers(neighbours)
     halo[count] = jnp.zeros((64, 128), F32)
     for q in range(count // 2):
-        one, two = from_a[q].astype(F32), from_b[64 * q : 64 * (q + 1), :].astype(F32)
+        one, two = from_a[q], from_b[64 * q : 64 * (q + 1), :]
         m = stack([jnp.where(odd, one, two), jnp.where(odd, two, one)]).T
-        halo[2 * q] = m[:64]
-        halo[2 * q + 1] = m[64:]
+        halo[2 * q] = m[:64].astype(F32)
+        halo[2 * q + 1] = m[64:].astype(F32)
     for b in range(count):
         low = [slot[b, q] for q in range(9)]
         high = [slot[b, 18 + q] for q in range(9)]
@@ -495,18 +493,13 @@
 
 
 def output_kernel(outer, inner, out):
-    lane = iota((64, 128), 1)
     for b in range(outer.shape[0]):
         ordered = [outer[b, 0], inner[b, 0], inner[b, 1], outer[b, 1]]
         for i in (0, 2):
-            m = stack(ordered[i : i + 2]).astype(F32).T
+            m = stack(ordered[i : i + 2]).T
             top, bottom = m[:64], m[64:]
-            out[b, :, 128 * i : 128 * (i + 1)] = jnp.where(
-                lane < 64, top, pltpu.roll(bottom, 64, 1)
-            ).astype(BF16)
-            out[b, :, 128 * (i + 1) : 128 * (i + 2)] = jnp.where(
-                lane < 64, pltpu.roll(top, 64, 1), bottom
-            ).astype(BF16)
+            out[b, :, 128 * i : 128 * (i + 1)] = beside([top[:, :64], bottom[:, :64]])
+            out[b, :, 128 * (i + 1) : 128 * (i + 2)] = beside([top[:, 64:], bottom[:, 64:]])
 
 
 def face_part(gather, face, kernel, high):
@@ -554,11 +547,6 @@
     copy.wait()
 
 
-def own_for_far_kernel(gather, to_b, kernel, part):
-    rows = part.shape[0]
-    part[...] = face_part(gather[...], to_b[:rows], kernel, jnp.where(on_odd_place(), 0, 1))
-
-
 def child_columns(picked, pairs, planes):
     return beside(
         [
@@ -575,7 +563,7 @@
 
 
 def faces_two_kernel(
-    gathers, far_gather, children, far_children, partial, own_for_far, from_b, kernel, reduce,
+    gathers, far_gather, children, far_children, partial, to_b, from_b, kernel, reduce,
     mask_two, mask_three, far_mask_two, far_mask_three,
     second, third, far_third,
 ):
@@ -599,20 +587,23 @@
         children[...], beside([stack(bricks[b : b + 2]) for b in range(0, count, 2)])
     )
 
+    none = jnp.zeros((rows, 128), BF16)
+    planes = [from_b[d * rows : (d + 1) * rows] for d in range(3)]
     moved = dot(
-        far_gather[...], beside([from_b[d * rows : (d + 1) * rows] for d in range(3)])
+        far_gather[...],
+        stack([beside(planes + [none]), beside([none, none, none, to_b[:rows]])]),
     ).astype(BF16)
     left = [
         beside([moved[q * rows : (q + 1) * rows, 128 * d : 128 * (d + 1)] for q in range(9)])
-        for d in range(3)
+        for d in range(4)
     ]
     toward, same, away = [
         kernel[pl.ds(begin, 9)].reshape(9 * 128, 128) for begin in (18 - 18 * high, 9, 18 * high)
     ]
-    zero = dot(left[0], beside([same, toward]))
+    zero = dot(stack([left[0], left[3]]), beside([same, toward]))
     one = dot(left[1], beside([away, same]))
-    near = own_for_far[...] + zero[:, :128] + one[:, :128]
-    past = zero[:, 128:] + one[:, 128:] + dot(left[2], away)
+    near = zero[rows:, 128:] + zero[:rows, :128] + one[:, :128]
+    past = zero[:rows, 128:] + one[:, 128:] + dot(left[2], away)
     far_planes = [
         (jnp.maximum(sums, 0.0) * far_mask_two[n * rows : (n + 1) * rows]).astype(BF16)
         for n, sums in enumerate((jnp.where(odd, near, past), jnp.where(odd, past, near)))
@@ -832,21 +823,18 @@
         [],
         neighbours, pick, to_a,
     )
-    far_two, toward_two, far_mask_two, far_mask_three = call(
+    far_two, far_mask_two, far_mask_three = call(
         far_tables_kernel,
         0.05,
-        (table, table, shape((2 * 16 * count, 128), F32), shape((4 * count, 256), F32)),
+        (
+            shape((9 * 16 * count, 32 * count), BF16),
+            shape((2 * 16 * count, 128), F32),
+            shape((4 * count, 256), F32),
+        ),
         [],
         message, pick, to_a,
     )
     first_level = call(output_kernel, 0.05, shape(features.shape, BF16), [], outer, inner)
-    own_for_far = call(
-        own_for_far_kernel,
-        0.05,
-        shape((16 * count, 128), F32),
-        [],
-        toward_two, to_b, conv_two,
-    )
     partial, first_level = call(
         own_two_kernel,
         1.0,
@@ -868,7 +856,7 @@
         1.5,
         (shape((count, 64, 128), BF16), shape((8 * count, 256), BF16), face),
         [],
-        sides_two, far_two, child_rows(2), child_rows(1), partial, own_for_far, from_b, conv_two,
+        sides_two, far_two, child_rows(2), child_rows(1), partial, to_b, from_b, conv_two,
         second_reduce_kernel, mask_two, mask_three, far_mask_two, far_mask_three,
     )
     to_a = call(near_face_kernel, 0.02, face, [], third, far_third)

time: 18.3 us -> 17.7 us (0.967)
  Pallas kernels: 11 us -> 10.4 us
    pallas_call x18 -> x17, Pallas kernels: 11 us -> 10.4 us  [call(): pl.pallas_call(kernel, out_shape=out_shape, in_specs=[ANY if n in remain...]
  transfers between devices with their start and end apart: 5 -> 5, of which waited for: 0 -> 1; matrix products, arithmetic and copies ran while one was open for 0% -> 0% of each run, Pallas kernels for 39% -> 36%
where the time goes in v5:
time: 17.7 us; the launch traced here: 17.6 us
  Pallas kernels  10.4 us (59%)
  starting transfers between devices  5.29 us (30%)
  local copies, waits for them, and re-layouts  0.9 us (5%)
  between operations  0.87 us (5%)
    pallas_call x17, Pallas kernels, call(): pl.pallas_call(kernel, out_shape=out_shape, in_specs=[ANY if n in remain...  10.4 us
    ppermute x2, starting transfers between devices, exchange(): from_b = lax.ppermute(to_b, axes, across)  4.59 us
    unnamed x24, local copies, waits for them, and re-layouts  0.9 us
    ppermute x1, starting transfers between devices, on_device(): from_a = lax.ppermute(to_a, axes, within)  0.38 us
  transfers between devices with their start and end apart: 5, of which 1 were waited for; matrix products, arithmetic and copies ran while one was open for 0% of the time, Pallas kernels for 36%

profile of v5, /device:TPU:0, one launch (start us, length us, event | category | flops | bytes accessed | tf_op | source)
XLA Modules:
  0.0 17.6 jit_solution(3959447466780524036)
XLA Ops:
  0.6 0.0 copy-start.6
  0.6 0.0 copy-start.2
  0.7 0.0 copy-start.7
  0.7 0.0 copy-start.4
  0.7 0.0 copy-start.5
  0.7 0.6 %copy-done.6 = s32[8,16]{1,0:T(8,128)S(1)} copy-done((s32[8,16]{1,0:T(8,128)S(1)}, s32[8,16]{1,0:T(8,128)}, u32[]{:S(2)}) %copy-start.6) | copy-done | bytes 536
  1.3 0.1 shard_map.140
  1.5 0.2 %copy-done.2 = bf16[8,512,64]{1,2,0:T(8,128)(2,1)S(1)} copy-done((bf16[8,512,64]{1,2,0:T(8,128)(2,1)S(1)}, bf16[8,512,64]{1,2,0:T(8,128)(2,1)}, u32[]{:S(2)}) %copy-start.2) | copy-done | bytes 524312
  1.7 0.0 copy-done.7
  1.7 0.1 shard_map.141.earlier
  1.8 3.0 %collective-permute-start.1 = (bf16[272,128]{1,0:T(8,128)(2,1)S(1)}, bf16[272,128]{1,0:T(8,128)(2,1)S(1)}, u32[]{:S(2)}, u32[]{:S(2)}) collective-permute-start(bf16[272,128]{1,0:T(8,128)(2,1)S(1)} %shard_map.141.earlier), channel_id=1, source_target_pairs={{0,16},{1,2},{2,1},{3,4},{4,3},{5,6},{6,5},{7,8},{8,7},{9,10},{10,... | collective-permute-start | bytes 208904 | tf_op jit(solution)/shard_map/ppermute | solution.py:747
  4.8 0.1 shard_map.142
  4.9 0.2 %collective-permute-start = (bf16[4,64,128]{2,1,0:T(8,128)(2,1)S(1)}, bf16[4,64,128]{2,1,0:T(8,128)(2,1)S(1)}, u32[]{:S(2)}, u32[]{:S(2)}) collective-permute-start(bf16[4,64,128]{2,1,0:T(8,128)(2,1)S(1)} %shard_map.142), channel_id=1, source_target_pairs={{0,1},{1,0},{2,3},{3,2},{4,5},{5,4},{6,7},{7,6},{8,9},{9,8},{10,11... | collective-permute-start | bytes 196616 | tf_op jit(solution)/shard_map/ppermute | solution.py:748
  5.1 0.0 copy-done.4
  5.1 0.0 copy-done.5
  5.1 1.6 %shard_map.143 = (bf16[8,3,6,16,128]{4,3,2,1,0:T(8,128)(2,1)S(1)}, bf16[1152,256]{1,0:T(8,128)(2,1)S(1)}, bf16[1152,128]{1,0:T(8,128)(2,1)S(1)}, bf16[256,256]{1,0:T(8,128)(2,1)S(1)}, f32[4,512,128]{2,1,0:T(8,128)S(1)}) custom-call(s32[8,27]{1,0:T(8,128)S(1)} %copy-done.7, f32[4,8,128]{2,1,0:T(8,128)S(1)} %get-tuple-element.32.bits, ...), custom_call_target="tpu_custom_call" | custom-call | flops 20000000000 | bytes 10000000 | tf_op jit(solution)/shard_map/pallas_call | solution.py:703
  6.8 0.8 %shard_map.144 = (bf16[8,2,64,128]{3,2,1,0:T(8,128)(2,1)S(1)}, bf16[2,128,128]{2,1,0:T(8,128)(2,1)S(1)}) custom-call(bf16[8,3,6,16,128]{4,3,2,1,0:T(8,128)(2,1)S(1)} %get-tuple-element.39.middle, bf16[1152,256]{1,0:T(8,128)(2,1)S(1)} %get-tuple-element.40.taps, f32[4,512,128]{2,1,0:T(8,128)S(1)} %get-tuple-element.35.partial, ...), custom_call_target="tpu_custom_call" | custom-call | flops 500000000 | bytes 10000000 | tf_op jit(solution)/shard_map/pallas_call | solution.py:703
  7.5 0.0 collective-permute-done.from_a
  7.6 0.0 collective-permute-done.1.from_b.message
  7.6 0.0 copy-start.8
  7.6 0.0 copy-start.9
  7.6 0.9 %shard_map.145 = (bf16[8,2,64,128]{3,2,1,0:T(8,128)(2,1)S(1)}, bf16[256,128]{1,0:T(8,128)(2,1)S(1)}, bf16[384,128]{1,0:T(8,128)(2,1)S(1)}) custom-call(s32[8,27]{1,0:T(8,128)S(1)} %copy-done.7, bf16[4,64,128]{2,1,0:T(8,128)(2,1)S(1)} %collective-permute-done.from_a, bf16[272,128]{1,0:T(8,128)(2,1)S(1)} %collective-permute-done.1.from_b.message, ...), custom_call_target="tpu_custom_call" | custom-call | flops 15000000512 | bytes 10000000 | tf_op jit(solution)/shard_map/pallas_call | solution.py:703
  8.5 1.6 %collective-permute-start.3 = (bf16[384,128]{1,0:T(8,128)(2,1)S(1)}, bf16[384,128]{1,0:T(8,128)(2,1)S(1)}, u32[]{:S(2)}, u32[]{:S(2)}) collective-permute-start(bf16[384,128]{1,0:T(8,128)(2,1)S(1)} %get-tuple-element.43.earlier.to_b), channel_id=1, source_target_pairs={{0,16},{1,2},{2,1},{3,4},{4,3},{5,6},{6,5},{7,8},{8,7},{9,10},{10,... | collective-permute-start | bytes 294920 | tf_op jit(solution)/shard_map/ppermute | solution.py:747
  10.1 0.0 copy-start.1
  10.1 0.1 collective-permute-start.2
  10.2 0.0 copy-done.8
  10.2 0.4 %shard_map.147 = (bf16[1152,128]{1,0:T(8,128)(2,1)S(1)}, bf16[2,1152,128]{2,1,0:T(8,128)(2,1)S(1)}) custom-call(s32[8,27]{1,0:T(8,128)S(1)} %copy-done.7, bf16[432,27]{1,0:T(8,128)(2,1)S(1)} %copy-done.8, bf16[128,128]{1,0:T(8,128)(2,1)S(1)} %shard_map.146.later), custom_call_target="tpu_custom_call" | custom-call | flops 500000000 | bytes 10000000 | tf_op jit(solution)/shard_map/pallas_call | solution.py:703
  10.7 0.0 copy-done.9
  10.7 0.4 %shard_map.150 = (bf16[1728,96]{1,0:T(8,128)(2,1)S(1)}, bf16[288,32]{1,0:T(8,128)(2,1)S(1)}) custom-call(s32[8,27]{1,0:T(8,128)S(1)} %copy-done.7, bf16[432,27]{1,0:T(8,128)(2,1)S(1)} %copy-done.9, bf16[128,128]{1,0:T(8,128)(2,1)S(1)} %shard_map.146.later), custom_call_target="tpu_custom_call" | custom-call | flops 500000000 | bytes 10000000 | tf_op jit(solution)/shard_map/pallas_call | solution.py:703
  11.1 0.4 %shard_map.148.first = bf16[8,64,512]{2,1,0:T(8,128)(2,1)S(1)} custom-call(bf16[8,2,64,128]{3,2,1,0:T(8,128)(2,1)S(1)} %get-tuple-element.46.outer, bf16[8,2,64,128]{3,2,1,0:T(8,128)(2,1)S(1)} %get-tuple-element.47.inner), custom_call_target="tpu_custom_call" | custom-call | flops 500000000 | bytes 10000000 | tf_op jit(solution)/shard_map/pallas_call | solution.py:703
  11.5 0.4 %shard_map.151 = (bf16[1152,256]{1,0:T(8,128)(2,1)S(1)}, f32[256,128]{1,0:T(8,128)S(1)}, f32[32,256]{1,0:T(8,128)S(1)}) custom-call(bf16[272,128]{1,0:T(8,128)(2,1)S(1)} %collective-permute-done.1.from_b.message, bf16[432,27]{1,0:T(8,128)(2,1)S(1)} %copy-done.8, bf16[128,128]{1,0:T(8,128)(2,1)S(1)} %shard_map.146.later), custom_call_target="tpu_custom_call" | custom-call | flops 500000000 | bytes 10000000 | tf_op jit(solution)/shard_map/pallas_call | solution.py:703
  11.8 0.0 collective-permute-done.2.from_a
  11.8 0.0 copy-done.1
  11.8 0.0 copy-start.3
  11.9 0.0 copy-start.10
  11.9 0.0 copy-start.11
  11.9 1.2 %shard_map.149 = (f32[512,128]{1,0:T(8,128)S(1)}, bf16[8,64,512]{2,1,0:T(8,128)(2,1)}) custom-call(bf16[256,128]{1,0:T(8,128)(2,1)S(1)} %get-tuple-element.42.planes.outer, bf16[2,128,128]{2,1,0:T(8,128)(2,1)S(1)} %get-tuple-element.41.inner, bf16[1152,128]{1,0:T(8,128)(2,1)S(1)} %get-tuple-element.44.own_gather, ...), custom_call_target="tpu_custom_call" | custom-call | flops 10000000000 | bytes 10000000 | tf_op jit(solution)/shard_map/pallas_call | solution.py:703
  13.1 0.1 collective-permute-done.3.from_b
  13.2 0.0 copy-done.3
  13.2 0.0 copy-done.10
  13.2 0.0 copy-done.11
  13.2 0.0 copy-start
  13.2 1.7 %shard_map.152 = (bf16[8,64,128]{2,1,0:T(8,128)(2,1)S(1)}, bf16[64,256]{1,0:T(8,128)(2,1)S(1)}, bf16[32,256]{1,0:T(8,128)(2,1)S(1)}) custom-call(bf16[2,1152,128]{2,1,0:T(8,128)(2,1)S(1)} %get-tuple-element.45.gathers, bf16[1152,256]{1,0:T(8,128)(2,1)S(1)} %get-tuple-element.50.far_gather, bf16[128,128]{1,0:T(8,128)(2,1)S(1)} %copy-done.10, ...), custom_call_target="tpu_custom_call" | custom-call | flops 15000000512 | bytes 10000000 | tf_op jit(solution)/shard_map/pallas_call | solution.py:703
  15.0 0.4 %collective-permute-start.4 = (bf16[32,256]{1,0:T(8,128)(2,1)S(1)}, bf16[32,256]{1,0:T(8,128)(2,1)S(1)}, u32[]{:S(2)}, u32[]{:S(2)}) collective-permute-start(bf16[32,256]{1,0:T(8,128)(2,1)S(1)} %shard_map.154), channel_id=1, source_target_pairs={{0,1},{1,0},{2,3},{3,2},{4,5},{5,4},{6,7},{7,6},{8,9},{9,8},{10,11... | collective-permute-start | bytes 49160 | tf_op jit(solution)/shard_map/ppermute | solution.py:863
  15.4 0.0 copy-done
  15.4 1.1 %shard_map.153 = (f32[64,256]{1,0:T(8,128)S(1)}, bf16[8,64,128]{2,1,0:T(8,128)(2,1)}) custom-call(bf16[1728,96]{1,0:T(8,128)(2,1)S(1)} %get-tuple-element.49.gather, bf16[64,256]{1,0:T(8,128)(2,1)S(1)} %get-tuple-element.55.third.planes, bf16[32,256]{1,0:T(8,128)(2,1)S(1)} %get-tuple-element.56.far.earlier, bf16[27,256,256]{2,1,0:T(8,128)(2,1)S(1)} %copy-done, ...), custom_call_target="tpu_custom_call" | custom-call | flops 10000000000 | bytes 10000000 | tf_op jit(solution)/shard_map/pallas_call | solution.py:703
  16.5 0.0 collective-permute-done.4.from_a
  16.5 1.1 %shard_map.155 = bf16[8,8,256]{2,1,0:T(8,128)(2,1)} custom-call(bf16[288,32]{1,0:T(8,128)(2,1)S(1)} %get-tuple-element.59.gather, f32[64,256]{1,0:T(8,128)S(1)} %get-tuple-element.60.partial, bf16[32,256]{1,0:T(8,128)(2,1)S(1)} %collective-permute-done.4.from_a, bf16[27,256,256]{2,1,0:T(8,128)(2,1)S(1)} %copy-done, f32[64,256]{1,0:T(8,128)S(1)} %get-tuple-element.52.mask_three), custom_call_target="tpu_custom_call" | custom-call | flops 10000000000 | bytes 10000000 | tf_op jit(solution)/shard_map/pallas_call | solution.py:703
  (3 shorter events, 0.0 us)
Async XLA Ops:
  0.6 0.7 %copy-start.6 = (s32[8,16]{1,0:T(8,128)S(1)}, s32[8,16]{1,0:T(8,128)}, u32[]{:S(2)}) copy-start(s32[8,16]{1,0:T(8,128)} %occupancy.1) | copy-start | bytes 1540
  0.6 1.0 %copy-start.2 = (bf16[8,512,64]{1,2,0:T(8,128)(2,1)S(1)}, bf16[8,512,64]{1,2,0:T(8,128)(2,1)}, u32[]{:S(2)}) copy-start(bf16[8,512,64]{1,2,0:T(8,128)(2,1)} %param.12) | copy-start | bytes 1572868
  0.7 1.0 %copy-start.7 = (s32[8,27]{1,0:T(8,128)S(1)}, s32[8,27]{1,0:T(8,128)}, u32[]{:S(2)}) copy-start(s32[8,27]{1,0:T(8,128)} %neighbours.9) | copy-start | bytes 2596
  0.7 4.5 %copy-start.4 = (bf16[27,64,64]{2,1,0:T(8,128)(2,1)S(1)}, bf16[27,64,64]{2,1,0:T(8,128)(2,1)}, u32[]{:S(2)}) copy-start(bf16[27,64,64]{2,1,0:T(8,128)(2,1)} %kernel.5) | copy-start | bytes 663556
  0.7 4.5 %copy-start.5 = (bf16[8,64,128]{2,1,0:T(8,128)(2,1)S(1)}, bf16[8,64,128]{2,1,0:T(8,128)(2,1)}, u32[]{:S(2)}) copy-start(bf16[8,64,128]{2,1,0:T(8,128)(2,1)} %reduce.2) | copy-start | bytes 393220
  1.8 5.8 %collective-permute-start.1 = (bf16[272,128]{1,0:T(8,128)(2,1)S(1)}, bf16[272,128]{1,0:T(8,128)(2,1)S(1)}, u32[]{:S(2)}, u32[]{:S(2)}) collective-permute-start(bf16[272,128]{1,0:T(8,128)(2,1)S(1)} %shard_map.141.earlier), channel_id=1, source_target_pairs={{0,16},{1,2},{2,1},{3,4},{4,3},{5,6},{6,5},{7,8},{8,7},{9,10},{10,... | collective-permute-start | bytes 208904 | tf_op jit(solution)/shard_map/ppermute | solution.py:747
  4.9 2.6 %collective-permute-start = (bf16[4,64,128]{2,1,0:T(8,128)(2,1)S(1)}, bf16[4,64,128]{2,1,0:T(8,128)(2,1)S(1)}, u32[]{:S(2)}, u32[]{:S(2)}) collective-permute-start(bf16[4,64,128]{2,1,0:T(8,128)(2,1)S(1)} %shard_map.142), channel_id=1, source_target_pairs={{0,1},{1,0},{2,3},{3,2},{4,5},{5,4},{6,7},{7,6},{8,9},{9,8},{10,11... | collective-permute-start | bytes 196616 | tf_op jit(solution)/shard_map/ppermute | solution.py:748
  7.6 2.7 %copy-start.8 = (bf16[432,27]{1,0:T(8,128)(2,1)S(1)}, bf16[432,27]{1,0:T(8,128)(2,1)}, u32[]{:S(2)}) copy-start(bf16[432,27]{1,0:T(8,128)(2,1)} %constant.8.clone.pick) | copy-start | bytes 69988
  7.6 3.1 %copy-start.9 = (bf16[432,27]{1,0:T(8,128)(2,1)S(1)}, bf16[432,27]{1,0:T(8,128)(2,1)}, u32[]{:S(2)}) copy-start(bf16[432,27]{1,0:T(8,128)(2,1)} %constant.9.clone.pick) | copy-start | bytes 69988
  8.5 4.7 %collective-permute-start.3 = (bf16[384,128]{1,0:T(8,128)(2,1)S(1)}, bf16[384,128]{1,0:T(8,128)(2,1)S(1)}, u32[]{:S(2)}, u32[]{:S(2)}) collective-permute-start(bf16[384,128]{1,0:T(8,128)(2,1)S(1)} %get-tuple-element.43.earlier.to_b), channel_id=1, source_target_pairs={{0,16},{1,2},{2,1},{3,4},{4,3},{5,6},{6,5},{7,8},{8,7},{9,10},{10,... | collective-permute-start | bytes 294920 | tf_op jit(solution)/shard_map/ppermute | solution.py:747
  10.1 1.7 %copy-start.1 = (bf16[27,128,128]{2,1,0:T(8,128)(2,1)S(1)}, bf16[27,128,128]{2,1,0:T(8,128)(2,1)}, u32[]{:S(2)}) copy-start(bf16[27,128,128]{2,1,0:T(8,128)(2,1)} %kernel.7) | copy-start | bytes 2654212
  10.1 1.7 %collective-permute-start.2 = (bf16[128,128]{1,0:T(8,128)(2,1)S(1)}, bf16[128,128]{1,0:T(8,128)(2,1)S(1)}, u32[]{:S(2)}, u32[]{:S(2)}) collective-permute-start(bf16[128,128]{1,0:T(8,128)(2,1)S(1)} %shard_map.146.later), channel_id=1, source_target_pairs={{0,1},{1,0},{2,3},{3,2},{4,5},{5,4},{6,7},{7,6},{8,9},{9,8},{10,11... | collective-permute-start | bytes 98312 | tf_op jit(solution)/shard_map/ppermute | solution.py:748
  11.8 1.4 %copy-start.3 = (bf16[8,128,256]{2,1,0:T(8,128)(2,1)S(1)}, bf16[8,128,256]{2,1,0:T(8,128)(2,1)}, u32[]{:S(2)}) copy-start(bf16[8,128,256]{2,1,0:T(8,128)(2,1)} %reduce.3) | copy-start | bytes 1572868
  11.9 1.4 %copy-start.10 = (bf16[128,128]{1,0:T(8,128)(2,1)S(1)}, bf16[128,128]{1,0:T(8,128)(2,1)}, u32[]{:S(2)}) copy-start(bf16[128,128]{1,0:T(8,128)(2,1)} %constant.10.clone.children) | copy-start | bytes 98308
  11.9 1.4 %copy-start.11 = (bf16[64,64]{1,0:T(8,128)(2,1)S(1)}, bf16[64,64]{1,0:T(8,128)(2,1)}, u32[]{:S(2)}) copy-start(bf16[64,64]{1,0:T(8,128)(2,1)} %constant.11.clone.far_children) | copy-start | bytes 24580
  13.2 2.2 %copy-start = (bf16[27,256,256]{2,1,0:T(8,128)(2,1)S(1)}, bf16[27,256,256]{2,1,0:T(8,128)(2,1)}, u32[]{:S(2)}) copy-start(bf16[27,256,256]{2,1,0:T(8,128)(2,1)} %kernel.9) | copy-start | bytes 10616836
  15.0 1.5 %collective-permute-start.4 = (bf16[32,256]{1,0:T(8,128)(2,1)S(1)}, bf16[32,256]{1,0:T(8,128)(2,1)S(1)}, u32[]{:S(2)}, u32[]{:S(2)}) collective-permute-start(bf16[32,256]{1,0:T(8,128)(2,1)S(1)} %shard_map.154), channel_id=1, source_target_pairs={{0,1},{1,0},{2,3},{3,2},{4,5},{5,4},{6,7},{7,6},{8,9},{9,8},{10,11... | collective-permute-start | bytes 49160 | tf_op jit(solution)/shard_map/ppermute | solution.py:863

commit v6 on v5

--- a/solution.py
+++ b/solution.py
@@ -390,8 +390,8 @@
         [beside([tiles[j], tiles[j + 1]]) for tiles in groups for j in (0, 2, 4, 6)]
     ).astype(BF16)
     sums = dot(left, weights[...])
-    low_sums[...] = sums[:, :128]
-    high_sums[...] = sums[:, 128:]
+    low_sums[: sums.shape[0], :] = sums[:, :128]
+    high_sums[: sums.shape[0], :] = sums[:, 128:]
     return [
         low_sums[pl.ds(32 * g, 16, stride=2), :] + high_sums[pl.ds(32 * g + 1, 16, stride=2), :]
         for g in range(len(groups))
@@ -571,7 +571,27 @@
     rows = 16 * count
     odd = on_odd_place()
     high = jnp.where(odd, 1, 0)
-    far = face_part(gathers[high], from_b[:rows], kernel, high)
+    none = jnp.zeros((rows, 128), BF16)
+    sent = [from_b[d * rows : (d + 1) * rows] for d in range(3)]
+    moved = dot(
+        far_gather[...],
+        stack([beside(sent + [none]), beside([none, none, none, to_b[:rows]])]),
+    ).astype(BF16)
+    left = [
+        beside([moved[q * rows : (q + 1) * rows, 128 * d : 128 * (d + 1)] for q in range(9)])
+        for d in range(4)
+    ]
+    moved = dot(gathers[high], sent[0]).astype(BF16)
+    left.append(beside([moved[q * rows : (q + 1) * rows] for q in range(9)]))
+    toward, same, away = [
+        kernel[pl.ds(begin, 9)].reshape(9 * 128, 128) for begin in (18 - 18 * high, 9, 18 * high)
+    ]
+    zero = dot(stack([left[0], left[3]]), beside([same, toward]))
+    one = dot(left[1], beside([away, same]))
+    near = zero[rows:, 128:] + zero[:rows, :128] + one[:, :128]
+    two = dot(stack([left[2], left[4]]), away)
+    past = zero[:rows, 128:] + one[:, 128:] + two[:rows]
+    far = two[rows:]
     planes = []
     for i in range(4):
         sums = partial[i * rows : (i + 1) * rows]
@@ -587,23 +607,6 @@
         children[...], beside([stack(bricks[b : b + 2]) for b in range(0, count, 2)])
     )
 
-    none = jnp.zeros((rows, 128), BF16)
-    planes = [from_b[d * rows : (d + 1) * rows] for d in range(3)]
-    moved = dot(
-        far_gather[...],
-        stack([beside(planes + [none]), beside([none, none, none, to_b[:rows]])]),
-    ).astype(BF16)
-    left = [
-        beside([moved[q * rows : (q + 1) * rows, 128 * d : 128 * (d + 1)] for q in range(9)])
-        for d in range(4)
-    ]
-    toward, same, away = [
-        kernel[pl.ds(begin, 9)].reshape(9 * 128, 128) for begin in (18 - 18 * high, 9, 18 * high)
-    ]
-    zero = dot(stack([left[0], left[3]]), beside([same, toward]))
-    one = dot(left[1], beside([away, same]))
-    near = zero[rows:, 128:] + zero[:rows, :128] + one[:, :128]
-    past = zero[:rows, 128:] + one[:, 128:] + dot(left[2], away)
     far_planes = [
         (jnp.maximum(sums, 0.0) * far_mask_two[n * rows : (n + 1) * rows]).astype(BF16)
         for n, sums in enumerate((jnp.where(odd, near, past), jnp.where(odd, past, near)))
@@ -790,7 +793,7 @@
     )
     plane = shape((16 * count, 128), BF16)
     rows = shape((count, 2, 64, 128), BF16)
-    sums = pltpu.VMEM((count * 64, 128), F32)
+    sums = pltpu.VMEM((count * 64 + 8, 128), F32)
     inner, inner_two = call(
         inner_kernel,
         0.05,

time: 17.7 us -> 17.6 us (level)
  Pallas kernels: 10.4 us -> 10.1 us
    pallas_call x17, Pallas kernels: 10.4 us -> 10.1 us  [call(): pl.pallas_call(kernel, out_shape=out_shape, in_specs=[ANY if n in remain...]
where the time goes in v6:
time: 17.6 us; the launch traced here: 17.4 us
  Pallas kernels  10.1 us (57%)
  starting transfers between devices  5.29 us (30%)
  local copies, waits for them, and re-layouts  1.07 us (6%)
  between operations  0.87 us (5%)
    pallas_call x17, Pallas kernels, call(): pl.pallas_call(kernel, out_shape=out_shape, in_specs=[ANY if n in remain...  10.1 us
    ppermute x2, starting transfers between devices, exchange(): from_b = lax.ppermute(to_b, axes, across)  4.59 us
    unnamed x24, local copies, waits for them, and re-layouts  1.07 us
    ppermute x1, starting transfers between devices, on_device(): from_a = lax.ppermute(to_a, axes, within)  0.38 us
  transfers between devices with their start and end apart: 5, of which 1 were waited for; matrix products, arithmetic and copies ran while one was open for 0% of the time, Pallas kernels for 36%

profile of v6, /device:TPU:0, one launch (start us, length us, event | category | flops | bytes accessed | tf_op | source)
XLA Modules:
  0.0 17.4 jit_solution(18410058769616898802)
XLA Ops:
  0.6 0.0 copy-start.6
  0.6 0.0 copy-start.2
  0.7 0.0 copy-start.7
  0.7 0.0 copy-start.4
  0.7 0.0 copy-start.5
  0.7 0.6 %copy-done.6 = s32[8,16]{1,0:T(8,128)S(1)} copy-done((s32[8,16]{1,0:T(8,128)S(1)}, s32[8,16]{1,0:T(8,128)}, u32[]{:S(2)}) %copy-start.6) | copy-done | bytes 536
  1.3 0.1 shard_map.140
  1.5 0.2 %copy-done.2 = bf16[8,512,64]{1,2,0:T(8,128)(2,1)S(1)} copy-done((bf16[8,512,64]{1,2,0:T(8,128)(2,1)S(1)}, bf16[8,512,64]{1,2,0:T(8,128)(2,1)}, u32[]{:S(2)}) %copy-start.2) | copy-done | bytes 524312
  1.7 0.0 copy-done.7
  1.7 0.1 shard_map.141.earlier
  1.8 3.0 %collective-permute-start.1 = (bf16[272,128]{1,0:T(8,128)(2,1)S(1)}, bf16[272,128]{1,0:T(8,128)(2,1)S(1)}, u32[]{:S(2)}, u32[]{:S(2)}) collective-permute-start(bf16[272,128]{1,0:T(8,128)(2,1)S(1)} %shard_map.141.earlier), channel_id=1, source_target_pairs={{0,16},{1,2},{2,1},{3,4},{4,3},{5,6},{6,5},{7,8},{8,7},{9,10},{10,... | collective-permute-start | bytes 208904 | tf_op jit(solution)/shard_map/ppermute | solution.py:750
  4.8 0.1 shard_map.142
  4.9 0.2 %collective-permute-start = (bf16[4,64,128]{2,1,0:T(8,128)(2,1)S(1)}, bf16[4,64,128]{2,1,0:T(8,128)(2,1)S(1)}, u32[]{:S(2)}, u32[]{:S(2)}) collective-permute-start(bf16[4,64,128]{2,1,0:T(8,128)(2,1)S(1)} %shard_map.142), channel_id=1, source_target_pairs={{0,1},{1,0},{2,3},{3,2},{4,5},{5,4},{6,7},{7,6},{8,9},{9,8},{10,11... | collective-permute-start | bytes 196616 | tf_op jit(solution)/shard_map/ppermute | solution.py:751
  5.1 0.0 copy-done.4
  5.1 0.0 copy-done.5
  5.1 1.6 %shard_map.143 = (bf16[8,3,6,16,128]{4,3,2,1,0:T(8,128)(2,1)S(1)}, bf16[1152,256]{1,0:T(8,128)(2,1)S(1)}, bf16[1152,128]{1,0:T(8,128)(2,1)S(1)}, bf16[256,256]{1,0:T(8,128)(2,1)S(1)}, f32[4,512,128]{2,1,0:T(8,128)S(1)}) custom-call(s32[8,27]{1,0:T(8,128)S(1)} %copy-done.7, f32[4,8,128]{2,1,0:T(8,128)S(1)} %get-tuple-element.32.bits, ...), custom_call_target="tpu_custom_call" | custom-call | flops 20000000000 | bytes 10000000 | tf_op jit(solution)/shard_map/pallas_call | solution.py:706
  6.8 0.8 %shard_map.144 = (bf16[8,2,64,128]{3,2,1,0:T(8,128)(2,1)S(1)}, bf16[2,128,128]{2,1,0:T(8,128)(2,1)S(1)}) custom-call(bf16[8,3,6,16,128]{4,3,2,1,0:T(8,128)(2,1)S(1)} %get-tuple-element.39.middle, bf16[1152,256]{1,0:T(8,128)(2,1)S(1)} %get-tuple-element.40.taps, f32[4,512,128]{2,1,0:T(8,128)S(1)} %get-tuple-element.35.partial, ...), custom_call_target="tpu_custom_call" | custom-call | flops 500000000 | bytes 10000000 | tf_op jit(solution)/shard_map/pallas_call | solution.py:706
  7.5 0.0 collective-permute-done.from_a
  7.6 0.0 collective-permute-done.1.from_b.message
  7.6 0.0 copy-start.8
  7.6 0.0 copy-start.9
  7.6 0.9 %shard_map.145 = (bf16[8,2,64,128]{3,2,1,0:T(8,128)(2,1)S(1)}, bf16[256,128]{1,0:T(8,128)(2,1)S(1)}, bf16[384,128]{1,0:T(8,128)(2,1)S(1)}) custom-call(s32[8,27]{1,0:T(8,128)S(1)} %copy-done.7, bf16[4,64,128]{2,1,0:T(8,128)(2,1)S(1)} %collective-permute-done.from_a, bf16[272,128]{1,0:T(8,128)(2,1)S(1)} %collective-permute-done.1.from_b.message, ...), custom_call_target="tpu_custom_call" | custom-call | flops 15000000512 | bytes 10000000 | tf_op jit(solution)/shard_map/pallas_call | solution.py:706
  8.5 1.6 %collective-permute-start.3 = (bf16[384,128]{1,0:T(8,128)(2,1)S(1)}, bf16[384,128]{1,0:T(8,128)(2,1)S(1)}, u32[]{:S(2)}, u32[]{:S(2)}) collective-permute-start(bf16[384,128]{1,0:T(8,128)(2,1)S(1)} %get-tuple-element.43.earlier.to_b), channel_id=1, source_target_pairs={{0,16},{1,2},{2,1},{3,4},{4,3},{5,6},{6,5},{7,8},{8,7},{9,10},{10,... | collective-permute-start | bytes 294920 | tf_op jit(solution)/shard_map/ppermute | solution.py:750
  10.1 0.0 copy-start.1
  10.1 0.1 collective-permute-start.2
  10.2 0.0 copy-done.8
  10.2 0.4 %shard_map.147 = (bf16[1152,128]{1,0:T(8,128)(2,1)S(1)}, bf16[2,1152,128]{2,1,0:T(8,128)(2,1)S(1)}) custom-call(s32[8,27]{1,0:T(8,128)S(1)} %copy-done.7, bf16[432,27]{1,0:T(8,128)(2,1)S(1)} %copy-done.8, bf16[128,128]{1,0:T(8,128)(2,1)S(1)} %shard_map.146.later), custom_call_target="tpu_custom_call" | custom-call | flops 500000000 | bytes 10000000 | tf_op jit(solution)/shard_map/pallas_call | solution.py:706
  10.6 0.0 copy-done.9
  10.7 0.4 %shard_map.150 = (bf16[1728,96]{1,0:T(8,128)(2,1)S(1)}, bf16[288,32]{1,0:T(8,128)(2,1)S(1)}) custom-call(s32[8,27]{1,0:T(8,128)S(1)} %copy-done.7, bf16[432,27]{1,0:T(8,128)(2,1)S(1)} %copy-done.9, bf16[128,128]{1,0:T(8,128)(2,1)S(1)} %shard_map.146.later), custom_call_target="tpu_custom_call" | custom-call | flops 500000000 | bytes 10000000 | tf_op jit(solution)/shard_map/pallas_call | solution.py:706
  11.1 0.4 %shard_map.148.first = bf16[8,64,512]{2,1,0:T(8,128)(2,1)S(1)} custom-call(bf16[8,2,64,128]{3,2,1,0:T(8,128)(2,1)S(1)} %get-tuple-element.46.outer, bf16[8,2,64,128]{3,2,1,0:T(8,128)(2,1)S(1)} %get-tuple-element.47.inner), custom_call_target="tpu_custom_call" | custom-call | flops 500000000 | bytes 10000000 | tf_op jit(solution)/shard_map/pallas_call | solution.py:706
  11.5 0.4 %shard_map.151 = (bf16[1152,256]{1,0:T(8,128)(2,1)S(1)}, f32[256,128]{1,0:T(8,128)S(1)}, f32[32,256]{1,0:T(8,128)S(1)}) custom-call(bf16[272,128]{1,0:T(8,128)(2,1)S(1)} %collective-permute-done.1.from_b.message, bf16[432,27]{1,0:T(8,128)(2,1)S(1)} %copy-done.8, bf16[128,128]{1,0:T(8,128)(2,1)S(1)} %shard_map.146.later), custom_call_target="tpu_custom_call" | custom-call | flops 500000000 | bytes 10000000 | tf_op jit(solution)/shard_map/pallas_call | solution.py:706
  11.8 0.0 collective-permute-done.2.from_a
  11.8 0.0 copy-done.1
  11.8 0.0 copy-start.3
  11.8 0.0 copy-start.10
  11.9 0.0 copy-start.11
  11.9 1.2 %shard_map.149 = (f32[512,128]{1,0:T(8,128)S(1)}, bf16[8,64,512]{2,1,0:T(8,128)(2,1)}) custom-call(bf16[256,128]{1,0:T(8,128)(2,1)S(1)} %get-tuple-element.42.planes.outer, bf16[2,128,128]{2,1,0:T(8,128)(2,1)S(1)} %get-tuple-element.41.inner, bf16[1152,128]{1,0:T(8,128)(2,1)S(1)} %get-tuple-element.44.own_gather, ...), custom_call_target="tpu_custom_call" | custom-call | flops 10000000000 | bytes 10000000 | tf_op jit(solution)/shard_map/pallas_call | solution.py:706
  13.1 0.1 collective-permute-done.3.from_b
  13.2 0.0 copy-done.3
  13.2 0.0 copy-done.10
  13.2 0.0 copy-done.11
  13.2 0.0 copy-start
  13.2 1.4 %shard_map.152 = (bf16[8,64,128]{2,1,0:T(8,128)(2,1)S(1)}, bf16[64,256]{1,0:T(8,128)(2,1)S(1)}, bf16[32,256]{1,0:T(8,128)(2,1)S(1)}) custom-call(bf16[2,1152,128]{2,1,0:T(8,128)(2,1)S(1)} %get-tuple-element.45.gathers, bf16[1152,256]{1,0:T(8,128)(2,1)S(1)} %get-tuple-element.50.far_gather, bf16[128,128]{1,0:T(8,128)(2,1)S(1)} %copy-done.10, ...), custom_call_target="tpu_custom_call" | custom-call | flops 15000000512 | bytes 10000000 | tf_op jit(solution)/shard_map/pallas_call | solution.py:706
  14.7 0.4 %collective-permute-start.4 = (bf16[32,256]{1,0:T(8,128)(2,1)S(1)}, bf16[32,256]{1,0:T(8,128)(2,1)S(1)}, u32[]{:S(2)}, u32[]{:S(2)}) collective-permute-start(bf16[32,256]{1,0:T(8,128)(2,1)S(1)} %shard_map.154), channel_id=1, source_target_pairs={{0,1},{1,0},{2,3},{3,2},{4,5},{5,4},{6,7},{7,6},{8,9},{9,8},{10,11... | collective-permute-start | bytes 49160 | tf_op jit(solution)/shard_map/ppermute | solution.py:866
  15.1 0.2 copy-done
  15.2 1.1 %shard_map.153 = (f32[64,256]{1,0:T(8,128)S(1)}, bf16[8,64,128]{2,1,0:T(8,128)(2,1)}) custom-call(bf16[1728,96]{1,0:T(8,128)(2,1)S(1)} %get-tuple-element.49.gather, bf16[64,256]{1,0:T(8,128)(2,1)S(1)} %get-tuple-element.55.third.planes, bf16[32,256]{1,0:T(8,128)(2,1)S(1)} %get-tuple-element.56.far.earlier, bf16[27,256,256]{2,1,0:T(8,128)(2,1)S(1)} %copy-done, ...), custom_call_target="tpu_custom_call" | custom-call | flops 10000000000 | bytes 10000000 | tf_op jit(solution)/shard_map/pallas_call | solution.py:706
  16.3 0.0 collective-permute-done.4.from_a
  16.3 1.1 %shard_map.155 = bf16[8,8,256]{2,1,0:T(8,128)(2,1)} custom-call(bf16[288,32]{1,0:T(8,128)(2,1)S(1)} %get-tuple-element.59.gather, f32[64,256]{1,0:T(8,128)S(1)} %get-tuple-element.60.partial, bf16[32,256]{1,0:T(8,128)(2,1)S(1)} %collective-permute-done.4.from_a, bf16[27,256,256]{2,1,0:T(8,128)(2,1)S(1)} %copy-done, f32[64,256]{1,0:T(8,128)S(1)} %get-tuple-element.52.mask_three), custom_call_target="tpu_custom_call" | custom-call | flops 10000000000 | bytes 10000000 | tf_op jit(solution)/shard_map/pallas_call | solution.py:706
  (3 shorter events, 0.0 us)
Async XLA Ops:
  0.6 0.7 %copy-start.6 = (s32[8,16]{1,0:T(8,128)S(1)}, s32[8,16]{1,0:T(8,128)}, u32[]{:S(2)}) copy-start(s32[8,16]{1,0:T(8,128)} %occupancy.1) | copy-start | bytes 1540
  0.6 1.0 %copy-start.2 = (bf16[8,512,64]{1,2,0:T(8,128)(2,1)S(1)}, bf16[8,512,64]{1,2,0:T(8,128)(2,1)}, u32[]{:S(2)}) copy-start(bf16[8,512,64]{1,2,0:T(8,128)(2,1)} %param.12) | copy-start | bytes 1572868
  0.7 1.0 %copy-start.7 = (s32[8,27]{1,0:T(8,128)S(1)}, s32[8,27]{1,0:T(8,128)}, u32[]{:S(2)}) copy-start(s32[8,27]{1,0:T(8,128)} %neighbours.9) | copy-start | bytes 2596
  0.7 4.5 %copy-start.4 = (bf16[27,64,64]{2,1,0:T(8,128)(2,1)S(1)}, bf16[27,64,64]{2,1,0:T(8,128)(2,1)}, u32[]{:S(2)}) copy-start(bf16[27,64,64]{2,1,0:T(8,128)(2,1)} %kernel.5) | copy-start | bytes 663556
  0.7 4.5 %copy-start.5 = (bf16[8,64,128]{2,1,0:T(8,128)(2,1)S(1)}, bf16[8,64,128]{2,1,0:T(8,128)(2,1)}, u32[]{:S(2)}) copy-start(bf16[8,64,128]{2,1,0:T(8,128)(2,1)} %reduce.2) | copy-start | bytes 393220
  1.8 5.8 %collective-permute-start.1 = (bf16[272,128]{1,0:T(8,128)(2,1)S(1)}, bf16[272,128]{1,0:T(8,128)(2,1)S(1)}, u32[]{:S(2)}, u32[]{:S(2)}) collective-permute-start(bf16[272,128]{1,0:T(8,128)(2,1)S(1)} %shard_map.141.earlier), channel_id=1, source_target_pairs={{0,16},{1,2},{2,1},{3,4},{4,3},{5,6},{6,5},{7,8},{8,7},{9,10},{10,... | collective-permute-start | bytes 208904 | tf_op jit(solution)/shard_map/ppermute | solution.py:750
  4.9 2.6 %collective-permute-start = (bf16[4,64,128]{2,1,0:T(8,128)(2,1)S(1)}, bf16[4,64,128]{2,1,0:T(8,128)(2,1)S(1)}, u32[]{:S(2)}, u32[]{:S(2)}) collective-permute-start(bf16[4,64,128]{2,1,0:T(8,128)(2,1)S(1)} %shard_map.142), channel_id=1, source_target_pairs={{0,1},{1,0},{2,3},{3,2},{4,5},{5,4},{6,7},{7,6},{8,9},{9,8},{10,11... | collective-permute-start | bytes 196616 | tf_op jit(solution)/shard_map/ppermute | solution.py:751
  7.6 2.7 %copy-start.8 = (bf16[432,27]{1,0:T(8,128)(2,1)S(1)}, bf16[432,27]{1,0:T(8,128)(2,1)}, u32[]{:S(2)}) copy-start(bf16[432,27]{1,0:T(8,128)(2,1)} %constant.8.clone.pick) | copy-start | bytes 69988
  7.6 3.1 %copy-start.9 = (bf16[432,27]{1,0:T(8,128)(2,1)S(1)}, bf16[432,27]{1,0:T(8,128)(2,1)}, u32[]{:S(2)}) copy-start(bf16[432,27]{1,0:T(8,128)(2,1)} %constant.9.clone.pick) | copy-start | bytes 69988
  8.5 4.7 %collective-permute-start.3 = (bf16[384,128]{1,0:T(8,128)(2,1)S(1)}, bf16[384,128]{1,0:T(8,128)(2,1)S(1)}, u32[]{:S(2)}, u32[]{:S(2)}) collective-permute-start(bf16[384,128]{1,0:T(8,128)(2,1)S(1)} %get-tuple-element.43.earlier.to_b), channel_id=1, source_target_pairs={{0,16},{1,2},{2,1},{3,4},{4,3},{5,6},{6,5},{7,8},{8,7},{9,10},{10,... | collective-permute-start | bytes 294920 | tf_op jit(solution)/shard_map/ppermute | solution.py:750
  10.1 1.7 %copy-start.1 = (bf16[27,128,128]{2,1,0:T(8,128)(2,1)S(1)}, bf16[27,128,128]{2,1,0:T(8,128)(2,1)}, u32[]{:S(2)}) copy-start(bf16[27,128,128]{2,1,0:T(8,128)(2,1)} %kernel.7) | copy-start | bytes 2654212
  10.1 1.7 %collective-permute-start.2 = (bf16[128,128]{1,0:T(8,128)(2,1)S(1)}, bf16[128,128]{1,0:T(8,128)(2,1)S(1)}, u32[]{:S(2)}, u32[]{:S(2)}) collective-permute-start(bf16[128,128]{1,0:T(8,128)(2,1)S(1)} %shard_map.146.later), channel_id=1, source_target_pairs={{0,1},{1,0},{2,3},{3,2},{4,5},{5,4},{6,7},{7,6},{8,9},{9,8},{10,11... | collective-permute-start | bytes 98312 | tf_op jit(solution)/shard_map/ppermute | solution.py:751
  11.8 1.4 %copy-start.3 = (bf16[8,128,256]{2,1,0:T(8,128)(2,1)S(1)}, bf16[8,128,256]{2,1,0:T(8,128)(2,1)}, u32[]{:S(2)}) copy-start(bf16[8,128,256]{2,1,0:T(8,128)(2,1)} %reduce.3) | copy-start | bytes 1572868
  11.8 1.4 %copy-start.10 = (bf16[128,128]{1,0:T(8,128)(2,1)S(1)}, bf16[128,128]{1,0:T(8,128)(2,1)}, u32[]{:S(2)}) copy-start(bf16[128,128]{1,0:T(8,128)(2,1)} %constant.10.clone.children) | copy-start | bytes 98308
  11.9 1.4 %copy-start.11 = (bf16[64,64]{1,0:T(8,128)(2,1)S(1)}, bf16[64,64]{1,0:T(8,128)(2,1)}, u32[]{:S(2)}) copy-start(bf16[64,64]{1,0:T(8,128)(2,1)} %constant.11.clone.far_children) | copy-start | bytes 24580
  13.2 2.0 %copy-start = (bf16[27,256,256]{2,1,0:T(8,128)(2,1)S(1)}, bf16[27,256,256]{2,1,0:T(8,128)(2,1)}, u32[]{:S(2)}) copy-start(bf16[27,256,256]{2,1,0:T(8,128)(2,1)} %kernel.9) | copy-start | bytes 10616836
  14.7 1.6 %collective-permute-start.4 = (bf16[32,256]{1,0:T(8,128)(2,1)S(1)}, bf16[32,256]{1,0:T(8,128)(2,1)S(1)}, u32[]{:S(2)}, u32[]{:S(2)}) collective-permute-start(bf16[32,256]{1,0:T(8,128)(2,1)S(1)} %shard_map.154), channel_id=1, source_target_pairs={{0,1},{1,0},{2,3},{3,2},{4,5},{5,4},{6,7},{7,6},{8,9},{9,8},{10,11... | collective-permute-start | bytes 49160 | tf_op jit(solution)/shard_map/ppermute | solution.py:866

commit v7 on v6

--- a/solution.py
+++ b/solution.py
@@ -856,7 +856,7 @@
     face = shape((4 * count, 256), BF16)
     second_level, third, far_third = call(
         faces_two_kernel,
-        1.5,
+        0.05,
         (shape((count, 64, 128), BF16), shape((8 * count, 256), BF16), face),
         [],
         sides_two, far_two, child_rows(2), child_rows(1), partial, to_b, from_b, conv_two,

time: 17.6 us -> 17.4 us (0.989)
  transfers between devices with their start and end apart: 5 -> 5, of which waited for: 1 -> 1; matrix products, arithmetic and copies ran while one was open for 0% -> 0% of each run, Pallas kernels for 36% -> 37%
where the time goes in v7:
time: 17.4 us; the launch traced here: 17.3 us
  Pallas kernels  10.1 us (58%)
  starting transfers between devices  5.29 us (30%)
  local copies, waits for them, and re-layouts  0.95 us (5%)
  between operations  0.87 us (5%)
    pallas_call x17, Pallas kernels, call(): pl.pallas_call(kernel, out_shape=out_shape, in_specs=[ANY if n in remain...  10.1 us
    ppermute x2, starting transfers between devices, exchange(): from_b = lax.ppermute(to_b, axes, across)  4.59 us
    unnamed x24, local copies, waits for them, and re-layouts  0.95 us
    ppermute x1, starting transfers between devices, on_device(): from_a = lax.ppermute(to_a, axes, within)  0.38 us
  transfers between devices with their start and end apart: 5, of which 1 were waited for; matrix products, arithmetic and copies ran while one was open for 0% of the time, Pallas kernels for 37%

profile of v7, /device:TPU:0, one launch (start us, length us, event | category | flops | bytes accessed | tf_op | source)
XLA Modules:
  0.0 17.3 jit_solution(4046061135402558422)
XLA Ops:
  0.6 0.0 copy-start.8
  0.6 0.0 copy-start.5
  0.7 0.0 copy-start.9
  0.7 0.0 copy-start.6
  0.7 0.0 copy-start.7
  0.7 0.6 %copy-done.8 = s32[8,16]{1,0:T(8,128)S(1)} copy-done((s32[8,16]{1,0:T(8,128)S(1)}, s32[8,16]{1,0:T(8,128)}, u32[]{:S(2)}) %copy-start.8) | copy-done | bytes 536
  1.3 0.1 shard_map.140
  1.5 0.2 %copy-done.5 = bf16[8,512,64]{1,2,0:T(8,128)(2,1)S(1)} copy-done((bf16[8,512,64]{1,2,0:T(8,128)(2,1)S(1)}, bf16[8,512,64]{1,2,0:T(8,128)(2,1)}, u32[]{:S(2)}) %copy-start.5) | copy-done | bytes 524312
  1.7 0.0 copy-done.9
  1.7 0.1 shard_map.141.earlier
  1.8 3.0 %collective-permute-start.1 = (bf16[272,128]{1,0:T(8,128)(2,1)S(1)}, bf16[272,128]{1,0:T(8,128)(2,1)S(1)}, u32[]{:S(2)}, u32[]{:S(2)}) collective-permute-start(bf16[272,128]{1,0:T(8,128)(2,1)S(1)} %shard_map.141.earlier), channel_id=1, source_target_pairs={{0,16},{1,2},{2,1},{3,4},{4,3},{5,6},{6,5},{7,8},{8,7},{9,10},{10,... | collective-permute-start | bytes 208904 | tf_op jit(solution)/shard_map/ppermute | solution.py:750
  4.8 0.1 shard_map.142
  4.9 0.2 %collective-permute-start = (bf16[4,64,128]{2,1,0:T(8,128)(2,1)S(1)}, bf16[4,64,128]{2,1,0:T(8,128)(2,1)S(1)}, u32[]{:S(2)}, u32[]{:S(2)}) collective-permute-start(bf16[4,64,128]{2,1,0:T(8,128)(2,1)S(1)} %shard_map.142), channel_id=1, source_target_pairs={{0,1},{1,0},{2,3},{3,2},{4,5},{5,4},{6,7},{7,6},{8,9},{9,8},{10,11... | collective-permute-start | bytes 196616 | tf_op jit(solution)/shard_map/ppermute | solution.py:751
  5.1 0.0 copy-done.6
  5.1 0.0 copy-done.7
  5.1 1.6 %shard_map.143 = (bf16[8,3,6,16,128]{4,3,2,1,0:T(8,128)(2,1)S(1)}, bf16[1152,256]{1,0:T(8,128)(2,1)S(1)}, bf16[1152,128]{1,0:T(8,128)(2,1)S(1)}, bf16[256,256]{1,0:T(8,128)(2,1)S(1)}, f32[4,512,128]{2,1,0:T(8,128)S(1)}) custom-call(s32[8,27]{1,0:T(8,128)S(1)} %copy-done.9, f32[4,8,128]{2,1,0:T(8,128)S(1)} %get-tuple-element.32.bits, ...), custom_call_target="tpu_custom_call" | custom-call | flops 20000000000 | bytes 10000000 | tf_op jit(solution)/shard_map/pallas_call | solution.py:706
  6.8 0.8 %shard_map.144 = (bf16[8,2,64,128]{3,2,1,0:T(8,128)(2,1)S(1)}, bf16[2,128,128]{2,1,0:T(8,128)(2,1)S(1)}) custom-call(bf16[8,3,6,16,128]{4,3,2,1,0:T(8,128)(2,1)S(1)} %get-tuple-element.39.middle, bf16[1152,256]{1,0:T(8,128)(2,1)S(1)} %get-tuple-element.40.taps, f32[4,512,128]{2,1,0:T(8,128)S(1)} %get-tuple-element.35.partial, ...), custom_call_target="tpu_custom_call" | custom-call | flops 500000000 | bytes 10000000 | tf_op jit(solution)/shard_map/pallas_call | solution.py:706
  7.6 0.0 collective-permute-done.from_a
  7.6 0.0 collective-permute-done.1.from_b.message
  7.6 0.0 copy-start.10
  7.6 0.0 copy-start.11
  7.6 0.9 %shard_map.145 = (bf16[8,2,64,128]{3,2,1,0:T(8,128)(2,1)S(1)}, bf16[256,128]{1,0:T(8,128)(2,1)S(1)}, bf16[384,128]{1,0:T(8,128)(2,1)S(1)}) custom-call(s32[8,27]{1,0:T(8,128)S(1)} %copy-done.9, bf16[4,64,128]{2,1,0:T(8,128)(2,1)S(1)} %collective-permute-done.from_a, bf16[272,128]{1,0:T(8,128)(2,1)S(1)} %collective-permute-done.1.from_b.message, ...), custom_call_target="tpu_custom_call" | custom-call | flops 15000000512 | bytes 10000000 | tf_op jit(solution)/shard_map/pallas_call | solution.py:706
  8.5 1.6 %collective-permute-start.3 = (bf16[384,128]{1,0:T(8,128)(2,1)S(1)}, bf16[384,128]{1,0:T(8,128)(2,1)S(1)}, u32[]{:S(2)}, u32[]{:S(2)}) collective-permute-start(bf16[384,128]{1,0:T(8,128)(2,1)S(1)} %get-tuple-element.43.earlier.to_b), channel_id=1, source_target_pairs={{0,16},{1,2},{2,1},{3,4},{4,3},{5,6},{6,5},{7,8},{8,7},{9,10},{10,... | collective-permute-start | bytes 294920 | tf_op jit(solution)/shard_map/ppermute | solution.py:750
  10.1 0.0 copy-start
  10.1 0.1 collective-permute-start.2
  10.2 0.0 copy-done.10
  10.2 0.4 %shard_map.147 = (bf16[1152,128]{1,0:T(8,128)(2,1)S(1)}, bf16[2,1152,128]{2,1,0:T(8,128)(2,1)S(1)}) custom-call(s32[8,27]{1,0:T(8,128)S(1)} %copy-done.9, bf16[432,27]{1,0:T(8,128)(2,1)S(1)} %copy-done.10, bf16[128,128]{1,0:T(8,128)(2,1)S(1)} %shard_map.146.later), custom_call_target="tpu_custom_call" | custom-call | flops 500000000 | bytes 10000000 | tf_op jit(solution)/shard_map/pallas_call | solution.py:706
  10.6 0.0 copy-done.11
  10.7 0.4 %shard_map.150 = (bf16[1728,96]{1,0:T(8,128)(2,1)S(1)}, bf16[288,32]{1,0:T(8,128)(2,1)S(1)}) custom-call(s32[8,27]{1,0:T(8,128)S(1)} %copy-done.9, bf16[432,27]{1,0:T(8,128)(2,1)S(1)} %copy-done.11, bf16[128,128]{1,0:T(8,128)(2,1)S(1)} %shard_map.146.later), custom_call_target="tpu_custom_call" | custom-call | flops 500000000 | bytes 10000000 | tf_op jit(solution)/shard_map/pallas_call | solution.py:706
  11.1 0.4 %shard_map.148.first = bf16[8,64,512]{2,1,0:T(8,128)(2,1)S(1)} custom-call(bf16[8,2,64,128]{3,2,1,0:T(8,128)(2,1)S(1)} %get-tuple-element.46.outer, bf16[8,2,64,128]{3,2,1,0:T(8,128)(2,1)S(1)} %get-tuple-element.47.inner), custom_call_target="tpu_custom_call" | custom-call | flops 500000000 | bytes 10000000 | tf_op jit(solution)/shard_map/pallas_call | solution.py:706
  11.5 0.4 %shard_map.151 = (bf16[1152,256]{1,0:T(8,128)(2,1)S(1)}, f32[256,128]{1,0:T(8,128)S(1)}, f32[32,256]{1,0:T(8,128)S(1)}) custom-call(bf16[272,128]{1,0:T(8,128)(2,1)S(1)} %collective-permute-done.1.from_b.message, bf16[432,27]{1,0:T(8,128)(2,1)S(1)} %copy-done.10, bf16[128,128]{1,0:T(8,128)(2,1)S(1)} %shard_map.146.later), custom_call_target="tpu_custom_call" | custom-call | flops 500000000 | bytes 10000000 | tf_op jit(solution)/shard_map/pallas_call | solution.py:706
  11.8 0.0 collective-permute-done.2.from_a
  11.8 0.0 copy-done
  11.8 0.0 copy-start.1
  11.8 0.0 copy-start.2
  11.9 0.0 copy-start.3
  11.9 1.2 %shard_map.149 = (f32[512,128]{1,0:T(8,128)S(1)}, bf16[8,64,512]{2,1,0:T(8,128)(2,1)}) custom-call(bf16[256,128]{1,0:T(8,128)(2,1)S(1)} %get-tuple-element.42.planes.outer, bf16[2,128,128]{2,1,0:T(8,128)(2,1)S(1)} %get-tuple-element.41.inner, bf16[1152,128]{1,0:T(8,128)(2,1)S(1)} %get-tuple-element.44.own_gather, ...), custom_call_target="tpu_custom_call" | custom-call | flops 10000000000 | bytes 10000000 | tf_op jit(solution)/shard_map/pallas_call | solution.py:706
  13.1 0.0 copy-start.4
  13.1 0.1 collective-permute-done.3.from_b
  13.2 0.0 copy-done.1
  13.2 0.0 copy-done.2
  13.2 0.0 copy-done.3
  13.2 1.4 %shard_map.152 = (bf16[8,64,128]{2,1,0:T(8,128)(2,1)S(1)}, bf16[64,256]{1,0:T(8,128)(2,1)S(1)}, bf16[32,256]{1,0:T(8,128)(2,1)S(1)}) custom-call(bf16[2,1152,128]{2,1,0:T(8,128)(2,1)S(1)} %get-tuple-element.45.gathers, bf16[1152,256]{1,0:T(8,128)(2,1)S(1)} %get-tuple-element.50.far_gather, bf16[128,128]{1,0:T(8,128)(2,1)S(1)} %copy-done.2, ...), custom_call_target="tpu_custom_call" | custom-call | flops 500000000 | bytes 10000000 | tf_op jit(solution)/shard_map/pallas_call | solution.py:706
  14.7 0.4 %collective-permute-start.4 = (bf16[32,256]{1,0:T(8,128)(2,1)S(1)}, bf16[32,256]{1,0:T(8,128)(2,1)S(1)}, u32[]{:S(2)}, u32[]{:S(2)}) collective-permute-start(bf16[32,256]{1,0:T(8,128)(2,1)S(1)} %shard_map.154), channel_id=1, source_target_pairs={{0,1},{1,0},{2,3},{3,2},{4,5},{5,4},{6,7},{7,6},{8,9},{9,8},{10,11... | collective-permute-start | bytes 49160 | tf_op jit(solution)/shard_map/ppermute | solution.py:866
  15.0 0.0 copy-done.4
  15.1 1.1 %shard_map.153 = (f32[64,256]{1,0:T(8,128)S(1)}, bf16[8,64,128]{2,1,0:T(8,128)(2,1)}) custom-call(bf16[1728,96]{1,0:T(8,128)(2,1)S(1)} %get-tuple-element.49.gather, bf16[64,256]{1,0:T(8,128)(2,1)S(1)} %get-tuple-element.55.third.planes, bf16[32,256]{1,0:T(8,128)(2,1)S(1)} %get-tuple-element.56.far.earlier, bf16[27,256,256]{2,1,0:T(8,128)(2,1)S(1)} %copy-done.4, ...), custom_call_target="tpu_custom_call" | custom-call | flops 10000000000 | bytes 10000000 | tf_op jit(solution)/shard_map/pallas_call | solution.py:706
  16.2 0.0 collective-permute-done.4.from_a
  16.2 1.1 %shard_map.155 = bf16[8,8,256]{2,1,0:T(8,128)(2,1)} custom-call(bf16[288,32]{1,0:T(8,128)(2,1)S(1)} %get-tuple-element.59.gather, f32[64,256]{1,0:T(8,128)S(1)} %get-tuple-element.60.partial, bf16[32,256]{1,0:T(8,128)(2,1)S(1)} %collective-permute-done.4.from_a, bf16[27,256,256]{2,1,0:T(8,128)(2,1)S(1)} %copy-done.4, f32[64,256]{1,0:T(8,128)S(1)} %get-tuple-element.52.mask_three), custom_call_target="tpu_custom_call" | custom-call | flops 10000000000 | bytes 10000000 | tf_op jit(solution)/shard_map/pallas_call | solution.py:706
  (3 shorter events, 0.0 us)
Async XLA Ops:
  0.6 0.7 %copy-start.8 = (s32[8,16]{1,0:T(8,128)S(1)}, s32[8,16]{1,0:T(8,128)}, u32[]{:S(2)}) copy-start(s32[8,16]{1,0:T(8,128)} %occupancy.1) | copy-start | bytes 1540
  0.6 1.0 %copy-start.5 = (bf16[8,512,64]{1,2,0:T(8,128)(2,1)S(1)}, bf16[8,512,64]{1,2,0:T(8,128)(2,1)}, u32[]{:S(2)}) copy-start(bf16[8,512,64]{1,2,0:T(8,128)(2,1)} %param.12) | copy-start | bytes 1572868
  0.7 1.0 %copy-start.9 = (s32[8,27]{1,0:T(8,128)S(1)}, s32[8,27]{1,0:T(8,128)}, u32[]{:S(2)}) copy-start(s32[8,27]{1,0:T(8,128)} %neighbours.9) | copy-start | bytes 2596
  0.7 4.5 %copy-start.6 = (bf16[27,64,64]{2,1,0:T(8,128)(2,1)S(1)}, bf16[27,64,64]{2,1,0:T(8,128)(2,1)}, u32[]{:S(2)}) copy-start(bf16[27,64,64]{2,1,0:T(8,128)(2,1)} %kernel.5) | copy-start | bytes 663556
  0.7 4.5 %copy-start.7 = (bf16[8,64,128]{2,1,0:T(8,128)(2,1)S(1)}, bf16[8,64,128]{2,1,0:T(8,128)(2,1)}, u32[]{:S(2)}) copy-start(bf16[8,64,128]{2,1,0:T(8,128)(2,1)} %reduce.2) | copy-start | bytes 393220
  1.8 5.8 %collective-permute-start.1 = (bf16[272,128]{1,0:T(8,128)(2,1)S(1)}, bf16[272,128]{1,0:T(8,128)(2,1)S(1)}, u32[]{:S(2)}, u32[]{:S(2)}) collective-permute-start(bf16[272,128]{1,0:T(8,128)(2,1)S(1)} %shard_map.141.earlier), channel_id=1, source_target_pairs={{0,16},{1,2},{2,1},{3,4},{4,3},{5,6},{6,5},{7,8},{8,7},{9,10},{10,... | collective-permute-start | bytes 208904 | tf_op jit(solution)/shard_map/ppermute | solution.py:750
  4.9 2.6 %collective-permute-start = (bf16[4,64,128]{2,1,0:T(8,128)(2,1)S(1)}, bf16[4,64,128]{2,1,0:T(8,128)(2,1)S(1)}, u32[]{:S(2)}, u32[]{:S(2)}) collective-permute-start(bf16[4,64,128]{2,1,0:T(8,128)(2,1)S(1)} %shard_map.142), channel_id=1, source_target_pairs={{0,1},{1,0},{2,3},{3,2},{4,5},{5,4},{6,7},{7,6},{8,9},{9,8},{10,11... | collective-permute-start | bytes 196616 | tf_op jit(solution)/shard_map/ppermute | solution.py:751
  7.6 2.7 %copy-start.10 = (bf16[432,27]{1,0:T(8,128)(2,1)S(1)}, bf16[432,27]{1,0:T(8,128)(2,1)}, u32[]{:S(2)}) copy-start(bf16[432,27]{1,0:T(8,128)(2,1)} %constant.8.clone.pick) | copy-start | bytes 69988
  7.6 3.1 %copy-start.11 = (bf16[432,27]{1,0:T(8,128)(2,1)S(1)}, bf16[432,27]{1,0:T(8,128)(2,1)}, u32[]{:S(2)}) copy-start(bf16[432,27]{1,0:T(8,128)(2,1)} %constant.9.clone.pick) | copy-start | bytes 69988
  8.5 4.7 %collective-permute-start.3 = (bf16[384,128]{1,0:T(8,128)(2,1)S(1)}, bf16[384,128]{1,0:T(8,128)(2,1)S(1)}, u32[]{:S(2)}, u32[]{:S(2)}) collective-permute-start(bf16[384,128]{1,0:T(8,128)(2,1)S(1)} %get-tuple-element.43.earlier.to_b), channel_id=1, source_target_pairs={{0,16},{1,2},{2,1},{3,4},{4,3},{5,6},{6,5},{7,8},{8,7},{9,10},{10,... | collective-permute-start | bytes 294920 | tf_op jit(solution)/shard_map/ppermute | solution.py:750
  10.1 1.7 %copy-start = (bf16[27,128,128]{2,1,0:T(8,128)(2,1)S(1)}, bf16[27,128,128]{2,1,0:T(8,128)(2,1)}, u32[]{:S(2)}) copy-start(bf16[27,128,128]{2,1,0:T(8,128)(2,1)} %kernel.7) | copy-start | bytes 2654212
  10.1 1.7 %collective-permute-start.2 = (bf16[128,128]{1,0:T(8,128)(2,1)S(1)}, bf16[128,128]{1,0:T(8,128)(2,1)S(1)}, u32[]{:S(2)}, u32[]{:S(2)}) collective-permute-start(bf16[128,128]{1,0:T(8,128)(2,1)S(1)} %shard_map.146.later), channel_id=1, source_target_pairs={{0,1},{1,0},{2,3},{3,2},{4,5},{5,4},{6,7},{7,6},{8,9},{9,8},{10,11... | collective-permute-start | bytes 98312 | tf_op jit(solution)/shard_map/ppermute | solution.py:751
  11.8 1.4 %copy-start.1 = (bf16[8,128,256]{2,1,0:T(8,128)(2,1)S(1)}, bf16[8,128,256]{2,1,0:T(8,128)(2,1)}, u32[]{:S(2)}) copy-start(bf16[8,128,256]{2,1,0:T(8,128)(2,1)} %reduce.3) | copy-start | bytes 1572868
  11.8 1.4 %copy-start.2 = (bf16[128,128]{1,0:T(8,128)(2,1)S(1)}, bf16[128,128]{1,0:T(8,128)(2,1)}, u32[]{:S(2)}) copy-start(bf16[128,128]{1,0:T(8,128)(2,1)} %constant.10.clone.children) | copy-start | bytes 98308
  11.9 1.4 %copy-start.3 = (bf16[64,64]{1,0:T(8,128)(2,1)S(1)}, bf16[64,64]{1,0:T(8,128)(2,1)}, u32[]{:S(2)}) copy-start(bf16[64,64]{1,0:T(8,128)(2,1)} %constant.11.clone.far_children) | copy-start | bytes 24580
  13.1 2.0 %copy-start.4 = (bf16[27,256,256]{2,1,0:T(8,128)(2,1)S(1)}, bf16[27,256,256]{2,1,0:T(8,128)(2,1)}, u32[]{:S(2)}) copy-start(bf16[27,256,256]{2,1,0:T(8,128)(2,1)} %kernel.9) | copy-start | bytes 10616836
  14.7 1.5 %collective-permute-start.4 = (bf16[32,256]{1,0:T(8,128)(2,1)S(1)}, bf16[32,256]{1,0:T(8,128)(2,1)S(1)}, u32[]{:S(2)}, u32[]{:S(2)}) collective-permute-start(bf16[32,256]{1,0:T(8,128)(2,1)S(1)} %shard_map.154), channel_id=1, source_target_pairs={{0,1},{1,0},{2,3},{3,2},{4,5},{5,4},{6,7},{7,6},{8,9},{9,8},{10,11... | collective-permute-start | bytes 49160 | tf_op jit(solution)/shard_map/ppermute | solution.py:866

commit v8 on v6

--- a/solution.py
+++ b/solution.py
@@ -518,17 +518,12 @@
     copy.start()
     rows = inner.shape[1]
     planes = beside([outer[:rows], inner[0], inner[1], outer[rows:]])
-    moved = dot(own_gather[...], planes).astype(BF16)
+    sides = stack([own_gather[: 4 * rows], own_gather[5 * rows :]])
+    moved = dot(sides, planes).astype(BF16)
+    taps = [moved[q * rows : (q + 1) * rows] for q in range(8)]
+    taps.insert(4, planes)
     left = beside(
-        [
-            stack(
-                [
-                    moved[q * rows : (q + 1) * rows, 128 * i : 128 * (i + 1)]
-                    for i in range(4)
-                ]
-            )
-            for q in range(9)
-        ]
+        [stack([tap[:, 128 * i : 128 * (i + 1)] for i in range(4)]) for tap in taps]
     )
     weights = [kernel[9 * a : 9 * (a + 1)].reshape(9 * 128, 128) for a in range(3)]
     sums = dot(left, beside(weights[:2]))

time: 17.6 us -> 17.6 us (level)
  no operation moved by 1% of the time
where the time goes in v8:
time: 17.6 us; the launch traced here: 17.4 us
  Pallas kernels  10 us (57%)
  starting transfers between devices  5.25 us (30%)
  local copies, waits for them, and re-layouts  1.1 us (6%)
  between operations  0.87 us (5%)
    pallas_call x17, Pallas kernels, call(): pl.pallas_call(kernel, out_shape=out_shape, in_specs=[ANY if n in remain...  10 us
    ppermute x2, starting transfers between devices, exchange(): from_b = lax.ppermute(to_b, axes, across)  4.59 us
    unnamed x24, local copies, waits for them, and re-layouts  1.1 us
  transfers between devices with their start and end apart: 5, of which 1 were waited for; matrix products, arithmetic and copies ran while one was open for 0% of the time, Pallas kernels for 36%

profile of v8, /device:TPU:0, one launch (start us, length us, event | category | flops | bytes accessed | tf_op | source)
XLA Modules:
  0.0 17.4 jit_solution(11919864136265750478)
XLA Ops:
  0.6 0.0 copy-start.6
  0.6 0.0 copy-start.2
  0.7 0.0 copy-start.7
  0.7 0.0 copy-start.4
  0.7 0.0 copy-start.5
  0.7 0.6 %copy-done.6 = s32[8,16]{1,0:T(8,128)S(1)} copy-done((s32[8,16]{1,0:T(8,128)S(1)}, s32[8,16]{1,0:T(8,128)}, u32[]{:S(2)}) %copy-start.6) | copy-done | bytes 536
  1.3 0.1 shard_map.140
  1.5 0.2 %copy-done.2 = bf16[8,512,64]{1,2,0:T(8,128)(2,1)S(1)} copy-done((bf16[8,512,64]{1,2,0:T(8,128)(2,1)S(1)}, bf16[8,512,64]{1,2,0:T(8,128)(2,1)}, u32[]{:S(2)}) %copy-start.2) | copy-done | bytes 524312
  1.7 0.0 copy-done.7
  1.7 0.1 shard_map.141.earlier
  1.8 3.0 %collective-permute-start.1 = (bf16[272,128]{1,0:T(8,128)(2,1)S(1)}, bf16[272,128]{1,0:T(8,128)(2,1)S(1)}, u32[]{:S(2)}, u32[]{:S(2)}) collective-permute-start(bf16[272,128]{1,0:T(8,128)(2,1)S(1)} %shard_map.141.earlier), channel_id=1, source_target_pairs={{0,16},{1,2},{2,1},{3,4},{4,3},{5,6},{6,5},{7,8},{8,7},{9,10},{10,... | collective-permute-start | bytes 208904 | tf_op jit(solution)/shard_map/ppermute | solution.py:745
  4.8 0.1 shard_map.142
  4.9 0.2 %collective-permute-start = (bf16[4,64,128]{2,1,0:T(8,128)(2,1)S(1)}, bf16[4,64,128]{2,1,0:T(8,128)(2,1)S(1)}, u32[]{:S(2)}, u32[]{:S(2)}) collective-permute-start(bf16[4,64,128]{2,1,0:T(8,128)(2,1)S(1)} %shard_map.142), channel_id=1, source_target_pairs={{0,1},{1,0},{2,3},{3,2},{4,5},{5,4},{6,7},{7,6},{8,9},{9,8},{10,11... | collective-permute-start | bytes 196616 | tf_op jit(solution)/shard_map/ppermute | solution.py:746
  5.1 0.0 copy-done.4
  5.1 0.0 copy-done.5
  5.1 1.6 %shard_map.143 = (bf16[8,3,6,16,128]{4,3,2,1,0:T(8,128)(2,1)S(1)}, bf16[1152,256]{1,0:T(8,128)(2,1)S(1)}, bf16[1152,128]{1,0:T(8,128)(2,1)S(1)}, bf16[256,256]{1,0:T(8,128)(2,1)S(1)}, f32[4,512,128]{2,1,0:T(8,128)S(1)}) custom-call(s32[8,27]{1,0:T(8,128)S(1)} %copy-done.7, f32[4,8,128]{2,1,0:T(8,128)S(1)} %get-tuple-element.32.bits, ...), custom_call_target="tpu_custom_call" | custom-call | flops 20000000000 | bytes 10000000 | tf_op jit(solution)/shard_map/pallas_call | solution.py:701
  6.8 0.8 %shard_map.144 = (bf16[8,2,64,128]{3,2,1,0:T(8,128)(2,1)S(1)}, bf16[2,128,128]{2,1,0:T(8,128)(2,1)S(1)}) custom-call(bf16[8,3,6,16,128]{4,3,2,1,0:T(8,128)(2,1)S(1)} %get-tuple-element.39.middle, bf16[1152,256]{1,0:T(8,128)(2,1)S(1)} %get-tuple-element.40.taps, f32[4,512,128]{2,1,0:T(8,128)S(1)} %get-tuple-element.35.partial, ...), custom_call_target="tpu_custom_call" | custom-call | flops 500000000 | bytes 10000000 | tf_op jit(solution)/shard_map/pallas_call | solution.py:701
  7.5 0.0 collective-permute-done.from_a
  7.6 0.0 collective-permute-done.1.from_b.message
  7.6 0.0 copy-start.8
  7.6 0.0 copy-start.9
  7.6 0.9 %shard_map.145 = (bf16[8,2,64,128]{3,2,1,0:T(8,128)(2,1)S(1)}, bf16[256,128]{1,0:T(8,128)(2,1)S(1)}, bf16[384,128]{1,0:T(8,128)(2,1)S(1)}) custom-call(s32[8,27]{1,0:T(8,128)S(1)} %copy-done.7, bf16[4,64,128]{2,1,0:T(8,128)(2,1)S(1)} %collective-permute-done.from_a, bf16[272,128]{1,0:T(8,128)(2,1)S(1)} %collective-permute-done.1.from_b.message, ...), custom_call_target="tpu_custom_call" | custom-call | flops 15000000512 | bytes 10000000 | tf_op jit(solution)/shard_map/pallas_call | solution.py:701
  8.5 1.6 %collective-permute-start.3 = (bf16[384,128]{1,0:T(8,128)(2,1)S(1)}, bf16[384,128]{1,0:T(8,128)(2,1)S(1)}, u32[]{:S(2)}, u32[]{:S(2)}) collective-permute-start(bf16[384,128]{1,0:T(8,128)(2,1)S(1)} %get-tuple-element.43.earlier.to_b), channel_id=1, source_target_pairs={{0,16},{1,2},{2,1},{3,4},{4,3},{5,6},{6,5},{7,8},{8,7},{9,10},{10,... | collective-permute-start | bytes 294920 | tf_op jit(solution)/shard_map/ppermute | solution.py:745
  10.1 0.0 copy-start.1
  10.1 0.1 collective-permute-start.2
  10.2 0.0 copy-done.8
  10.2 0.4 %shard_map.147 = (bf16[1152,128]{1,0:T(8,128)(2,1)S(1)}, bf16[2,1152,128]{2,1,0:T(8,128)(2,1)S(1)}) custom-call(s32[8,27]{1,0:T(8,128)S(1)} %copy-done.7, bf16[432,27]{1,0:T(8,128)(2,1)S(1)} %copy-done.8, bf16[128,128]{1,0:T(8,128)(2,1)S(1)} %shard_map.146.later), custom_call_target="tpu_custom_call" | custom-call | flops 500000000 | bytes 10000000 | tf_op jit(solution)/shard_map/pallas_call | solution.py:701
  10.6 0.0 copy-done.9
  10.7 0.4 %shard_map.150 = (bf16[1728,96]{1,0:T(8,128)(2,1)S(1)}, bf16[288,32]{1,0:T(8,128)(2,1)S(1)}) custom-call(s32[8,27]{1,0:T(8,128)S(1)} %copy-done.7, bf16[432,27]{1,0:T(8,128)(2,1)S(1)} %copy-done.9, bf16[128,128]{1,0:T(8,128)(2,1)S(1)} %shard_map.146.later), custom_call_target="tpu_custom_call" | custom-call | flops 500000000 | bytes 10000000 | tf_op jit(solution)/shard_map/pallas_call | solution.py:701
  11.1 0.4 %shard_map.148.first = bf16[8,64,512]{2,1,0:T(8,128)(2,1)S(1)} custom-call(bf16[8,2,64,128]{3,2,1,0:T(8,128)(2,1)S(1)} %get-tuple-element.46.outer, bf16[8,2,64,128]{3,2,1,0:T(8,128)(2,1)S(1)} %get-tuple-element.47.inner), custom_call_target="tpu_custom_call" | custom-call | flops 500000000 | bytes 10000000 | tf_op jit(solution)/shard_map/pallas_call | solution.py:701
  11.5 0.4 %shard_map.151 = (bf16[1152,256]{1,0:T(8,128)(2,1)S(1)}, f32[256,128]{1,0:T(8,128)S(1)}, f32[32,256]{1,0:T(8,128)S(1)}) custom-call(bf16[272,128]{1,0:T(8,128)(2,1)S(1)} %collective-permute-done.1.from_b.message, bf16[432,27]{1,0:T(8,128)(2,1)S(1)} %copy-done.8, bf16[128,128]{1,0:T(8,128)(2,1)S(1)} %shard_map.146.later), custom_call_target="tpu_custom_call" | custom-call | flops 500000000 | bytes 10000000 | tf_op jit(solution)/shard_map/pallas_call | solution.py:701
  11.8 0.0 collective-permute-done.2.from_a
  11.8 0.0 copy-done.1
  11.8 0.0 copy-start.3
  11.8 0.0 copy-start.10
  11.9 0.0 copy-start.11
  11.9 1.2 %shard_map.149 = (f32[512,128]{1,0:T(8,128)S(1)}, bf16[8,64,512]{2,1,0:T(8,128)(2,1)}) custom-call(bf16[256,128]{1,0:T(8,128)(2,1)S(1)} %get-tuple-element.42.planes.outer, bf16[2,128,128]{2,1,0:T(8,128)(2,1)S(1)} %get-tuple-element.41.inner, bf16[1152,128]{1,0:T(8,128)(2,1)S(1)} %get-tuple-element.44.own_gather, ...), custom_call_target="tpu_custom_call" | custom-call | flops 10000000000 | bytes 10000000 | tf_op jit(solution)/shard_map/pallas_call | solution.py:701
  13.1 0.2 collective-permute-done.3.from_b
  13.2 0.0 copy-done.3
  13.2 0.0 copy-done.10
  13.2 0.0 copy-done.11
  13.2 0.0 copy-start
  13.2 1.4 %shard_map.152 = (bf16[8,64,128]{2,1,0:T(8,128)(2,1)S(1)}, bf16[64,256]{1,0:T(8,128)(2,1)S(1)}, bf16[32,256]{1,0:T(8,128)(2,1)S(1)}) custom-call(bf16[2,1152,128]{2,1,0:T(8,128)(2,1)S(1)} %get-tuple-element.45.gathers, bf16[1152,256]{1,0:T(8,128)(2,1)S(1)} %get-tuple-element.50.far_gather, bf16[128,128]{1,0:T(8,128)(2,1)S(1)} %copy-done.10, ...), custom_call_target="tpu_custom_call" | custom-call | flops 15000000512 | bytes 10000000 | tf_op jit(solution)/shard_map/pallas_call | solution.py:701
  14.7 0.3 %collective-permute-start.4 = (bf16[32,256]{1,0:T(8,128)(2,1)S(1)}, bf16[32,256]{1,0:T(8,128)(2,1)S(1)}, u32[]{:S(2)}, u32[]{:S(2)}) collective-permute-start(bf16[32,256]{1,0:T(8,128)(2,1)S(1)} %shard_map.154), channel_id=1, source_target_pairs={{0,1},{1,0},{2,3},{3,2},{4,5},{5,4},{6,7},{7,6},{8,9},{9,8},{10,11... | collective-permute-start | bytes 49160 | tf_op jit(solution)/shard_map/ppermute | solution.py:861
  15.0 0.2 %copy-done = bf16[27,256,256]{2,1,0:T(8,128)(2,1)S(1)} copy-done((bf16[27,256,256]{2,1,0:T(8,128)(2,1)S(1)}, bf16[27,256,256]{2,1,0:T(8,128)(2,1)}, u32[]{:S(2)}) %copy-start) | copy-done | bytes 3538968
  15.2 1.1 %shard_map.153 = (f32[64,256]{1,0:T(8,128)S(1)}, bf16[8,64,128]{2,1,0:T(8,128)(2,1)}) custom-call(bf16[1728,96]{1,0:T(8,128)(2,1)S(1)} %get-tuple-element.49.gather, bf16[64,256]{1,0:T(8,128)(2,1)S(1)} %get-tuple-element.55.third.planes, bf16[32,256]{1,0:T(8,128)(2,1)S(1)} %get-tuple-element.56.far.earlier, bf16[27,256,256]{2,1,0:T(8,128)(2,1)S(1)} %copy-done, ...), custom_call_target="tpu_custom_call" | custom-call | flops 10000000000 | bytes 10000000 | tf_op jit(solution)/shard_map/pallas_call | solution.py:701
  16.3 0.0 collective-permute-done.4.from_a
  16.3 1.1 %shard_map.155 = bf16[8,8,256]{2,1,0:T(8,128)(2,1)} custom-call(bf16[288,32]{1,0:T(8,128)(2,1)S(1)} %get-tuple-element.59.gather, f32[64,256]{1,0:T(8,128)S(1)} %get-tuple-element.60.partial, bf16[32,256]{1,0:T(8,128)(2,1)S(1)} %collective-permute-done.4.from_a, bf16[27,256,256]{2,1,0:T(8,128)(2,1)S(1)} %copy-done, f32[64,256]{1,0:T(8,128)S(1)} %get-tuple-element.52.mask_three), custom_call_target="tpu_custom_call" | custom-call | flops 10000000000 | bytes 10000000 | tf_op jit(solution)/shard_map/pallas_call | solution.py:701
  (3 shorter events, 0.0 us)
Async XLA Ops:
  0.6 0.7 %copy-start.6 = (s32[8,16]{1,0:T(8,128)S(1)}, s32[8,16]{1,0:T(8,128)}, u32[]{:S(2)}) copy-start(s32[8,16]{1,0:T(8,128)} %occupancy.1) | copy-start | bytes 1540
  0.6 1.0 %copy-start.2 = (bf16[8,512,64]{1,2,0:T(8,128)(2,1)S(1)}, bf16[8,512,64]{1,2,0:T(8,128)(2,1)}, u32[]{:S(2)}) copy-start(bf16[8,512,64]{1,2,0:T(8,128)(2,1)} %param.12) | copy-start | bytes 1572868
  0.7 1.0 %copy-start.7 = (s32[8,27]{1,0:T(8,128)S(1)}, s32[8,27]{1,0:T(8,128)}, u32[]{:S(2)}) copy-start(s32[8,27]{1,0:T(8,128)} %neighbours.9) | copy-start | bytes 2596
  0.7 4.5 %copy-start.4 = (bf16[27,64,64]{2,1,0:T(8,128)(2,1)S(1)}, bf16[27,64,64]{2,1,0:T(8,128)(2,1)}, u32[]{:S(2)}) copy-start(bf16[27,64,64]{2,1,0:T(8,128)(2,1)} %kernel.5) | copy-start | bytes 663556
  0.7 4.5 %copy-start.5 = (bf16[8,64,128]{2,1,0:T(8,128)(2,1)S(1)}, bf16[8,64,128]{2,1,0:T(8,128)(2,1)}, u32[]{:S(2)}) copy-start(bf16[8,64,128]{2,1,0:T(8,128)(2,1)} %reduce.2) | copy-start | bytes 393220
  1.8 5.8 %collective-permute-start.1 = (bf16[272,128]{1,0:T(8,128)(2,1)S(1)}, bf16[272,128]{1,0:T(8,128)(2,1)S(1)}, u32[]{:S(2)}, u32[]{:S(2)}) collective-permute-start(bf16[272,128]{1,0:T(8,128)(2,1)S(1)} %shard_map.141.earlier), channel_id=1, source_target_pairs={{0,16},{1,2},{2,1},{3,4},{4,3},{5,6},{6,5},{7,8},{8,7},{9,10},{10,... | collective-permute-start | bytes 208904 | tf_op jit(solution)/shard_map/ppermute | solution.py:745
  4.9 2.6 %collective-permute-start = (bf16[4,64,128]{2,1,0:T(8,128)(2,1)S(1)}, bf16[4,64,128]{2,1,0:T(8,128)(2,1)S(1)}, u32[]{:S(2)}, u32[]{:S(2)}) collective-permute-start(bf16[4,64,128]{2,1,0:T(8,128)(2,1)S(1)} %shard_map.142), channel_id=1, source_target_pairs={{0,1},{1,0},{2,3},{3,2},{4,5},{5,4},{6,7},{7,6},{8,9},{9,8},{10,11... | collective-permute-start | bytes 196616 | tf_op jit(solution)/shard_map/ppermute | solution.py:746
  7.6 2.7 %copy-start.8 = (bf16[432,27]{1,0:T(8,128)(2,1)S(1)}, bf16[432,27]{1,0:T(8,128)(2,1)}, u32[]{:S(2)}) copy-start(bf16[432,27]{1,0:T(8,128)(2,1)} %constant.8.clone.pick) | copy-start | bytes 69988
  7.6 3.1 %copy-start.9 = (bf16[432,27]{1,0:T(8,128)(2,1)S(1)}, bf16[432,27]{1,0:T(8,128)(2,1)}, u32[]{:S(2)}) copy-start(bf16[432,27]{1,0:T(8,128)(2,1)} %constant.9.clone.pick) | copy-start | bytes 69988
  8.5 4.7 %collective-permute-start.3 = (bf16[384,128]{1,0:T(8,128)(2,1)S(1)}, bf16[384,128]{1,0:T(8,128)(2,1)S(1)}, u32[]{:S(2)}, u32[]{:S(2)}) collective-permute-start(bf16[384,128]{1,0:T(8,128)(2,1)S(1)} %get-tuple-element.43.earlier.to_b), channel_id=1, source_target_pairs={{0,16},{1,2},{2,1},{3,4},{4,3},{5,6},{6,5},{7,8},{8,7},{9,10},{10,... | collective-permute-start | bytes 294920 | tf_op jit(solution)/shard_map/ppermute | solution.py:745
  10.1 1.7 %copy-start.1 = (bf16[27,128,128]{2,1,0:T(8,128)(2,1)S(1)}, bf16[27,128,128]{2,1,0:T(8,128)(2,1)}, u32[]{:S(2)}) copy-start(bf16[27,128,128]{2,1,0:T(8,128)(2,1)} %kernel.7) | copy-start | bytes 2654212
  10.1 1.7 %collective-permute-start.2 = (bf16[128,128]{1,0:T(8,128)(2,1)S(1)}, bf16[128,128]{1,0:T(8,128)(2,1)S(1)}, u32[]{:S(2)}, u32[]{:S(2)}) collective-permute-start(bf16[128,128]{1,0:T(8,128)(2,1)S(1)} %shard_map.146.later), channel_id=1, source_target_pairs={{0,1},{1,0},{2,3},{3,2},{4,5},{5,4},{6,7},{7,6},{8,9},{9,8},{10,11... | collective-permute-start | bytes 98312 | tf_op jit(solution)/shard_map/ppermute | solution.py:746
  11.8 1.4 %copy-start.3 = (bf16[8,128,256]{2,1,0:T(8,128)(2,1)S(1)}, bf16[8,128,256]{2,1,0:T(8,128)(2,1)}, u32[]{:S(2)}) copy-start(bf16[8,128,256]{2,1,0:T(8,128)(2,1)} %reduce.3) | copy-start | bytes 1572868
  11.8 1.4 %copy-start.10 = (bf16[128,128]{1,0:T(8,128)(2,1)S(1)}, bf16[128,128]{1,0:T(8,128)(2,1)}, u32[]{:S(2)}) copy-start(bf16[128,128]{1,0:T(8,128)(2,1)} %constant.10.clone.children) | copy-start | bytes 98308
  11.9 1.4 %copy-start.11 = (bf16[64,64]{1,0:T(8,128)(2,1)S(1)}, bf16[64,64]{1,0:T(8,128)(2,1)}, u32[]{:S(2)}) copy-start(bf16[64,64]{1,0:T(8,128)(2,1)} %constant.11.clone.far_children) | copy-start | bytes 24580
  13.2 2.0 %copy-start = (bf16[27,256,256]{2,1,0:T(8,128)(2,1)S(1)}, bf16[27,256,256]{2,1,0:T(8,128)(2,1)}, u32[]{:S(2)}) copy-start(bf16[27,256,256]{2,1,0:T(8,128)(2,1)} %kernel.9) | copy-start | bytes 10616836
  14.7 1.6 %collective-permute-start.4 = (bf16[32,256]{1,0:T(8,128)(2,1)S(1)}, bf16[32,256]{1,0:T(8,128)(2,1)S(1)}, u32[]{:S(2)}, u32[]{:S(2)}) collective-permute-start(bf16[32,256]{1,0:T(8,128)(2,1)S(1)} %shard_map.154), channel_id=1, source_target_pairs={{0,1},{1,0},{2,3},{3,2},{4,5},{5,4},{6,7},{7,6},{8,9},{9,8},{10,11... | collective-permute-start | bytes 49160 | tf_op jit(solution)/shard_map/ppermute | solution.py:861

commit v9 on v8

--- a/solution.py
+++ b/solution.py
@@ -349,27 +349,23 @@
                     else:
                         windows[b, e, pair, jr] = tiles[jr][e]
 
-    group = count // 2
-    for g in range(2):
-        bricks = slice(g * group, (g + 1) * group)
-        rows = slice(g * group * 64, (g + 1) * group * 64)
-        low, high, wrap = [
-            dot(
-                beside(
-                    [
-                        windows[bricks, e, pair, c : c + 4].reshape(group * 64, 128)
-                        for c in range(3)
-                        for e in range(3)
-                    ]
-                ),
-                weights[...],
-            )
-            for pair, weights in ((0, taps), (2, taps), (3, wrap_taps))
-        ]
-        partial[0, rows] = low[:, :128] + wrap[:, 128:]
-        partial[1, rows] = low[:, 128:]
-        partial[2, rows] = high[:, :128]
-        partial[3, rows] = high[:, 128:] + wrap[:, :128]
+    columns = [
+        beside(
+            [
+                windows[:, e, pair, c : c + 4].reshape(count * 64, 128)
+                for c in range(3)
+                for e in range(3)
+            ]
+        )
+        for pair in (0, 2, 3)
+    ]
+    both = dot(stack(columns[:2]), taps[...])
+    wrap = dot(columns[2], wrap_taps[...])
+    low, high = both[: count * 64], both[count * 64 :]
+    partial[0] = low[:, :128] + wrap[:, 128:]
+    partial[1] = low[:, 128:]
+    partial[2] = high[:, :128]
+    partial[3] = high[:, 128:] + wrap[:, :128]
 
 
 def masked_tiles(sums, pair_words, b, i):
@@ -851,7 +847,7 @@
     face = shape((4 * count, 256), BF16)
     second_level, third, far_third = call(
         faces_two_kernel,
-        1.5,
+        0.05,
         (shape((count, 64, 128), BF16), shape((8 * count, 256), BF16), face),
         [],
         sides_two, far_two, child_rows(2), child_rows(1), partial, to_b, from_b, conv_two,

time: 17.6 us -> 17.4 us (0.989)
  transfers between devices with their start and end apart: 5 -> 5, of which waited for: 1 -> 1; matrix products, arithmetic and copies ran while one was open for 0% -> 0% of each run, Pallas kernels for 36% -> 37%
where the time goes in v9:
time: 17.4 us; the launch traced here: 17.3 us
  Pallas kernels  10.1 us (58%)
  starting transfers between devices  5.23 us (30%)
  local copies, waits for them, and re-layouts  0.98 us (6%)
  between operations  0.87 us (5%)
    pallas_call x17, Pallas kernels, call(): pl.pallas_call(kernel, out_shape=out_shape, in_specs=[ANY if n in remain...  10.1 us
    ppermute x2, starting transfers between devices, exchange(): from_b = lax.ppermute(to_b, axes, across)  4.56 us
    unnamed x24, local copies, waits for them, and re-layouts  0.98 us
    ppermute x2, starting transfers between devices, exchange(): return (lax.ppermute(to_a, axes, within), from_b)  0.35 us
  transfers between devices with their start and end apart: 5, of which 1 were waited for; matrix products, arithmetic and copies ran while one was open for 0% of the time, Pallas kernels for 37%

profile of v9, /device:TPU:0, one launch (start us, length us, event | category | flops | bytes accessed | tf_op | source)
XLA Modules:
  0.0 17.3 jit_solution(6482225297644716066)
XLA Ops:
  0.6 0.0 copy-start.8
  0.6 0.0 copy-start.5
  0.7 0.0 copy-start.9
  0.7 0.0 copy-start.6
  0.7 0.0 copy-start.7
  0.7 0.6 %copy-done.8 = s32[8,16]{1,0:T(8,128)S(1)} copy-done((s32[8,16]{1,0:T(8,128)S(1)}, s32[8,16]{1,0:T(8,128)}, u32[]{:S(2)}) %copy-start.8) | copy-done | bytes 536
  1.3 0.1 shard_map.140
  1.5 0.2 %copy-done.5 = bf16[8,512,64]{1,2,0:T(8,128)(2,1)S(1)} copy-done((bf16[8,512,64]{1,2,0:T(8,128)(2,1)S(1)}, bf16[8,512,64]{1,2,0:T(8,128)(2,1)}, u32[]{:S(2)}) %copy-start.5) | copy-done | bytes 524312
  1.7 0.0 copy-done.9
  1.7 0.1 shard_map.141.earlier
  1.8 3.0 %collective-permute-start.1 = (bf16[272,128]{1,0:T(8,128)(2,1)S(1)}, bf16[272,128]{1,0:T(8,128)(2,1)S(1)}, u32[]{:S(2)}, u32[]{:S(2)}) collective-permute-start(bf16[272,128]{1,0:T(8,128)(2,1)S(1)} %shard_map.141.earlier), channel_id=1, source_target_pairs={{0,16},{1,2},{2,1},{3,4},{4,3},{5,6},{6,5},{7,8},{8,7},{9,10},{10,... | collective-permute-start | bytes 208904 | tf_op jit(solution)/shard_map/ppermute | solution.py:741
  4.8 0.1 shard_map.142
  4.9 0.2 %collective-permute-start = (bf16[4,64,128]{2,1,0:T(8,128)(2,1)S(1)}, bf16[4,64,128]{2,1,0:T(8,128)(2,1)S(1)}, u32[]{:S(2)}, u32[]{:S(2)}) collective-permute-start(bf16[4,64,128]{2,1,0:T(8,128)(2,1)S(1)} %shard_map.142), channel_id=1, source_target_pairs={{0,1},{1,0},{2,3},{3,2},{4,5},{5,4},{6,7},{7,6},{8,9},{9,8},{10,11... | collective-permute-start | bytes 196616 | tf_op jit(solution)/shard_map/ppermute | solution.py:742
  5.1 0.0 copy-done.6
  5.1 0.0 copy-done.7
  5.1 1.7 %shard_map.143 = (bf16[8,3,6,16,128]{4,3,2,1,0:T(8,128)(2,1)S(1)}, bf16[1152,256]{1,0:T(8,128)(2,1)S(1)}, bf16[1152,128]{1,0:T(8,128)(2,1)S(1)}, bf16[256,256]{1,0:T(8,128)(2,1)S(1)}, f32[4,512,128]{2,1,0:T(8,128)S(1)}) custom-call(s32[8,27]{1,0:T(8,128)S(1)} %copy-done.9, f32[4,8,128]{2,1,0:T(8,128)S(1)} %get-tuple-element.32.bits, ...), custom_call_target="tpu_custom_call" | custom-call | flops 20000000000 | bytes 10000000 | tf_op jit(solution)/shard_map/pallas_call | solution.py:697
  6.8 0.8 %shard_map.144 = (bf16[8,2,64,128]{3,2,1,0:T(8,128)(2,1)S(1)}, bf16[2,128,128]{2,1,0:T(8,128)(2,1)S(1)}) custom-call(bf16[8,3,6,16,128]{4,3,2,1,0:T(8,128)(2,1)S(1)} %get-tuple-element.39.middle, bf16[1152,256]{1,0:T(8,128)(2,1)S(1)} %get-tuple-element.40.taps, f32[4,512,128]{2,1,0:T(8,128)S(1)} %get-tuple-element.35.partial, ...), custom_call_target="tpu_custom_call" | custom-call | flops 500000000 | bytes 10000000 | tf_op jit(solution)/shard_map/pallas_call | solution.py:697
  7.6 0.0 collective-permute-done.from_a
  7.6 0.0 collective-permute-done.1.from_b.message
  7.6 0.0 copy-start.10
  7.6 0.0 copy-start.11
  7.6 0.9 %shard_map.145 = (bf16[8,2,64,128]{3,2,1,0:T(8,128)(2,1)S(1)}, bf16[256,128]{1,0:T(8,128)(2,1)S(1)}, bf16[384,128]{1,0:T(8,128)(2,1)S(1)}) custom-call(s32[8,27]{1,0:T(8,128)S(1)} %copy-done.9, bf16[4,64,128]{2,1,0:T(8,128)(2,1)S(1)} %collective-permute-done.from_a, bf16[272,128]{1,0:T(8,128)(2,1)S(1)} %collective-permute-done.1.from_b.message, ...), custom_call_target="tpu_custom_call" | custom-call | flops 15000000512 | bytes 10000000 | tf_op jit(solution)/shard_map/pallas_call | solution.py:697
  8.6 1.6 %collective-permute-start.3 = (bf16[384,128]{1,0:T(8,128)(2,1)S(1)}, bf16[384,128]{1,0:T(8,128)(2,1)S(1)}, u32[]{:S(2)}, u32[]{:S(2)}) collective-permute-start(bf16[384,128]{1,0:T(8,128)(2,1)S(1)} %get-tuple-element.43.earlier.to_b), channel_id=1, source_target_pairs={{0,16},{1,2},{2,1},{3,4},{4,3},{5,6},{6,5},{7,8},{8,7},{9,10},{10,... | collective-permute-start | bytes 294920 | tf_op jit(solution)/shard_map/ppermute | solution.py:741
  10.1 0.0 copy-start
  10.1 0.1 collective-permute-start.2
  10.3 0.0 copy-done.10
  10.3 0.4 %shard_map.147 = (bf16[1152,128]{1,0:T(8,128)(2,1)S(1)}, bf16[2,1152,128]{2,1,0:T(8,128)(2,1)S(1)}) custom-call(s32[8,27]{1,0:T(8,128)S(1)} %copy-done.9, bf16[432,27]{1,0:T(8,128)(2,1)S(1)} %copy-done.10, bf16[128,128]{1,0:T(8,128)(2,1)S(1)} %shard_map.146.later), custom_call_target="tpu_custom_call" | custom-call | flops 500000000 | bytes 10000000 | tf_op jit(solution)/shard_map/pallas_call | solution.py:697
  10.7 0.0 copy-done.11
  10.7 0.4 %shard_map.150 = (bf16[1728,96]{1,0:T(8,128)(2,1)S(1)}, bf16[288,32]{1,0:T(8,128)(2,1)S(1)}) custom-call(s32[8,27]{1,0:T(8,128)S(1)} %copy-done.9, bf16[432,27]{1,0:T(8,128)(2,1)S(1)} %copy-done.11, bf16[128,128]{1,0:T(8,128)(2,1)S(1)} %shard_map.146.later), custom_call_target="tpu_custom_call" | custom-call | flops 500000000 | bytes 10000000 | tf_op jit(solution)/shard_map/pallas_call | solution.py:697
  11.1 0.4 %shard_map.148.first = bf16[8,64,512]{2,1,0:T(8,128)(2,1)S(1)} custom-call(bf16[8,2,64,128]{3,2,1,0:T(8,128)(2,1)S(1)} %get-tuple-element.46.outer, bf16[8,2,64,128]{3,2,1,0:T(8,128)(2,1)S(1)} %get-tuple-element.47.inner), custom_call_target="tpu_custom_call" | custom-call | flops 500000000 | bytes 10000000 | tf_op jit(solution)/shard_map/pallas_call | solution.py:697
  11.5 0.4 %shard_map.151 = (bf16[1152,256]{1,0:T(8,128)(2,1)S(1)}, f32[256,128]{1,0:T(8,128)S(1)}, f32[32,256]{1,0:T(8,128)S(1)}) custom-call(bf16[272,128]{1,0:T(8,128)(2,1)S(1)} %collective-permute-done.1.from_b.message, bf16[432,27]{1,0:T(8,128)(2,1)S(1)} %copy-done.10, bf16[128,128]{1,0:T(8,128)(2,1)S(1)} %shard_map.146.later), custom_call_target="tpu_custom_call" | custom-call | flops 500000000 | bytes 10000000 | tf_op jit(solution)/shard_map/pallas_call | solution.py:697
  11.9 0.0 collective-permute-done.2.from_a
  11.9 0.0 copy-done
  11.9 0.0 copy-start.1
  11.9 0.0 copy-start.2
  11.9 0.0 copy-start.3
  11.9 1.2 %shard_map.149 = (f32[512,128]{1,0:T(8,128)S(1)}, bf16[8,64,512]{2,1,0:T(8,128)(2,1)}) custom-call(bf16[256,128]{1,0:T(8,128)(2,1)S(1)} %get-tuple-element.42.planes.outer, bf16[2,128,128]{2,1,0:T(8,128)(2,1)S(1)} %get-tuple-element.41.inner, bf16[1152,128]{1,0:T(8,128)(2,1)S(1)} %get-tuple-element.44.own_gather, ...), custom_call_target="tpu_custom_call" | custom-call | flops 10000000000 | bytes 10000000 | tf_op jit(solution)/shard_map/pallas_call | solution.py:697
  13.1 0.0 copy-start.4
  13.1 0.1 collective-permute-done.3.from_b
  13.2 0.0 copy-done.1
  13.3 0.0 copy-done.2
  13.3 0.0 copy-done.3
  13.3 1.4 %shard_map.152 = (bf16[8,64,128]{2,1,0:T(8,128)(2,1)S(1)}, bf16[64,256]{1,0:T(8,128)(2,1)S(1)}, bf16[32,256]{1,0:T(8,128)(2,1)S(1)}) custom-call(bf16[2,1152,128]{2,1,0:T(8,128)(2,1)S(1)} %get-tuple-element.45.gathers, bf16[1152,256]{1,0:T(8,128)(2,1)S(1)} %get-tuple-element.50.far_gather, bf16[128,128]{1,0:T(8,128)(2,1)S(1)} %copy-done.2, ...), custom_call_target="tpu_custom_call" | custom-call | flops 500000000 | bytes 10000000 | tf_op jit(solution)/shard_map/pallas_call | solution.py:697
  14.7 0.3 %collective-permute-start.4 = (bf16[32,256]{1,0:T(8,128)(2,1)S(1)}, bf16[32,256]{1,0:T(8,128)(2,1)S(1)}, u32[]{:S(2)}, u32[]{:S(2)}) collective-permute-start(bf16[32,256]{1,0:T(8,128)(2,1)S(1)} %shard_map.154), channel_id=1, source_target_pairs={{0,1},{1,0},{2,3},{3,2},{4,5},{5,4},{6,7},{7,6},{8,9},{9,8},{10,11... | collective-permute-start | bytes 49160 | tf_op jit(solution)/shard_map/ppermute | solution.py:857
  15.0 0.1 copy-done.4
  15.1 1.1 %shard_map.153 = (f32[64,256]{1,0:T(8,128)S(1)}, bf16[8,64,128]{2,1,0:T(8,128)(2,1)}) custom-call(bf16[1728,96]{1,0:T(8,128)(2,1)S(1)} %get-tuple-element.49.gather, bf16[64,256]{1,0:T(8,128)(2,1)S(1)} %get-tuple-element.55.third.planes, bf16[32,256]{1,0:T(8,128)(2,1)S(1)} %get-tuple-element.56.far.earlier, bf16[27,256,256]{2,1,0:T(8,128)(2,1)S(1)} %copy-done.4, ...), custom_call_target="tpu_custom_call" | custom-call | flops 10000000000 | bytes 10000000 | tf_op jit(solution)/shard_map/pallas_call | solution.py:697
  16.2 0.0 collective-permute-done.4.from_a
  16.2 1.1 %shard_map.155 = bf16[8,8,256]{2,1,0:T(8,128)(2,1)} custom-call(bf16[288,32]{1,0:T(8,128)(2,1)S(1)} %get-tuple-element.59.gather, f32[64,256]{1,0:T(8,128)S(1)} %get-tuple-element.60.partial, bf16[32,256]{1,0:T(8,128)(2,1)S(1)} %collective-permute-done.4.from_a, bf16[27,256,256]{2,1,0:T(8,128)(2,1)S(1)} %copy-done.4, f32[64,256]{1,0:T(8,128)S(1)} %get-tuple-element.52.mask_three), custom_call_target="tpu_custom_call" | custom-call | flops 10000000000 | bytes 10000000 | tf_op jit(solution)/shard_map/pallas_call | solution.py:697
  (3 shorter events, 0.0 us)
Async XLA Ops:
  0.6 0.7 %copy-start.8 = (s32[8,16]{1,0:T(8,128)S(1)}, s32[8,16]{1,0:T(8,128)}, u32[]{:S(2)}) copy-start(s32[8,16]{1,0:T(8,128)} %occupancy.1) | copy-start | bytes 1540
  0.6 1.0 %copy-start.5 = (bf16[8,512,64]{1,2,0:T(8,128)(2,1)S(1)}, bf16[8,512,64]{1,2,0:T(8,128)(2,1)}, u32[]{:S(2)}) copy-start(bf16[8,512,64]{1,2,0:T(8,128)(2,1)} %param.12) | copy-start | bytes 1572868
  0.7 1.0 %copy-start.9 = (s32[8,27]{1,0:T(8,128)S(1)}, s32[8,27]{1,0:T(8,128)}, u32[]{:S(2)}) copy-start(s32[8,27]{1,0:T(8,128)} %neighbours.9) | copy-start | bytes 2596
  0.7 4.5 %copy-start.6 = (bf16[27,64,64]{2,1,0:T(8,128)(2,1)S(1)}, bf16[27,64,64]{2,1,0:T(8,128)(2,1)}, u32[]{:S(2)}) copy-start(bf16[27,64,64]{2,1,0:T(8,128)(2,1)} %kernel.5) | copy-start | bytes 663556
  0.7 4.5 %copy-start.7 = (bf16[8,64,128]{2,1,0:T(8,128)(2,1)S(1)}, bf16[8,64,128]{2,1,0:T(8,128)(2,1)}, u32[]{:S(2)}) copy-start(bf16[8,64,128]{2,1,0:T(8,128)(2,1)} %reduce.2) | copy-start | bytes 393220
  1.8 5.8 %collective-permute-start.1 = (bf16[272,128]{1,0:T(8,128)(2,1)S(1)}, bf16[272,128]{1,0:T(8,128)(2,1)S(1)}, u32[]{:S(2)}, u32[]{:S(2)}) collective-permute-start(bf16[272,128]{1,0:T(8,128)(2,1)S(1)} %shard_map.141.earlier), channel_id=1, source_target_pairs={{0,16},{1,2},{2,1},{3,4},{4,3},{5,6},{6,5},{7,8},{8,7},{9,10},{10,... | collective-permute-start | bytes 208904 | tf_op jit(solution)/shard_map/ppermute | solution.py:741
  4.9 2.7 %collective-permute-start = (bf16[4,64,128]{2,1,0:T(8,128)(2,1)S(1)}, bf16[4,64,128]{2,1,0:T(8,128)(2,1)S(1)}, u32[]{:S(2)}, u32[]{:S(2)}) collective-permute-start(bf16[4,64,128]{2,1,0:T(8,128)(2,1)S(1)} %shard_map.142), channel_id=1, source_target_pairs={{0,1},{1,0},{2,3},{3,2},{4,5},{5,4},{6,7},{7,6},{8,9},{9,8},{10,11... | collective-permute-start | bytes 196616 | tf_op jit(solution)/shard_map/ppermute | solution.py:742
  7.6 2.7 %copy-start.10 = (bf16[432,27]{1,0:T(8,128)(2,1)S(1)}, bf16[432,27]{1,0:T(8,128)(2,1)}, u32[]{:S(2)}) copy-start(bf16[432,27]{1,0:T(8,128)(2,1)} %constant.8.clone.pick) | copy-start | bytes 69988
  7.6 3.1 %copy-start.11 = (bf16[432,27]{1,0:T(8,128)(2,1)S(1)}, bf16[432,27]{1,0:T(8,128)(2,1)}, u32[]{:S(2)}) copy-start(bf16[432,27]{1,0:T(8,128)(2,1)} %constant.9.clone.pick) | copy-start | bytes 69988
  8.6 4.7 %collective-permute-start.3 = (bf16[384,128]{1,0:T(8,128)(2,1)S(1)}, bf16[384,128]{1,0:T(8,128)(2,1)S(1)}, u32[]{:S(2)}, u32[]{:S(2)}) collective-permute-start(bf16[384,128]{1,0:T(8,128)(2,1)S(1)} %get-tuple-element.43.earlier.to_b), channel_id=1, source_target_pairs={{0,16},{1,2},{2,1},{3,4},{4,3},{5,6},{6,5},{7,8},{8,7},{9,10},{10,... | collective-permute-start | bytes 294920 | tf_op jit(solution)/shard_map/ppermute | solution.py:741
  10.1 1.7 %copy-start = (bf16[27,128,128]{2,1,0:T(8,128)(2,1)S(1)}, bf16[27,128,128]{2,1,0:T(8,128)(2,1)}, u32[]{:S(2)}) copy-start(bf16[27,128,128]{2,1,0:T(8,128)(2,1)} %kernel.7) | copy-start | bytes 2654212
  10.1 1.7 %collective-permute-start.2 = (bf16[128,128]{1,0:T(8,128)(2,1)S(1)}, bf16[128,128]{1,0:T(8,128)(2,1)S(1)}, u32[]{:S(2)}, u32[]{:S(2)}) collective-permute-start(bf16[128,128]{1,0:T(8,128)(2,1)S(1)} %shard_map.146.later), channel_id=1, source_target_pairs={{0,1},{1,0},{2,3},{3,2},{4,5},{5,4},{6,7},{7,6},{8,9},{9,8},{10,11... | collective-permute-start | bytes 98312 | tf_op jit(solution)/shard_map/ppermute | solution.py:742
  11.9 1.4 %copy-start.1 = (bf16[8,128,256]{2,1,0:T(8,128)(2,1)S(1)}, bf16[8,128,256]{2,1,0:T(8,128)(2,1)}, u32[]{:S(2)}) copy-start(bf16[8,128,256]{2,1,0:T(8,128)(2,1)} %reduce.3) | copy-start | bytes 1572868
  11.9 1.4 %copy-start.2 = (bf16[128,128]{1,0:T(8,128)(2,1)S(1)}, bf16[128,128]{1,0:T(8,128)(2,1)}, u32[]{:S(2)}) copy-start(bf16[128,128]{1,0:T(8,128)(2,1)} %constant.10.clone.children) | copy-start | bytes 98308
  11.9 1.4 %copy-start.3 = (bf16[64,64]{1,0:T(8,128)(2,1)S(1)}, bf16[64,64]{1,0:T(8,128)(2,1)}, u32[]{:S(2)}) copy-start(bf16[64,64]{1,0:T(8,128)(2,1)} %constant.11.clone.far_children) | copy-start | bytes 24580
  13.1 2.0 %copy-start.4 = (bf16[27,256,256]{2,1,0:T(8,128)(2,1)S(1)}, bf16[27,256,256]{2,1,0:T(8,128)(2,1)}, u32[]{:S(2)}) copy-start(bf16[27,256,256]{2,1,0:T(8,128)(2,1)} %kernel.9) | copy-start | bytes 10616836
  14.7 1.5 %collective-permute-start.4 = (bf16[32,256]{1,0:T(8,128)(2,1)S(1)}, bf16[32,256]{1,0:T(8,128)(2,1)S(1)}, u32[]{:S(2)}, u32[]{:S(2)}) collective-permute-start(bf16[32,256]{1,0:T(8,128)(2,1)S(1)} %shard_map.154), channel_id=1, source_target_pairs={{0,1},{1,0},{2,3},{3,2},{4,5},{5,4},{6,7},{7,6},{8,9},{9,8},{10,11... | collective-permute-start | bytes 49160 | tf_op jit(solution)/shard_map/ppermute | solution.py:857
